TPU v7x, 32 devices: a whole 2x2x4 slice. The times are simulated.
32 devices in a mesh: dp: 2 (over core), row: 4 (over y, x), col: 4 (over z).
Axes of the slice: x: 2, y: 2, z: 4, core: 2. Of those that a mesh axis runs over, the one named last changes fastest.
Arguments:
- tokens: bfloat16 [384, 8192], P(('dp', 'col'), 'row'), may hold values from -160 to 160
- norm_gain: float32 [8192], P('row'), may hold values from 0.3 to 3
- gate_weight: bfloat16 [8192, 14336], P('row', ('dp', 'col')), may hold values from -0.0625 to 0.0625
- up_weight: bfloat16 [8192, 14336], P('row', ('dp', 'col')), may hold values from -0.0625 to 0.0625
- down_weight: bfloat16 [14336, 8192], P(('dp', 'col'), 'row'), may hold values from -0.046875 to 0.046875
- gate_keep: int32 [64, 112], P('row', ('dp', 'col')), may hold values from 0 to 1, as said below
- up_keep: int32 [64, 112], P('row', ('dp', 'col')), may hold values from 0 to 1, as said below
- down_keep: int32 [112, 64], P(('dp', 'col'), 'row'), may hold values from 0 to 1, as said below
- cotangent: bfloat16 [384, 8192], P(('dp', 'col'), 'row'), may hold values from -80 to 80
Outputs:
- branch: bfloat16 [384, 8192], P(('dp', 'col'), 'row')
- grad_tokens: float32 [384, 8192], P(('dp', 'col'), 'row')
- grad_gain: float32 [8192], P('row')
- grad_gate: float32 [8192, 14336], P('row', ('dp', 'col'))
- grad_up: float32 [8192, 14336], P('row', ('dp', 'col'))
- grad_down: float32 [14336, 8192], P(('dp', 'col'), 'row')
Inputs may be any that keep to these rules, and one draw needn't show every extreme that they name: `gate_keep`: 1 keeps a 128 x 128 block of the gate projection, 0 prunes it. `up_keep`: 1 keeps a 128 x 128 block of the up projection, 0 prunes it. `down_keep`: 1 keeps a 128 x 128 block of the down projection, 0 prunes it.
All inputs are finite; a program needn't handle non-finite values.
Results may differ from a plain program's by a relative error of at most 0.0065.
Values may be sent and summed in bfloat16 or wider, within the bound.
No kernel may reach another device: no remote copies, remote signals or barrier semaphores. Data moves between devices by JAX's collectives and lax.ppermute only.
A program may use at most 320 MiB of HBM per device.

v0:
```python
import jax
import jax.numpy as jnp
from jax import lax
from jax.sharding import PartitionSpec as P

D = 8192
BLOCK = 128


def expand_keep(keep, target_type):
    return jnp.repeat(jnp.repeat(keep, BLOCK, axis=0), BLOCK, axis=1).astype(target_type)


def activate(gate, up_value):
    return (gate * jax.nn.sigmoid(gate) * up_value).astype(jnp.bfloat16)


def on_device(
    tokens, norm_gain, gate_weight, up_weight, down_weight, gate_keep, up_keep, down_keep, cotangent
):
    token_f = tokens.astype(jnp.float32)
    square = lax.psum(jnp.sum(token_f * token_f, axis=1), "row")
    inv_rms = lax.rsqrt(square[:, None] / D + 1e-05)
    normed = (token_f * inv_rms * norm_gain).astype(jnp.bfloat16)
    gate_masked = gate_weight * expand_keep(gate_keep, jnp.bfloat16)
    up_masked = up_weight * expand_keep(up_keep, jnp.bfloat16)
    down_masked = down_weight * expand_keep(down_keep, jnp.bfloat16)
    gate_full, up_full = (
        lax.all_gather(gate_masked, "dp", axis=1, tiled=True),
        lax.all_gather(up_masked, "dp", axis=1, tiled=True),
    )
    down_full = lax.all_gather(down_masked, "dp", axis=0, tiled=True)
    seen_rows = lax.all_gather(normed, "col", axis=0, tiled=True)
    seen_cot = lax.all_gather(cotangent, "col", axis=0, tiled=True)
    width_f = gate_full.shape[1]
    contract_last = (((1,), (1,)), ((), ()))
    contract_first = (((0,), (0,)), ((), ()))
    row_block = seen_rows
    summed = lax.psum_scatter(
        jnp.concatenate(
            [
                jnp.dot(row_block, gate_full, preferred_element_type=jnp.float32),
                jnp.dot(row_block, up_full, preferred_element_type=jnp.float32),
            ],
            axis=1,
        ),
        "row",
        scatter_dimension=0,
        tiled=True,
    )
    gate_part = summed[:, :width_f]
    up_part = summed[:, width_f:]
    hidden = lax.all_gather(activate(gate_part, up_part), "row", axis=0, tiled=True)
    row_block = hidden
    branch_sum = lax.psum_scatter(
        jnp.dot(row_block, down_full, preferred_element_type=jnp.float32),
        "col",
        scatter_dimension=0,
        tiled=True,
    )
    branch = branch_sum.astype(jnp.bfloat16)
    row_block = seen_cot
    hidden_grad = lax.psum_scatter(
        lax.dot_general(row_block, down_full, contract_last, preferred_element_type=jnp.float32),
        "row",
        scatter_dimension=0,
        tiled=True,
    )
    sigmoid_gate = jax.nn.sigmoid(gate_part)
    gate_grad = (
        hidden_grad * up_part * sigmoid_gate * (1.0 + gate_part * (1.0 - sigmoid_gate))
    ).astype(jnp.bfloat16)
    up_grad = (hidden_grad * gate_part * sigmoid_gate).astype(jnp.bfloat16)
    gate_grads, up_grads = (
        lax.all_gather(gate_grad, "row", axis=0, tiled=True),
        lax.all_gather(up_grad, "row", axis=0, tiled=True),
    )
    normed_grad = lax.psum_scatter(
        lax.dot_general(gate_grads, gate_full, contract_last, preferred_element_type=jnp.float32)
        + lax.dot_general(up_grads, up_full, contract_last, preferred_element_type=jnp.float32),
        "col",
        scatter_dimension=0,
        tiled=True,
    )
    down_local = lax.dot_general(
        hidden, seen_cot, contract_first, preferred_element_type=jnp.float32
    )
    gate_local = lax.dot_general(
        seen_rows, gate_grads, contract_first, preferred_element_type=jnp.float32
    )
    up_local = lax.dot_general(
        seen_rows, up_grads, contract_first, preferred_element_type=jnp.float32
    )
    gate_total, up_total = (
        lax.psum_scatter(gate_local, "dp", scatter_dimension=1, tiled=True),
        lax.psum_scatter(up_local, "dp", scatter_dimension=1, tiled=True),
    )
    down_total = lax.psum_scatter(down_local, "dp", scatter_dimension=0, tiled=True)
    grad_gate = gate_total * expand_keep(gate_keep, jnp.float32)
    grad_up = up_total * expand_keep(up_keep, jnp.float32)
    grad_down = down_total * expand_keep(down_keep, jnp.float32)
    grad_gain = lax.psum(jnp.sum(normed_grad * token_f * inv_rms, axis=0), ("dp", "col"))
    inner_dot = lax.psum(jnp.sum(norm_gain * normed_grad * token_f, axis=1), "row")
    grad_tokens = (
        inv_rms * norm_gain * normed_grad
        - token_f * inv_rms * inv_rms * inv_rms * inner_dot[:, None] / D
    )
    return (branch, grad_tokens, grad_gain, grad_gate, grad_up, grad_down)


def solution(mesh):
    in_specs = (
        P(("dp", "col"), "row"),
        P("row"),
        P("row", ("dp", "col")),
        P("row", ("dp", "col")),
        P(("dp", "col"), "row"),
        P("row", ("dp", "col")),
        P("row", ("dp", "col")),
        P(("dp", "col"), "row"),
        P(("dp", "col"), "row"),
    )
    out_specs = (
        P(("dp", "col"), "row"),
        P(("dp", "col"), "row"),
        P("row"),
        P("row", ("dp", "col")),
        P("row", ("dp", "col")),
        P(("dp", "col"), "row"),
    )
    return jax.shard_map(
        on_device, mesh=mesh, in_specs=in_specs, out_specs=out_specs, check_vma=False
    )
```

profile of v0, /device:TPU:0, one launch (start us, length us, event | category | flops | bytes accessed | tf_op | source)
XLA Modules:
  0.0 550.3 jit_solution(2003280147903016930)
XLA Ops:
  25.0 10.6 %copy.18 = bf16[2048,1792]{0,1:T(8,128)(2,1)} copy(bf16[2048,1792]{1,0:T(8,128)(2,1)} %param.12) | data formatting | bytes 14680064 | tf_op args[3]
  45.8 10.7 %copy.16 = bf16[2048,1792]{0,1:T(8,128)(2,1)} copy(bf16[2048,1792]{1,0:T(8,128)(2,1)} %param.11) | data formatting | bytes 14680064 | tf_op args[2]
  64.5 20.9 %all_gather.29 = bf16[192,2048]{1,0:T(8,128)(2,1)S(1)} all-gather(bf16[48,2048]{1,0:T(8,128)(2,1)S(1)} %copy-done.6), channel_id=1, replica_groups=mesh['dp'=2,'row'=4,'col'=4] {'col'}, dimensions={0}, use_global_device_ids=true | all-gather | bytes 983040 | tf_op jit(solution)/shard_map/all_gather | solution.py:34
  85.4 11.9 %convolution_bitcast_fusion = f32[192,3584]{1,0:T(8,128)} fusion(bf16[3584,2048]{1,0:T(8,128)(2,1)} %all-gather.13.cloned.1.call-done, bf16[192,2048]{1,0:T(8,128)(2,1)S(1)} %all_gather.29), kind=kOutput, calls=%fused_computation.5 | convolution fusion | flops 2818572288 | bytes 18219008 | tf_op jit(solution)/shard_map/dot_general | solution.py:64
  97.5 9.9 %psum.21 = f32[48]{0:T(128)S(1)} all-reduce(f32[48]{0:T(128)S(1)} %fusion.7), channel_id=1, replica_groups=mesh['dp'=2,'row'=4,'col'=4] {'row'}, use_global_device_ids=true, to_apply=%region_1.0 | all-reduce | flops 48 | bytes 384 | tf_op jit(solution)/shard_map/psum | solution.py:22
  107.6 17.4 %all_gather.24 = bf16[192,2048]{1,0:T(8,128)(2,1)S(1)} all-gather(bf16[48,2048]{1,0:T(8,128)(2,1)S(1)} %fusion.2), channel_id=1, replica_groups=mesh['dp'=2,'row'=4,'col'=4] {'col'}, dimensions={0}, use_global_device_ids=true | all-gather | bytes 983040 | tf_op jit(solution)/shard_map/all_gather | solution.py:33
  125.0 12.1 %fusion.15 = f32[192,3584]{1,0:T(8,128)} fusion(bf16[192,2048]{1,0:T(8,128)(2,1)S(1)} %all_gather.24, bf16[2048,3584]{0,1:T(8,128)(2,1)} %all-gather.9.cloned.1.call-done), kind=kOutput, calls=%fused_computation.35 | convolution fusion | flops 2818572288 | bytes 18219008 | tf_op jit(solution)/shard_map/dot_general | solution.py:43
  137.2 12.0 %fusion.14 = f32[192,3584]{1,0:T(8,128)} fusion(bf16[192,2048]{1,0:T(8,128)(2,1)S(1)} %all_gather.24, bf16[2048,3584]{0,1:T(8,128)(2,1)} %all-gather.7.cloned.1.call-done), kind=kOutput, calls=%fused_computation.34 | convolution fusion | flops 2818572288 | bytes 18219008 | tf_op jit(solution)/shard_map/dot_general | solution.py:42
  160.9 67.1 %reduce-scatter.8.cloned.1.call-done = f32[48,7168]{1,0:T(8,128)} async-done(((f32[192,7168]{1,0:T(8,128)}), f32[48,7168]{1,0:T(8,128)}) %reduce-scatter.8.cloned.1.call-update) | async-done | bytes 1376272 | tf_op jit(solution)/shard_map/reduce_scatter | solution.py:39
  232.4 28.0 %all-gather.11.cloned.1.call-done = bf16[192,3584]{1,0:T(8,128)(2,1)} async-done(((bf16[48,3584]{1,0:T(8,128)(2,1)}), bf16[192,3584]{1,0:T(8,128)(2,1)}) %all-gather.11.cloned.1.call-update) | async-done | bytes 1376272 | tf_op jit(solution)/shard_map/all_gather | solution.py:53
  270.4 21.7 %all-gather.15.cloned.1.call-done = bf16[192,3584]{1,0:T(8,128)(2,1)} async-done(((bf16[48,3584]{1,0:T(8,128)(2,1)}), bf16[192,3584]{1,0:T(8,128)(2,1)}) %all-gather.15.cloned.1.call-update) | async-done | bytes 1376272 | tf_op jit(solution)/shard_map/all_gather | solution.py:75
  301.9 22.0 %all-gather.17.cloned.1.call-done = bf16[192,3584]{1,0:T(8,128)(2,1)} async-done(((bf16[48,3584]{1,0:T(8,128)(2,1)}), bf16[192,3584]{1,0:T(8,128)(2,1)}) %all-gather.17.cloned.1.call-update) | async-done | bytes 1376272 | tf_op jit(solution)/shard_map/all_gather | solution.py:76
  323.9 10.2 %convolution_add_fusion = f32[192,2048]{1,0:T(8,128)} fusion(f32[192,2048]{1,0:T(8,128)} %fusion.17, bf16[192,3584]{1,0:T(8,128)(2,1)} %all-gather.17.cloned.1.call-done, bf16[2048,3584]{0,1:T(8,128)(2,1)} %all-gather.9.cloned.1.call-done), kind=kOutput, calls=%fused_computation.6 | convolution fusion | flops 2818965504 | bytes 19202048 | tf_op jit(solution)/shard_map/dot_general | solution.py:80
  334.2 11.9 %fusion.18 = f32[2048,3584]{1,0:T(8,128)} fusion(bf16[192,2048]{1,0:T(8,128)(2,1)S(1)} %all_gather.24, bf16[192,3584]{1,0:T(8,128)(2,1)S(1)} %copy-done.5), kind=kOutput, calls=%fused_computation.38 | convolution fusion | flops 2818572288 | bytes 31522816 | tf_op jit(solution)/shard_map/dot_general | solution.py:88
  347.4 11.9 %fusion.19 = f32[2048,3584]{1,0:T(8,128)} fusion(bf16[192,2048]{1,0:T(8,128)(2,1)S(1)} %all_gather.24, bf16[192,3584]{1,0:T(8,128)(2,1)S(1)} %copy-done.4), kind=kOutput, calls=%fused_computation.39 | convolution fusion | flops 2818572288 | bytes 31522816 | tf_op jit(solution)/shard_map/dot_general | solution.py:91
  360.7 12.0 %fusion.20 = f32[3584,2048]{1,0:T(8,128)} fusion(bf16[192,3584]{1,0:T(8,128)(2,1)S(1)} %copy-done.3, bf16[192,2048]{1,0:T(8,128)(2,1)S(1)} %all_gather.29), kind=kOutput, calls=%fused_computation.40 | convolution fusion | flops 2818572288 | bytes 31522816 | tf_op jit(solution)/shard_map/dot_general | solution.py:85
  380.2 14.3 %copy.20 = f32[2048,1792]{1,0:T(8,128)} copy(f32[2048,1792]{0,1:T(8,128)} %bitcast.58) | data formatting | bytes 29360128 | tf_op jit(solution)/shard_map/convert_element_type | solution.py:11
  402.1 15.5 %copy.22 = f32[2048,1792]{1,0:T(8,128)} copy(f32[2048,1792]{0,1:T(8,128)} %bitcast.59) | data formatting | bytes 29360128 | tf_op jit(solution)/shard_map/convert_element_type | solution.py:11
  429.8 16.1 %psum.23 = f32[2048]{0:T(1024)} all-reduce(f32[2048]{0:T(1024)S(1)} %get-tuple-element.6), channel_id=1, replica_groups=mesh['dp'=2,'row'=4,'col'=4] {'dp','col'}, use_global_device_ids=true, to_apply=%region_9.0 | all-reduce | flops 2048 | bytes 16384 | tf_op jit(solution)/shard_map/psum | solution.py:102
  447.9 21.9 %mul.141 = f32[2048,1792]{1,0:T(8,128)} multiply(f32[2048,1792]{1,0:T(8,128)} %reduce-scatter.16.cloned.1.call-done, f32[2048,1792]{1,0:T(8,128)} %copy.20) | non-fusion elementwise | flops 3670016 | bytes 44040192 | tf_op jit(solution)/shard_map/mul | solution.py:99
  469.8 13.9 %reduce-scatter.18.cloned.1.call-done = f32[2048,1792]{1,0:T(8,128)} async-done(((f32[2048,3584]{1,0:T(8,128)}), f32[2048,1792]{1,0:T(8,128)}) %reduce-scatter.18.cloned.1.call-update) | async-done | bytes 14680080 | tf_op jit(solution)/shard_map/reduce_scatter | solution.py:96
  483.7 18.2 %mul.142 = f32[2048,1792]{1,0:T(8,128)} multiply(f32[2048,1792]{1,0:T(8,128)} %reduce-scatter.18.cloned.1.call-done, f32[2048,1792]{1,0:T(8,128)} %copy.22) | non-fusion elementwise | flops 3670016 | bytes 44040192 | tf_op jit(solution)/shard_map/mul | solution.py:100
  501.8 25.6 %reduce-scatter.20.cloned.1.call-done = f32[1792,2048]{1,0:T(8,128)} async-done(((f32[3584,2048]{1,0:T(8,128)}), f32[1792,2048]{1,0:T(8,128)}) %reduce-scatter.20.cloned.1.call-update) | async-done | bytes 14680080 | tf_op jit(solution)/shard_map/reduce_scatter | solution.py:98
  532.7 10.6 %bitcast_multiply_fusion = f32[1792,2048]{1,0:T(8,128)} fusion(f32[1792,2048]{1,0:T(8,128)S(1)} %copy-done, f32[224,8,16,128]{3,2,1,0:T(8,128)S(1)} %bitcast.60), kind=kLoop, calls=%fused_computation | loop fusion | flops 3670016 | bytes 44040192 | tf_op jit(solution)/shard_map/mul | solution.py:101
  (94 shorter events, 109.3 us)
Async XLA Ops:
  7.2 78.2 %all-gather.13.cloned.1.call-start = ((), (), s32[]{:S(2)}) async-start(), calls=%async_computation.11 | async-start | bytes 22020096 | tf_op jit(solution)/shard_map/all_gather | solution.py:32
  25.0 10.6 %copy-start.9 = (s32[16,14]{1,0:T(8,128)S(1)}, s32[16,14]{1,0:T(8,128)}, u32[]{:S(2)}) copy-start(s32[16,14]{1,0:T(8,128)} %param.15) | copy-start | bytes 2692
  25.0 100.1 %all-gather.9.cloned.1.call-start = ((), (), s32[]{:S(2)}) async-start(), calls=%async_computation.8 | async-start | bytes 22020096 | tf_op jit(solution)/shard_map/all_gather | solution.py:30
  45.8 10.8 %copy-start.10 = (s32[16,14]{1,0:T(8,128)S(1)}, s32[16,14]{1,0:T(8,128)}, u32[]{:S(2)}) copy-start(s32[16,14]{1,0:T(8,128)} %param.14) | copy-start | bytes 2692
  45.8 91.4 %all-gather.7.cloned.1.call-start = ((), (), s32[]{:S(2)}) async-start(), calls=%async_computation.7 | async-start | bytes 22020096 | tf_op jit(solution)/shard_map/all_gather | solution.py:29
  63.5 1.0 copy-start.6
  63.5 97.4 %reduce-scatter.12.cloned.1.call-start = ((), (), s32[]{:S(2)}) async-start(), calls=%async_computation.13 | async-start | bytes 3440640 | tf_op jit(solution)/shard_map/reduce_scatter | solution.py:63
  85.4 12.0 %copy-start.1 = (bf16[48,2048]{1,0:T(8,128)(2,1)S(1)}, bf16[48,2048]{1,0:T(8,128)(2,1)}, u32[]{:S(2)}) copy-start(bf16[48,2048]{1,0:T(8,128)(2,1)} %param.9) | copy-start | bytes 589828
  85.4 22.1 %copy-start.7 = (f32[2048]{0:T(1024)S(1)}, f32[2048]{0:T(1024)}, u32[]{:S(2)}) copy-start(f32[2048]{0:T(1024)} %param.10) | copy-start | bytes 24580
  97.3 130.7 %reduce-scatter.8.cloned.1.call-start = ((), (), s32[]{:S(2)}) async-start(), calls=%async_computation.9 | async-start | bytes 6881280 | tf_op jit(solution)/shard_map/reduce_scatter | solution.py:39
  137.2 12.0 %copy-start.2 = (f32[192,3584]{1,0:T(8,128)S(1)}, f32[192,3584]{1,0:T(8,128)}, u32[]{:S(2)}) copy-start(f32[192,3584]{1,0:T(8,128)} %fusion.15) | copy-start | bytes 8257540
  154.3 106.1 %all-gather.11.cloned.1.call-start = ((), (), s32[]{:S(2)}) async-start(), calls=%async_computation.10 | async-start | bytes 1720320 | tf_op jit(solution)/shard_map/all_gather | solution.py:53
  230.8 61.3 %all-gather.15.cloned.1.call-start = ((), (), s32[]{:S(2)}) async-start(), calls=%async_computation.14 | async-start | bytes 1720320 | tf_op jit(solution)/shard_map/all_gather | solution.py:75
  231.6 92.3 %all-gather.17.cloned.1.call-start = ((), (), s32[]{:S(2)}) async-start(), calls=%async_computation.15 | async-start | bytes 1720320 | tf_op jit(solution)/shard_map/all_gather | solution.py:76
  232.3 185.2 %reduce-scatter.10.cloned.1.call-start = ((), (), s32[]{:S(2)}) async-start(), calls=%async_computation.12 | async-start | bytes 1966080 | tf_op jit(solution)/shard_map/reduce_scatter | solution.py:55
  270.1 149.2 %reduce-scatter.14.cloned.1.call-start = ((), (), s32[]{:S(2)}) async-start(), calls=%async_computation.16 | async-start | bytes 1966080 | tf_op jit(solution)/shard_map/reduce_scatter | solution.py:78
  301.9 32.3 %copy-start.5 = (bf16[192,3584]{1,0:T(8,128)(2,1)S(1)}, bf16[192,3584]{1,0:T(8,128)(2,1)}, u32[]{:S(2)}) copy-start(bf16[192,3584]{1,0:T(8,128)(2,1)} %all-gather.15.cloned.1.call-done) | copy-start | bytes 4128772
  334.1 113.8 %reduce-scatter.16.cloned.1.call-start = ((), (), s32[]{:S(2)}) async-start(), calls=%async_computation.17 | async-start | bytes 44040192 | tf_op jit(solution)/shard_map/reduce_scatter | solution.py:95
  346.1 1.3 copy-start.4
  346.1 137.6 %reduce-scatter.18.cloned.1.call-start = ((), (), s32[]{:S(2)}) async-start(), calls=%async_computation.18 | async-start | bytes 44040192 | tf_op jit(solution)/shard_map/reduce_scatter | solution.py:96
  359.3 1.4 copy-start.3
  359.3 168.1 %reduce-scatter.20.cloned.1.call-start = ((), (), s32[]{:S(2)}) async-start(), calls=%async_computation.19 | async-start | bytes 44040192 | tf_op jit(solution)/shard_map/reduce_scatter | solution.py:98
  469.8 57.6 %copy-start.8 = (f32[14,16]{1,0:T(8,128)S(1)}, f32[14,16]{1,0:T(8,128)}, u32[]{:S(2)}) copy-start(f32[14,16]{1,0:T(8,128)} %get-tuple-element.11) | copy-start | bytes 2692
  527.5 5.2 copy-start
Sparse Core Ops, SparseCore 0:
  25.1 29.7 all-gather.12
  57.0 28.1 all-gather.8
  87.4 28.1 all-gather.6
  119.0 41.8 reduce-scatter.11
  164.4 63.5 reduce-scatter.7
  231.0 29.3 all-gather.10
  262.8 29.3 all-gather.14
  294.5 29.3 all-gather.16
  326.8 35.2 reduce-scatter.9
  364.3 34.2 reduce-scatter.13
  400.9 39.2 reduce-scatter.15
  442.3 41.3 reduce-scatter.17
  486.0 41.4 reduce-scatter.19
where the time goes:
time: 558 us; the launch traced here: 550 us
  waiting for transfers between devices  186 us (33%)
  matrix products  102 us (18%)
  other arithmetic  91.8 us (16%)
  local copies, waits for them, and re-layouts  81.5 us (15%)
  blocking collectives  73.5 us (13%)
  between operations  14.5 us (3%)
    reduce_scatter x1, waiting for transfers between devices, on_device(): lax.psum_scatter(jnp.concatenate([jnp.dot(row_block, gate_full, preferred...  67.1 us
    convert_element_type x6, local copies, waits for them, and re-layouts, expand_keep(): jnp.repeat(jnp.repeat(keep, BLOCK, axis=0), BLOCK, axis=1)  30.1 us
    all_gather x1, waiting for transfers between devices, on_device(): lax.all_gather(activate(gate_part, up_part), 'row', axis=0, tiled=True)  28 us
    unnamed x36, local copies, waits for them, and re-layouts  26.2 us
    reduce_scatter x1, waiting for transfers between devices, on_device(): lax.psum_scatter(down_local, 'dp', scatter_dimension=0, tiled=True)  25.6 us
    broadcast_in_dim x4, local copies, waits for them, and re-layouts, expand_keep(): jnp.repeat(jnp.repeat(keep, BLOCK, axis=0), BLOCK, axis=1)  25.1 us
    all_gather x1, waiting for transfers between devices, on_device(): lax.all_gather(up_grad, 'row', axis=0, tiled=True)  22 us
    mul x1, other arithmetic, on_device(): grad_gate = gate_total * expand_keep(gate_keep, jnp.float32)  21.9 us
  transfers between devices with their start and end apart: 13, of which 7 were waited for; matrix products, arithmetic and copies ran while one was open for 43% of the time, Pallas kernels for 0%

commit v1 on v0

v1 whole, which is shorter than its diff:
```python
import functools
import jax
import jax.numpy as jnp
from jax import lax
from jax.experimental import pallas as pl
from jax.experimental.pallas import tpu as pltpu
from jax.sharding import PartitionSpec as P

BLOCK = 128
VMEM_BYTES = 44 * 1024 * 1024
BF16 = jnp.bfloat16
F32 = jnp.float32


def block_edge(extent):
    return 256 if extent % 256 == 0 else 128


def masked(weight, mask):
    groups, width = mask.shape
    shaped = weight.reshape(groups, BLOCK, width) * mask[:, None, :]
    return shaped.reshape(groups * BLOCK, width)


def swap(value, axis, size, step):
    return lax.ppermute(value, axis, [(i, i ^ step) for i in range(size)])


def shift(value, axis, size, step):
    return lax.ppermute(value, axis, [(i, (i + step) % size) for i in range(size)])


def kernel_params(steps):
    return pltpu.CompilerParams(
        dimension_semantics=("arbitrary",) * steps, vmem_limit_bytes=VMEM_BYTES
    )


def whole(shape):
    return pl.BlockSpec(shape, lambda *_: (0,) * len(shape))


def place_rows(result, plan, outs, lead):
    for ref, pieces in zip(outs, plan):
        at = 0
        for start, count in pieces:
            rows = result[start : start + count].astype(ref.dtype)
            if lead is None:
                ref[at : at + count, :] = rows
            else:
                ref[lead, at : at + count, :] = rows
            at += count


def plan_rows(pieces):
    return sum(count for _, count in pieces)


def project_kernel(ring, plan, by_unit, amount, place_ref, *refs):
    parts, refs = refs[: max(1, 2 * ring)], refs[max(1, 2 * ring) :]
    weights, masks, rows_ref, outs = refs[:amount], refs[amount : 2 * amount], refs[2 * amount], refs[2 * amount + 1 :]

    @pl.when(pl.program_id(0) == 0)
    def _():
        if not ring:
            rows_ref[...] = parts[0][...]
        else:
            place = place_ref[0]
            unit = parts[0].shape[0]
            for slot in range(ring):
                for source in range(ring):

                    @pl.when((place ^ slot) == source)
                    def _(slot=slot, source=source):
                        at = 2 * unit * slot
                        rows_ref[at : at + unit, :] = parts[source][...]
                        rows_ref[at + unit : at + 2 * unit, :] = parts[ring + source][...]

    rows = rows_ref[...]
    for lead, (weight, mask) in enumerate(zip(weights, masks)):
        if by_unit:
            result = lax.dot_general(
                rows, masked(weight[...], mask[0]), (((1,), (1,)), ((), ())), preferred_element_type=F32
            )
        else:
            result = jnp.dot(rows, masked(weight[...], mask[...]), preferred_element_type=F32)
        place_rows(result, plan, outs, lead)


def project(place, parts, weights, masks, plan, by_unit):
    ring = len(parts) // 2
    amount = len(weights)
    features = parts[0].shape[1]
    tokens = sum(part.shape[0] for part in parts)
    units = weights[0].shape[0] if by_unit else weights[0].shape[1]
    edge = block_edge(units)
    groups = features // BLOCK
    if by_unit:
        weight_spec = pl.BlockSpec((edge, features), lambda j, _: (j, 0))
        mask_spec = pl.BlockSpec((1, edge // BLOCK, features), lambda j, _: (j, 0, 0))
        masks = [mask.reshape(units // edge, edge // BLOCK, features) for mask in masks]
    else:
        weight_spec = pl.BlockSpec((features, edge), lambda j, _: (0, j))
        mask_spec = pl.BlockSpec((groups, edge), lambda j, _: (0, j))
    counts = [plan_rows(pieces) for pieces in plan]
    return pl.pallas_call(
        functools.partial(project_kernel, ring, plan, by_unit, amount),
        grid_spec=pltpu.PrefetchScalarGridSpec(
            num_scalar_prefetch=1,
            grid=(units // edge,),
            in_specs=[whole(part.shape) for part in parts] + [weight_spec] * amount + [mask_spec] * amount,
            out_specs=[whole((tokens, features))]
            + [pl.BlockSpec((amount, count, edge), lambda j, _: (0, 0, j)) for count in counts],
        ),
        out_shape=[jax.ShapeDtypeStruct((tokens, features), BF16)]
        + [jax.ShapeDtypeStruct((amount, count, units), BF16) for count in counts],
        compiler_params=kernel_params(1),
        cost_estimate=pl.CostEstimate(
            flops=2 * tokens * features * units * amount,
            bytes_accessed=2 * amount * features * units + 4 * tokens * features,
            transcendentals=0,
        ),
    )(place, *parts, *weights, *masks)


def contract_kernel(pieces, plan, by_unit, amount, *refs):
    parts, refs = refs[: len(pieces)], refs[len(pieces) :]
    weights, masks, rows_ref, outs = refs[:amount], refs[amount : 2 * amount], refs[2 * amount], refs[2 * amount + 1 :]

    @pl.when(pl.program_id(0) == 0)
    def _():
        at = 0
        for part, count in zip(parts, pieces):
            rows_ref[:, at : at + count, :] = part[...]
            at += count

    total = None
    for lead, (weight, mask) in enumerate(zip(weights, masks)):
        if by_unit:
            result = jnp.dot(rows_ref[lead], masked(weight[...], mask[...]), preferred_element_type=F32)
        else:
            result = lax.dot_general(
                rows_ref[lead],
                masked(weight[...], mask[0]),
                (((1,), (1,)), ((), ())),
                preferred_element_type=F32,
            )
        total = result if total is None else total + result
    place_rows(total, plan, outs, None)


def contract(parts, weights, masks, plan, types, by_unit):
    amount = len(weights)
    units = parts[0].shape[2]
    pieces = [part.shape[1] for part in parts]
    tokens = sum(pieces)
    features = weights[0].shape[1] if by_unit else weights[0].shape[0]
    edge = block_edge(features)
    if by_unit:
        weight_spec = pl.BlockSpec((units, edge), lambda j: (0, j))
        mask_spec = pl.BlockSpec((units // BLOCK, edge), lambda j: (0, j))
    else:
        weight_spec = pl.BlockSpec((edge, units), lambda j: (j, 0))
        mask_spec = pl.BlockSpec((1, edge // BLOCK, units), lambda j: (j, 0, 0))
        masks = [mask.reshape(features // edge, edge // BLOCK, units) for mask in masks]
    counts = [plan_rows(piece) for piece in plan]
    return pl.pallas_call(
        functools.partial(contract_kernel, pieces, plan, by_unit, amount),
        grid=(features // edge,),
        in_specs=[whole(part.shape) for part in parts] + [weight_spec] * amount + [mask_spec] * amount,
        out_specs=[whole((amount, tokens, units))]
        + [pl.BlockSpec((count, edge), lambda j: (0, j)) for count in counts],
        out_shape=[jax.ShapeDtypeStruct((amount, tokens, units), BF16)]
        + [jax.ShapeDtypeStruct((count, features), kind) for count, kind in zip(counts, types)],
        compiler_params=kernel_params(1),
        cost_estimate=pl.CostEstimate(
            flops=2 * tokens * features * units * amount,
            bytes_accessed=2 * amount * features * units + 4 * amount * tokens * units,
            transcendentals=0,
        ),
    )(*parts, *weights, *masks)


def outer_kernel(left_ref, right_ref, *refs):
    amount = right_ref.shape[0]
    masks, outs = refs[:amount], refs[amount:]
    for lead in range(amount):
        result = lax.dot_general(
            left_ref[...], right_ref[lead], (((0,), (0,)), ((), ())), preferred_element_type=F32
        )
        outs[lead][...] = masked(result, masks[lead][0].astype(F32))


def outer(left, right, masks):
    tokens, rows = left.shape
    amount, _, width = right.shape
    edge = block_edge(rows)
    masks = [mask.reshape(rows // edge, edge // BLOCK, width) for mask in masks]
    return pl.pallas_call(
        outer_kernel,
        grid=(rows // edge,),
        in_specs=[pl.BlockSpec((tokens, edge), lambda j: (0, j)), whole(right.shape)]
        + [pl.BlockSpec((1, edge // BLOCK, width), lambda j: (j, 0, 0))] * amount,
        out_specs=[pl.BlockSpec((edge, width), lambda j: (j, 0))] * amount,
        out_shape=[jax.ShapeDtypeStruct((rows, width), F32)] * amount,
        compiler_params=kernel_params(1),
        cost_estimate=pl.CostEstimate(
            flops=2 * tokens * rows * width * amount,
            bytes_accessed=4 * amount * rows * width + 2 * tokens * (rows + amount * width),
            transcendentals=0,
        ),
    )(left, right, *masks)


def activation(gate, up_value, hidden_grad):
    sigmoid_gate = 1.0 / (1.0 + jnp.exp(-gate))
    scaled = gate * sigmoid_gate
    hidden = scaled * up_value
    gate_grad = hidden_grad * up_value * sigmoid_gate * (1.0 + gate * (1.0 - sigmoid_gate))
    up_grad = hidden_grad * scaled
    return hidden, gate_grad, up_grad


def activate_kernel(pair0, pair_x, pair_y, pair_y2, pair_x2, one0, one_x, one_y, one_y2, one_x2, hidden_ref, grads_ref):
    half = pair_y2.shape[1]

    def summed(refs, lead, second):
        own, first_x, first_y, last_y, last_x = refs
        first, last = (first_y, last_x) if second else (first_x, last_y)
        at = half if second else 0
        return (
            own[lead, at : at + half, :].astype(F32)
            + first[lead, half:, :].astype(F32)
            + last[lead].astype(F32)
        )

    pair = (pair0, pair_x, pair_y, pair_y2, pair_x2)
    one = (one0, one_x, one_y, one_y2, one_x2)
    for second in (False, True):
        at = half if second else 0
        results = activation(summed(pair, 0, second), summed(pair, 1, second), summed(one, 0, second))
        hidden_ref[0, at : at + half, :] = results[0].astype(BF16)
        grads_ref[0, at : at + half, :] = results[1].astype(BF16)
        grads_ref[1, at : at + half, :] = results[2].astype(BF16)


def activate(pair, one):
    _, share, units = pair[0].shape
    edge = block_edge(units)
    spec = lambda array: pl.BlockSpec(array.shape[:2] + (edge,), lambda j: (0, 0, j))
    outs = [jax.ShapeDtypeStruct((amount, share, units), BF16) for amount in (1, 2)]
    return pl.pallas_call(
        activate_kernel,
        grid=(units // edge,),
        in_specs=[spec(array) for array in pair + one],
        out_specs=[spec(array) for array in outs],
        out_shape=outs,
        compiler_params=kernel_params(1),
    )(*pair, *one)


def widen(keep):
    return jnp.repeat(keep, BLOCK, axis=1).astype(BF16)


def finish(token_f, inv_rms, norm_gain, normed_grad, inner_sum, gain_sum):
    grad_gain = gain_sum(jnp.sum(normed_grad * token_f * inv_rms, axis=0))
    inner_dot = inner_sum(jnp.sum(norm_gain * normed_grad * token_f, axis=1))
    width = norm_gain.shape[0] * lax.axis_size("row")
    grad_tokens = (
        inv_rms * norm_gain * normed_grad
        - token_f * inv_rms * inv_rms * inv_rms * inner_dot[:, None] / width
    )
    return grad_tokens, grad_gain


def exchange_device(
    tokens, norm_gain, gate_weight, up_weight, down_weight, gate_keep, up_keep, down_keep, cotangent
):
    rows, cols = 4, 4
    unit, features = tokens.shape
    place = lax.axis_index("row")
    place_arg = place.astype(jnp.int32).reshape(1)
    level = lax.axis_index("col")

    def row_sum(value):
        return value + swap(value, "row", rows, 1) + swap(value, "row", rows, 2) + swap(value, "row", rows, 3)

    def spread(value):
        own = [value] + [shift(value, "col", cols, step) for step in range(1, cols)]
        return own + [swap(part, "dp", 2, 1) for part in own]

    def exchange_sum(x_first, y_first, x_keep, y_keep, kept):
        half = x_keep.shape[1]
        got_x = swap(x_first, "row", rows, 1)
        got_y = swap(y_first, "row", rows, 2)
        add = lambda a, b: (a.astype(F32) + b[:, :half].astype(F32)).astype(BF16)
        last_y = swap(add(y_keep, got_x), "row", rows, 2)
        last_x = swap(add(x_keep, got_y), "row", rows, 1)
        return [kept, got_x, got_y, last_y, last_x]

    def exchange_gather(share):
        half = share.shape[1] // 2
        got_x = swap(share, "row", rows, 1)
        got_y = swap(share, "row", rows, 2)
        far_x = swap(got_y[:, :half], "row", rows, 1)
        far_y = swap(got_x[:, half:], "row", rows, 2)
        return [share, got_x, got_y, far_x, far_y]

    def owner_sum(own, other):
        got = swap(other, "dp", 2, 1)
        total = None
        for step in range(cols):
            at = (place ^ step) * unit
            part = lax.dynamic_slice_in_dim(own, at, unit, 0) + lax.dynamic_slice_in_dim(got, at, unit, 0).astype(F32)
            if step:
                part = shift(part.astype(BF16), "col", cols, -step).astype(F32)
            total = part if total is None else total + part
        return total

    def gain_sum(value):
        value = value + swap(value, "dp", 2, 1)
        parts = jnp.stack([value] + [shift(value, "col", cols, step) for step in range(1, cols)])
        return jnp.sum(jnp.take(parts, (level - jnp.arange(cols)) % cols, axis=0), axis=0)

    token_f = tokens.astype(F32)
    square = row_sum(jnp.sum(token_f * token_f, axis=1))
    inv_rms = lax.rsqrt(square[:, None] / (features * rows) + 1e-05)
    normed = (token_f * inv_rms * norm_gain).astype(BF16)
    gate_mask, up_mask, down_mask = widen(gate_keep), widen(up_keep), widen(down_keep)

    def rows_of(slot, second):
        return (2 * unit * slot + (unit if second else 0), unit)

    first_plan = [
        [rows_of(3, False), rows_of(1, False)],
        [rows_of(3, True), rows_of(2, True)],
        [rows_of(1, True)],
        [rows_of(2, False)],
        [(0, 2 * unit)],
    ]
    last_plan = [[rows_of(slot, False) for slot in range(rows)], [rows_of(slot, True) for slot in range(rows)]]

    seen_cot, *grad_parts = project(place_arg, spread(cotangent), [down_weight], [down_mask], first_plan, True)
    one = exchange_sum(*grad_parts)
    seen_rows, *pair_parts = project(
        place_arg, spread(normed), [gate_weight, up_weight], [gate_mask, up_mask], first_plan, False
    )
    pair = exchange_sum(*pair_parts)
    hidden_share, grads_share = activate(pair, one)
    hidden, branch_own, branch_other = contract(
        exchange_gather(hidden_share), [down_weight], [down_mask], last_plan, (F32, BF16), True
    )
    branch = owner_sum(branch_own, branch_other).astype(BF16)
    (grad_down,) = outer(hidden[0], seen_cot[None], [down_mask])
    grads, normed_own, normed_other = contract(
        exchange_gather(grads_share), [gate_weight, up_weight], [gate_mask, up_mask], last_plan, (F32, BF16), False
    )
    normed_grad = owner_sum(normed_own, normed_other)
    grad_gate, grad_up = outer(seen_rows, grads, [gate_mask, up_mask])
    grad_tokens, grad_gain = finish(token_f, inv_rms, norm_gain, normed_grad, row_sum, gain_sum)
    return (branch, grad_tokens, grad_gain, grad_gate, grad_up, grad_down)


def general_device(
    tokens, norm_gain, gate_weight, up_weight, down_weight, gate_keep, up_keep, down_keep, cotangent
):
    owners = ("dp", "col")
    features = tokens.shape[1]
    place_arg = jnp.zeros((1,), jnp.int32)
    token_f = tokens.astype(F32)
    square = lax.psum(jnp.sum(token_f * token_f, axis=1), "row")
    inv_rms = lax.rsqrt(square[:, None] / (features * lax.axis_size("row")) + 1e-05)
    normed = (token_f * inv_rms * norm_gain).astype(BF16)
    gate_mask, up_mask, down_mask = widen(gate_keep), widen(up_keep), widen(down_keep)
    seen_cot = lax.all_gather(cotangent, owners, axis=0, tiled=True)
    seen_rows = lax.all_gather(normed, owners, axis=0, tiled=True)
    plan = [[(0, seen_cot.shape[0])]]

    def share(value):
        return lax.psum_scatter(value.astype(F32), "row", scatter_dimension=1, tiled=True)

    def collect(value):
        return lax.all_gather(value.astype(BF16), "row", axis=1, tiled=True)

    def owner_sum(value):
        return lax.psum_scatter(value, owners, scatter_dimension=0, tiled=True)

    _, one = project(place_arg, [seen_cot], [down_weight], [down_mask], plan, True)
    _, pair = project(place_arg, [seen_rows], [gate_weight, up_weight], [gate_mask, up_mask], plan, False)
    pair = share(pair)
    hidden, gate_grad, up_grad = activation(pair[0], pair[1], share(one)[0])
    hidden, branch = contract([collect(hidden[None])], [down_weight], [down_mask], plan, (F32,), True)
    branch = owner_sum(branch).astype(BF16)
    grads, normed_grad = contract(
        [collect(jnp.stack([gate_grad, up_grad]))], [gate_weight, up_weight], [gate_mask, up_mask], plan, (F32,), False
    )
    normed_grad = owner_sum(normed_grad)
    (grad_down,) = outer(hidden[0], seen_cot[None], [down_mask])
    grad_gate, grad_up = outer(seen_rows, grads, [gate_mask, up_mask])
    grad_tokens, grad_gain = finish(
        token_f,
        inv_rms,
        norm_gain,
        normed_grad,
        lambda value: lax.psum(value, "row"),
        lambda value: lax.psum(value, owners),
    )
    return (branch, grad_tokens, grad_gain, grad_gate, grad_up, grad_down)


def solution(mesh):
    split = P(("dp", "col"), "row")
    turned = P("row", ("dp", "col"))
    sizes = (mesh.shape["dp"], mesh.shape["row"], mesh.shape["col"])
    on_device = exchange_device if sizes == (2, 4, 4) else general_device
    return jax.shard_map(
        on_device,
        mesh=mesh,
        in_specs=(split, P("row"), turned, turned, split, turned, turned, split, split),
        out_specs=(split, split, P("row"), turned, turned, split),
        check_vma=False,
    )
```

time: 558 us -> 236 us (0.42); the launches traced: 550 us -> 235 us
  matrix products: 102 us -> 0 us
  waiting for transfers between devices: 186 us -> 85.1 us
  other arithmetic: 91.8 us -> 7.52 us
  blocking collectives: 73.5 us -> 0 us
  local copies, waits for them, and re-layouts: 81.5 us -> 8.09 us
  starting transfers between devices: 1 us -> 72.5 us
  Pallas kernels: 0 us -> 60.9 us
  between operations: 14.5 us -> 1.01 us
    reduce_scatter x7 -> x0, waiting for transfers between devices: 113 us -> none  [the longest x1 67.1 us: on_device(): lax.psum_scatter(jnp.concatenate([jnp.dot(row_block, gate_full, preferred...]
    dot_general x9 -> x0, matrix products: 102 us -> none  [the longest x1 12.1 us: on_device(): jnp.dot(row_block, up_full, preferred_element_type=jnp.float32)]
    ppermute x0 -> x48, waiting for transfers between devices: none -> 85.1 us  [the longest x33 53.7 us: swap(): return lax.ppermute(value, axis, [(i, i ^ step) for i in range(size)])]
    mul x6 -> x0, other arithmetic: 77.2 us -> none  [the longest x1 21.9 us: on_device(): grad_gate = gate_total * expand_keep(gate_keep, jnp.float32)]
    ppermute x0 -> x48, starting transfers between devices: none -> 72.5 us  [the longest x15 44 us: shift(): lax.ppermute(value, axis, [(i, (i + step) % size) for i in range(size)])]
    all_gather x6 -> x0, waiting for transfers between devices: 71.7 us -> none  [the longest x1 28 us: on_device(): lax.all_gather(activate(gate_part, up_part), 'row', axis=0, tiled=True)]
    pallas_call x0 -> x7, Pallas kernels: none -> 60.9 us  [the longest x2 19.7 us: outer(): pl.pallas_call(outer_kernel, grid=(rows // edge,), in_specs=[pl.BlockSpec...]
    all_gather x2 -> x0, blocking collectives: 38.3 us -> none  [the longest x1 20.9 us: on_device(): seen_cot = lax.all_gather(cotangent, 'col', axis=0, tiled=True)]
  transfers between devices with their start and end apart: 13 -> 48, of which waited for: 7 -> 18; matrix products, arithmetic and copies ran while one was open for 43% -> 3% of each run, Pallas kernels for 0% -> 25%
where the time goes in v1:
time: 236 us; the launch traced here: 235 us
  waiting for transfers between devices  85.1 us (36%)
  starting transfers between devices  72.5 us (31%)
  Pallas kernels  60.9 us (26%)
  local copies, waits for them, and re-layouts  8.09 us (3%)
  other arithmetic  7.52 us (3%)
    ppermute x33, waiting for transfers between devices, swap(): return lax.ppermute(value, axis, [(i, i ^ step) for i in range(size)])  53.7 us
    ppermute x15, starting transfers between devices, shift(): lax.ppermute(value, axis, [(i, (i + step) % size) for i in range(size)])  44 us
    ppermute x15, waiting for transfers between devices, shift(): lax.ppermute(value, axis, [(i, (i + step) % size) for i in range(size)])  31.4 us
    ppermute x33, starting transfers between devices, swap(): return lax.ppermute(value, axis, [(i, i ^ step) for i in range(size)])  28.5 us
    pallas_call x2, Pallas kernels, outer(): pl.pallas_call(outer_kernel, grid=(rows // edge,), in_specs=[pl.BlockSpec...  19.7 us
    pallas_call x2, Pallas kernels, contract(): pl.pallas_call(functools.partial(contract_kernel, pieces, plan, by_unit,...  19.4 us
    pallas_call x2, Pallas kernels, project(): pl.pallas_call(functools.partial(project_kernel, ring, plan, by_unit, amo...  18.6 us
    unnamed x30, local copies, waits for them, and re-layouts  6.15 us
  transfers between devices with their start and end apart: 48, of which 18 were waited for; matrix products, arithmetic and copies ran while one was open for 3% of the time, Pallas kernels for 25%

profile of v1, /device:TPU:0, one launch (start us, length us, event | category | flops | bytes accessed | tf_op | source)
XLA Modules:
  0.0 235.2 jit_solution(10736492469754755797)
XLA Ops:
  1.7 4.0 %collective-permute-start.2 = (f32[48]{0:T(128)S(1)}, f32[48]{0:T(128)S(1)}, u32[]{:S(2)}, u32[]{:S(2)}) collective-permute-start(f32[48]{0:T(128)S(1)} %fusion.7), channel_id=1, source_target_pairs={{0,12},{4,8},{8,4},{12,0},{1,13},{5,9},{9,5},{13,1},{2,14},{6,10},... | collective-permute-start | bytes 584 | tf_op jit(solution)/shard_map/ppermute | solution.py:26
  8.3 2.6 %collective-permute-start.15 = (bf16[48,2048]{1,0:T(8,128)(2,1)}, bf16[48,2048]{1,0:T(8,128)(2,1)S(1)}, u32[]{:S(2)}, u32[]{:S(2)}) collective-permute-start(bf16[48,2048]{1,0:T(8,128)(2,1)} %refs_0_.1), channel_id=1, source_target_pairs={{0,2},{1,3},{2,0},{3,1},{4,6},{5,7},{6,4},{7,5},{8,10},{9,11},{10,... | collective-permute-start | bytes 589832 | tf_op jit(solution)/shard_map/ppermute | solution.py:30
  16.4 9.3 %collective-permute-start.4 = (bf16[48,2048]{1,0:T(8,128)(2,1)S(1)}, bf16[48,2048]{1,0:T(8,128)(2,1)S(1)}, u32[]{:S(2)}, u32[]{:S(2)}) collective-permute-start(bf16[48,2048]{1,0:T(8,128)(2,1)S(1)} %fusion.2.refs_0_), channel_id=1, source_target_pairs={{0,2},{1,3},{2,0},{3,1},{4,6},{5,7},{6,4},{7,5},{8,10},{9,11},{10,... | collective-permute-start | bytes 589832 | tf_op jit(solution)/shard_map/ppermute | solution.py:30
  25.8 11.4 %collective-permute-start.5 = (bf16[48,2048]{1,0:T(8,128)(2,1)S(1)}, bf16[48,2048]{1,0:T(8,128)(2,1)S(1)}, u32[]{:S(2)}, u32[]{:S(2)}) collective-permute-start(bf16[48,2048]{1,0:T(8,128)(2,1)S(1)} %fusion.2.refs_0_), channel_id=1, source_target_pairs={{0,3},{1,0},{2,1},{3,2},{4,7},{5,4},{6,5},{7,6},{8,11},{9,8},{10,9... | collective-permute-start | bytes 589832 | tf_op jit(solution)/shard_map/ppermute | solution.py:30
  46.7 7.8 %shard_map.137 = (bf16[384,2048]{1,0:T(8,128)(2,1)S(1)}, bf16[1,96,1792]{2,1,0:T(8,128)(2,1)S(1)}, bf16[1,96,1792]{2,1,0:T(8,128)(2,1)S(1)}, bf16[1,48,1792]{2,1...) custom-call(s32[1]{0:T(128)} %bitcast.place_ref, bf16[48,2048]{1,0:T(8,128)(2,1)S(1)} %copy-done, ...), custom_call_target="tpu_custom_call" | custom-call | flops 2818572288 | bytes 10485760 | tf_op jit(solution)/shard_map/pallas_call | solution.py:106
  56.0 10.8 %shard_map.136 = (bf16[384,2048]{1,0:T(8,128)(2,1)S(1)}, bf16[2,96,1792]{2,1,0:T(8,128)(2,1)S(1)}, bf16[2,96,1792]{2,1,0:T(8,128)(2,1)S(1)}, bf16[2,48,1792]{2,1...) custom-call(s32[1]{0:T(128)} %bitcast.place_ref, ...), custom_call_target="tpu_custom_call" | custom-call | flops 5637144576 | bytes 17825792 | tf_op jit(solution)/shard_map/pallas_call | solution.py:106
  72.1 13.4 %collective-permute-done.10.pair_x = bf16[2,96,1792]{2,1,0:T(8,128)(2,1)S(1)} collective-permute-done((bf16[2,96,1792]{2,1,0:T(8,128)(2,1)S(1)}, bf16[2,96,1792]{2,1,0:T(8,128)(2,1)S(1)}, u32[]{:S(2)}, u32[]{:S(2)}) %collective-permute-start.10) | collective-permute-done | bytes 688160 | tf_op jit(solution)/shard_map/ppermute | solution.py:26
  87.2 7.0 %collective-permute-done.11.pair_y = bf16[2,96,1792]{2,1,0:T(8,128)(2,1)S(1)} collective-permute-done((bf16[2,96,1792]{2,1,0:T(8,128)(2,1)S(1)}, bf16[2,96,1792]{2,1,0:T(8,128)(2,1)S(1)}, u32[]{:S(2)}, u32[]{:S(2)}) %collective-permute-start.11) | collective-permute-done | bytes 688160 | tf_op jit(solution)/shard_map/ppermute | solution.py:26
  97.9 8.1 %collective-permute-done.24.one_x2 = bf16[1,48,1792]{2,1,0:T(8,128)(2,1)S(1)} collective-permute-done((bf16[1,48,1792]{2,1,0:T(8,128)(2,1)S(1)}, bf16[1,48,1792]{2,1,0:T(8,128)(2,1)S(1)}, u32[]{:S(2)}, u32[]{:S(2)}) %collective-permute-start.24) | collective-permute-done | bytes 172064 | tf_op jit(solution)/shard_map/ppermute | solution.py:26
  106.0 3.3 %shard_map.138 = (bf16[1,96,1792]{2,1,0:T(8,128)(2,1)}, bf16[2,96,1792]{2,1,0:T(8,128)(2,1)}) custom-call(bf16[2,96,1792]{2,1,0:T(8,128)(2,1)S(1)} %get-tuple-element.28.pair0, bf16[2,96,1792]{2,1,0:T(8,128)(2,1)S(1)} %collective-permute-done.10.pair_x, bf16[2,96,1792]{2,1,0:T(8,128)(2,1)S(1)} %collective-permute-done.11.pair_y, ...), custom_call_target="tpu_custom_call" | custom-call | tf_op jit(solution)/shard_map/pallas_call | solution.py:252
  114.3 17.1 %collective-permute-done.26.refs_2_ = bf16[1,96,1792]{2,1,0:T(8,128)(2,1)S(1)} collective-permute-done((bf16[1,96,1792]{2,1,0:T(8,128)(2,1)}, bf16[1,96,1792]{2,1,0:T(8,128)(2,1)S(1)}, u32[]{:S(2)}, u32[]{:S(2)}) %collective-permute-start.26) | collective-permute-done | bytes 344096 | tf_op jit(solution)/shard_map/ppermute | solution.py:26
  137.6 2.1 collective-permute-start.36
  141.4 8.1 %shard_map.139 = (bf16[1,384,1792]{2,1,0:T(8,128)(2,1)S(1)}, f32[192,2048]{1,0:T(8,128)S(1)}, bf16[192,2048]{1,0:T(8,128)(2,1)S(1)}) custom-call(bf16[1,96,1792]{2,1,0:T(8,128)(2,1)} %get-tuple-element.38.refs_0_, bf16[1,96,1792]{2,1,0:T(8,128)(2,1)} %collective-permute-done.25.refs_1_, bf16[1,96,1792]{2,1,0:T(8,128)(2,1)S(1)} %collective-permute-done.26.refs_2_, ...), custom_call_target="tpu_custom_call" | custom-call | flops 2818572288 | bytes 10092544 | tf_op jit(solution)/shard_map/pallas_call | solution.py:167
  149.6 11.3 %shard_map.140 = (bf16[2,384,1792]{2,1,0:T(8,128)(2,1)S(1)}, f32[192,2048]{1,0:T(8,128)S(1)}, bf16[192,2048]{1,0:T(8,128)(2,1)S(1)}) custom-call(bf16[2,96,1792]{2,1,0:T(8,128)(2,1)} %get-tuple-element.41.refs_0_, bf16[2,96,1792]{2,1,0:T(8,128)(2,1)S(1)} %collective-permute-done.33.refs_1_, bf16[2,96,1792]{2,1,0:T(8,128)(2,1)S(1)} %collective-permute-done.34.refs_2_, ...), custom_call_target="tpu_custom_call" | custom-call | flops 5637144576 | bytes 20185088 | tf_op jit(solution)/shard_map/pallas_call | solution.py:167
  161.4 8.3 %shard_map.142 = f32[1792,2048]{1,0:T(8,128)} custom-call(bf16[384,1792]{1,0:T(8,128)(2,1)S(1)} %bitcast.19, bf16[1,384,2048]{2,1,0:T(8,128)(2,1)S(1)} %bitcast.18, bf16[7,2,2048]{2,1,0:T(2,128)(2,1)S(1)} %convert_element_type.139.refs_9_.refs_0_), custom_call_target="tpu_custom_call" | custom-call | flops 2818572288 | bytes 17629184 | tf_op jit(solution)/shard_map/pallas_call | solution.py:199
  169.7 11.4 %shard_map.141 = (f32[2048,1792]{1,0:T(8,128)}, f32[2048,1792]{1,0:T(8,128)}) custom-call(bf16[384,2048]{1,0:T(8,128)(2,1)S(1)} %copy-done.6, bf16[2,384,1792]{2,1,0:T(8,128)(2,1)S(1)} %get-tuple-element.45.right_ref, bf16[8,2,1792]{2,1,0:T(2,128)(2,1)S(1)} %convert_element_type.158.refs_7_.refs_0_, bf16[8,2,1792]{2,1,0:T(2,128)(2,1)S(1)} %convert_element_type.159.refs_8_.refs_1_), custom_call_target="tpu_custom_call" | custom-call | flops 5637144576 | bytes 33685504 | tf_op jit(solution)/shard_map/pallas_call | solution.py:199
  181.3 2.8 %collective-permute-start.32 = (bf16[48,2048]{1,0:T(8,128)(2,1)S(1)}, bf16[48,2048]{1,0:T(8,128)(2,1)S(1)}, u32[]{:S(2)}, u32[]{:S(2)}) collective-permute-start(bf16[48,2048]{1,0:T(8,128)(2,1)S(1)} %get-tuple-element.57), channel_id=1, source_target_pairs={{0,1},{1,2},{2,3},{3,0},{4,5},{5,6},{6,7},{7,4},{8,9},{9,10},{10,1... | collective-permute-start | bytes 589832 | tf_op jit(solution)/shard_map/ppermute | solution.py:30
  191.1 2.5 %collective-permute-start.38 = (bf16[48,2048]{1,0:T(8,128)(2,1)S(1)}, bf16[48,2048]{1,0:T(8,128)(2,1)S(1)}, u32[]{:S(2)}, u32[]{:S(2)}) collective-permute-start(bf16[48,2048]{1,0:T(8,128)(2,1)S(1)} %get-tuple-element.53), channel_id=1, source_target_pairs={{0,3},{1,0},{2,1},{3,2},{4,7},{5,4},{6,5},{7,6},{8,11},{9,8},{10,9... | collective-permute-start | bytes 589832 | tf_op jit(solution)/shard_map/ppermute | solution.py:30
  193.6 6.0 %collective-permute-done.31 = bf16[48,2048]{1,0:T(8,128)(2,1)S(1)} collective-permute-done((bf16[48,2048]{1,0:T(8,128)(2,1)S(1)}, bf16[48,2048]{1,0:T(8,128)(2,1)S(1)}, u32[]{:S(2)}, u32[]{:S(2)}) %collective-permute-start.31) | collective-permute-done | bytes 196640 | tf_op jit(solution)/shard_map/ppermute | solution.py:30
  200.3 3.4 %collective-permute-done.40 = bf16[48,2048]{1,0:T(8,128)(2,1)S(1)} collective-permute-done((bf16[48,2048]{1,0:T(8,128)(2,1)S(1)}, bf16[48,2048]{1,0:T(8,128)(2,1)S(1)}, u32[]{:S(2)}, u32[]{:S(2)}) %collective-permute-start.40) | collective-permute-done | bytes 196640 | tf_op jit(solution)/shard_map/ppermute | solution.py:30
  203.7 11.7 %collective-permute-done.39 = bf16[48,2048]{1,0:T(8,128)(2,1)S(1)} collective-permute-done((bf16[48,2048]{1,0:T(8,128)(2,1)S(1)}, bf16[48,2048]{1,0:T(8,128)(2,1)S(1)}, u32[]{:S(2)}, u32[]{:S(2)}) %collective-permute-start.39) | collective-permute-done | bytes 196640 | tf_op jit(solution)/shard_map/ppermute | solution.py:30
  216.7 2.0 collective-permute-start.42
  222.3 5.6 %collective-permute-start.47 = (f32[2048]{0:T(1024)S(1)}, f32[2048]{0:T(1024)S(1)}, u32[]{:S(2)}, u32[]{:S(2)}) collective-permute-start(f32[2048]{0:T(1024)S(1)} %add.170), channel_id=1, source_target_pairs={{0,3},{1,0},{2,1},{3,2},{4,7},{5,4},{6,5},{7,6},{8,11},{9,8},{10,9... | collective-permute-start | bytes 24584 | tf_op jit(solution)/shard_map/ppermute | solution.py:30
  229.5 3.0 %collective-permute-done.46 = f32[2048]{0:T(1024)S(1)} collective-permute-done((f32[2048]{0:T(1024)S(1)}, f32[2048]{0:T(1024)S(1)}, u32[]{:S(2)}, u32[]{:S(2)}) %collective-permute-start.46) | collective-permute-done | bytes 8224 | tf_op jit(solution)/shard_map/ppermute | solution.py:30
  (143 shorter events, 61.2 us)
Async XLA Ops:
  8.3 17.5 %collective-permute-start.15 = (bf16[48,2048]{1,0:T(8,128)(2,1)}, bf16[48,2048]{1,0:T(8,128)(2,1)S(1)}, u32[]{:S(2)}, u32[]{:S(2)}) collective-permute-start(bf16[48,2048]{1,0:T(8,128)(2,1)} %refs_0_.1), channel_id=1, source_target_pairs={{0,2},{1,3},{2,0},{3,1},{4,6},{5,7},{6,4},{7,5},{8,10},{9,11},{10,... | collective-permute-start | bytes 589832 | tf_op jit(solution)/shard_map/ppermute | solution.py:30
  10.9 26.3 %collective-permute-start.16 = (bf16[48,2048]{1,0:T(8,128)(2,1)}, bf16[48,2048]{1,0:T(8,128)(2,1)S(1)}, u32[]{:S(2)}, u32[]{:S(2)}) collective-permute-start(bf16[48,2048]{1,0:T(8,128)(2,1)} %refs_0_.1), channel_id=1, source_target_pairs={{0,3},{1,0},{2,1},{3,2},{4,7},{5,4},{6,5},{7,6},{8,11},{9,8},{10,9... | collective-permute-start | bytes 589832 | tf_op jit(solution)/shard_map/ppermute | solution.py:30
  12.2 25.0 %collective-permute-start.17 = (bf16[48,2048]{1,0:T(8,128)(2,1)}, bf16[48,2048]{1,0:T(8,128)(2,1)S(1)}, u32[]{:S(2)}, u32[]{:S(2)}) collective-permute-start(bf16[48,2048]{1,0:T(8,128)(2,1)} %refs_0_.1), channel_id=1, source_target_pairs={{0,16},{16,0},{1,17},{17,1},{2,18},{18,2},{3,19},{19,3},{4,20},{20... | collective-permute-start | bytes 589832 | tf_op jit(solution)/shard_map/ppermute | solution.py:26
  13.3 24.4 %collective-permute-start.3 = (bf16[48,2048]{1,0:T(8,128)(2,1)S(1)}, bf16[48,2048]{1,0:T(8,128)(2,1)S(1)}, u32[]{:S(2)}, u32[]{:S(2)}) collective-permute-start(bf16[48,2048]{1,0:T(8,128)(2,1)S(1)} %fusion.2.refs_0_), channel_id=1, source_target_pairs={{0,1},{1,2},{2,3},{3,0},{4,5},{5,6},{6,7},{7,4},{8,9},{9,10},{10,1... | collective-permute-start | bytes 589832 | tf_op jit(solution)/shard_map/ppermute | solution.py:30
  16.4 23.6 %collective-permute-start.4 = (bf16[48,2048]{1,0:T(8,128)(2,1)S(1)}, bf16[48,2048]{1,0:T(8,128)(2,1)S(1)}, u32[]{:S(2)}, u32[]{:S(2)}) collective-permute-start(bf16[48,2048]{1,0:T(8,128)(2,1)S(1)} %fusion.2.refs_0_), channel_id=1, source_target_pairs={{0,2},{1,3},{2,0},{3,1},{4,6},{5,7},{6,4},{7,5},{8,10},{9,11},{10,... | collective-permute-start | bytes 589832 | tf_op jit(solution)/shard_map/ppermute | solution.py:30
  25.8 16.2 %collective-permute-start.5 = (bf16[48,2048]{1,0:T(8,128)(2,1)S(1)}, bf16[48,2048]{1,0:T(8,128)(2,1)S(1)}, u32[]{:S(2)}, u32[]{:S(2)}) collective-permute-start(bf16[48,2048]{1,0:T(8,128)(2,1)S(1)} %fusion.2.refs_0_), channel_id=1, source_target_pairs={{0,3},{1,0},{2,1},{3,2},{4,7},{5,4},{6,5},{7,6},{8,11},{9,8},{10,9... | collective-permute-start | bytes 589832 | tf_op jit(solution)/shard_map/ppermute | solution.py:30
  40.0 16.0 %collective-permute-start.6 = (bf16[48,2048]{1,0:T(8,128)(2,1)S(1)}, bf16[48,2048]{1,0:T(8,128)(2,1)S(1)}, u32[]{:S(2)}, u32[]{:S(2)}) collective-permute-start(bf16[48,2048]{1,0:T(8,128)(2,1)S(1)} %fusion.2.refs_0_), channel_id=1, source_target_pairs={{0,16},{16,0},{1,17},{17,1},{2,18},{18,2},{3,19},{19,3},{4,20},{20... | collective-permute-start | bytes 589832 | tf_op jit(solution)/shard_map/ppermute | solution.py:26
  54.4 16.1 %collective-permute-start.21 = (bf16[1,96,1792]{2,1,0:T(8,128)(2,1)S(1)}, bf16[1,96,1792]{2,1,0:T(8,128)(2,1)S(1)}, u32[]{:S(2)}, u32[]{:S(2)}) collective-permute-start(bf16[1,96,1792]{2,1,0:T(8,128)(2,1)S(1)} %get-tuple-element.34), channel_id=1, source_target_pairs={{0,4},{4,0},{8,12},{12,8},{1,5},{5,1},{9,13},{13,9},{2,6},{6,2},{1... | collective-permute-start | bytes 1032200 | tf_op jit(solution)/shard_map/ppermute | solution.py:26
  67.9 17.6 %collective-permute-start.10 = (bf16[2,96,1792]{2,1,0:T(8,128)(2,1)S(1)}, bf16[2,96,1792]{2,1,0:T(8,128)(2,1)S(1)}, u32[]{:S(2)}, u32[]{:S(2)}) collective-permute-start(bf16[2,96,1792]{2,1,0:T(8,128)(2,1)S(1)} %get-tuple-element.29), channel_id=1, source_target_pairs={{0,4},{4,0},{8,12},{12,8},{1,5},{5,1},{9,13},{13,9},{2,6},{6,2},{1... | collective-permute-start | bytes 2064392 | tf_op jit(solution)/shard_map/ppermute | solution.py:26
  68.5 27.3 %collective-permute-start.22 = (bf16[1,96,1792]{2,1,0:T(8,128)(2,1)S(1)}, bf16[1,96,1792]{2,1,0:T(8,128)(2,1)S(1)}, u32[]{:S(2)}, u32[]{:S(2)}) collective-permute-start(bf16[1,96,1792]{2,1,0:T(8,128)(2,1)S(1)} %get-tuple-element.35), channel_id=1, source_target_pairs={{0,8},{4,12},{8,0},{12,4},{1,9},{5,13},{9,1},{13,5},{2,10},{6,14},... | collective-permute-start | bytes 1032200 | tf_op jit(solution)/shard_map/ppermute | solution.py:26
  70.0 24.2 %collective-permute-start.11 = (bf16[2,96,1792]{2,1,0:T(8,128)(2,1)S(1)}, bf16[2,96,1792]{2,1,0:T(8,128)(2,1)S(1)}, u32[]{:S(2)}, u32[]{:S(2)}) collective-permute-start(bf16[2,96,1792]{2,1,0:T(8,128)(2,1)S(1)} %get-tuple-element.30), channel_id=1, source_target_pairs={{0,8},{4,12},{8,0},{12,4},{1,9},{5,13},{9,1},{13,5},{2,10},{6,14},... | collective-permute-start | bytes 2064392 | tf_op jit(solution)/shard_map/ppermute | solution.py:26
  70.6 27.3 %collective-permute-start.23 = (bf16[1,48,1792]{2,1,0:T(8,128)(2,1)S(1)}, bf16[1,48,1792]{2,1,0:T(8,128)(2,1)S(1)}, u32[]{:S(2)}, u32[]{:S(2)}) collective-permute-start(bf16[1,48,1792]{2,1,0:T(8,128)(2,1)S(1)} %add_convert_fusion.10), channel_id=1, source_target_pairs={{0,8},{4,12},{8,0},{12,4},{1,9},{5,13},{9,1},{13,5},{2,10},{6,14},... | collective-permute-start | bytes 516104 | tf_op jit(solution)/shard_map/ppermute | solution.py:26
  85.6 20.4 %collective-permute-start.12 = (bf16[2,48,1792]{2,1,0:T(8,128)(2,1)S(1)}, bf16[2,48,1792]{2,1,0:T(8,128)(2,1)S(1)}, u32[]{:S(2)}, u32[]{:S(2)}) collective-permute-start(bf16[2,48,1792]{2,1,0:T(8,128)(2,1)S(1)} %add_convert_fusion.1), channel_id=1, source_target_pairs={{0,8},{4,12},{8,0},{12,4},{1,9},{5,13},{9,1},{13,5},{2,10},{6,14},... | collective-permute-start | bytes 1032200 | tf_op jit(solution)/shard_map/ppermute | solution.py:26
  109.3 26.7 %collective-permute-start.34 = (bf16[2,96,1792]{2,1,0:T(8,128)(2,1)}, bf16[2,96,1792]{2,1,0:T(8,128)(2,1)S(1)}, u32[]{:S(2)}, u32[]{:S(2)}) collective-permute-start(bf16[2,96,1792]{2,1,0:T(8,128)(2,1)} %get-tuple-element.41.refs_0_), channel_id=1, source_target_pairs={{0,8},{4,12},{8,0},{12,4},{1,9},{5,13},{9,1},{13,5},{2,10},{6,14},... | collective-permute-start | bytes 2064392 | tf_op jit(solution)/shard_map/ppermute | solution.py:26
  110.8 26.7 %collective-permute-start.33 = (bf16[2,96,1792]{2,1,0:T(8,128)(2,1)}, bf16[2,96,1792]{2,1,0:T(8,128)(2,1)S(1)}, u32[]{:S(2)}, u32[]{:S(2)}) collective-permute-start(bf16[2,96,1792]{2,1,0:T(8,128)(2,1)} %get-tuple-element.41.refs_0_), channel_id=1, source_target_pairs={{0,4},{4,0},{8,12},{12,8},{1,5},{5,1},{9,13},{13,9},{2,6},{6,2},{1... | collective-permute-start | bytes 2064392 | tf_op jit(solution)/shard_map/ppermute | solution.py:26
  112.3 19.2 %collective-permute-start.26 = (bf16[1,96,1792]{2,1,0:T(8,128)(2,1)}, bf16[1,96,1792]{2,1,0:T(8,128)(2,1)S(1)}, u32[]{:S(2)}, u32[]{:S(2)}) collective-permute-start(bf16[1,96,1792]{2,1,0:T(8,128)(2,1)} %get-tuple-element.38.refs_0_), channel_id=1, source_target_pairs={{0,8},{4,12},{8,0},{12,4},{1,9},{5,13},{9,1},{13,5},{2,10},{6,14},... | collective-permute-start | bytes 1032200 | tf_op jit(solution)/shard_map/ppermute | solution.py:26
  112.9 22.1 %collective-permute-start.25 = (bf16[1,96,1792]{2,1,0:T(8,128)(2,1)}, bf16[1,96,1792]{2,1,0:T(8,128)(2,1)}, u32[]{:S(2)}, u32[]{:S(2)}) collective-permute-start(bf16[1,96,1792]{2,1,0:T(8,128)(2,1)} %get-tuple-element.38.refs_0_), channel_id=1, source_target_pairs={{0,4},{4,0},{8,12},{12,8},{1,5},{5,1},{9,13},{13,9},{2,6},{6,2},{1... | collective-permute-start | bytes 1032200 | tf_op jit(solution)/shard_map/ppermute | solution.py:26
  149.5 31.7 %collective-permute-start.29 = (bf16[192,2048]{1,0:T(8,128)(2,1)S(1)}, bf16[192,2048]{1,0:T(8,128)(2,1)S(1)}, u32[]{:S(2)}, u32[]{:S(2)}) collective-permute-start(bf16[192,2048]{1,0:T(8,128)(2,1)S(1)} %get-tuple-element.40), channel_id=1, source_target_pairs={{0,16},{16,0},{1,17},{17,1},{2,18},{18,2},{3,19},{19,3},{4,20},{20... | collective-permute-start | bytes 2359304 | tf_op jit(solution)/shard_map/ppermute | solution.py:26
  160.9 25.6 %collective-permute-start.37 = (bf16[192,2048]{1,0:T(8,128)(2,1)S(1)}, bf16[192,2048]{1,0:T(8,128)(2,1)S(1)}, u32[]{:S(2)}, u32[]{:S(2)}) collective-permute-start(bf16[192,2048]{1,0:T(8,128)(2,1)S(1)} %get-tuple-element.43), channel_id=1, source_target_pairs={{0,16},{16,0},{1,17},{17,1},{2,18},{18,2},{3,19},{19,3},{4,20},{20... | collective-permute-start | bytes 2359304 | tf_op jit(solution)/shard_map/ppermute | solution.py:26
  184.1 15.5 %collective-permute-start.31 = (bf16[48,2048]{1,0:T(8,128)(2,1)S(1)}, bf16[48,2048]{1,0:T(8,128)(2,1)S(1)}, u32[]{:S(2)}, u32[]{:S(2)}) collective-permute-start(bf16[48,2048]{1,0:T(8,128)(2,1)S(1)} %get-tuple-element.58), channel_id=1, source_target_pairs={{0,2},{1,3},{2,0},{3,1},{4,6},{5,7},{6,4},{7,5},{8,10},{9,11},{10,... | collective-permute-start | bytes 589832 | tf_op jit(solution)/shard_map/ppermute | solution.py:30
  185.2 14.3 %collective-permute-start.30 = (bf16[48,2048]{1,0:T(8,128)(2,1)S(1)}, bf16[48,2048]{1,0:T(8,128)(2,1)S(1)}, u32[]{:S(2)}, u32[]{:S(2)}) collective-permute-start(bf16[48,2048]{1,0:T(8,128)(2,1)S(1)} %get-tuple-element.56), channel_id=1, source_target_pairs={{0,3},{1,0},{2,1},{3,2},{4,7},{5,4},{6,5},{7,6},{8,11},{9,8},{10,9... | collective-permute-start | bytes 589832 | tf_op jit(solution)/shard_map/ppermute | solution.py:30
  186.6 17.1 %collective-permute-start.40 = (bf16[48,2048]{1,0:T(8,128)(2,1)S(1)}, bf16[48,2048]{1,0:T(8,128)(2,1)S(1)}, u32[]{:S(2)}, u32[]{:S(2)}) collective-permute-start(bf16[48,2048]{1,0:T(8,128)(2,1)S(1)} %get-tuple-element.54), channel_id=1, source_target_pairs={{0,1},{1,2},{2,3},{3,0},{4,5},{5,6},{6,7},{7,4},{8,9},{9,10},{10,1... | collective-permute-start | bytes 589832 | tf_op jit(solution)/shard_map/ppermute | solution.py:30
  187.4 28.0 %collective-permute-start.39 = (bf16[48,2048]{1,0:T(8,128)(2,1)S(1)}, bf16[48,2048]{1,0:T(8,128)(2,1)S(1)}, u32[]{:S(2)}, u32[]{:S(2)}) collective-permute-start(bf16[48,2048]{1,0:T(8,128)(2,1)S(1)} %get-tuple-element.55), channel_id=1, source_target_pairs={{0,2},{1,3},{2,0},{3,1},{4,6},{5,7},{6,4},{7,5},{8,10},{9,11},{10,... | collective-permute-start | bytes 589832 | tf_op jit(solution)/shard_map/ppermute | solution.py:30
  191.1 24.4 %collective-permute-start.38 = (bf16[48,2048]{1,0:T(8,128)(2,1)S(1)}, bf16[48,2048]{1,0:T(8,128)(2,1)S(1)}, u32[]{:S(2)}, u32[]{:S(2)}) collective-permute-start(bf16[48,2048]{1,0:T(8,128)(2,1)S(1)} %get-tuple-element.53), channel_id=1, source_target_pairs={{0,3},{1,0},{2,1},{3,2},{4,7},{5,4},{6,5},{7,6},{8,11},{9,8},{10,9... | collective-permute-start | bytes 589832 | tf_op jit(solution)/shard_map/ppermute | solution.py:30
  (38 other events, 291.8 us)

commit v2 on v1

v2 whole, which is shorter than its diff:
```python
import functools
import jax
import jax.numpy as jnp
from jax import lax
from jax.experimental import pallas as pl
from jax.experimental.pallas import tpu as pltpu
from jax.sharding import PartitionSpec as P

BLOCK = 128
VMEM_BYTES = 10 * 1024 * 1024
BF16 = jnp.bfloat16
F32 = jnp.float32


def block_edge(extent):
    return 256 if extent % 256 == 0 else 128


def masked(weight, mask):
    groups, width = mask.shape
    shaped = weight.reshape(groups, BLOCK, width) * mask[:, None, :]
    return shaped.reshape(groups * BLOCK, width)


def swap(value, axis, size, step):
    return lax.ppermute(value, axis, [(i, i ^ step) for i in range(size)])


def kernel_params(steps=0):
    return pltpu.CompilerParams(
        dimension_semantics=("arbitrary",) * steps if steps else None, vmem_limit_bytes=VMEM_BYTES
    )


IN_VMEM = pl.BlockSpec(memory_space=pltpu.VMEM)
IN_SMEM = pl.BlockSpec(memory_space=pltpu.SMEM)


def place_rows(result, plan, outs, lead, columns):
    for ref, pieces in zip(outs, plan):
        at = 0
        for start, count in pieces:
            rows = result[start : start + count].astype(ref.dtype)
            if lead is None:
                ref[at : at + count, columns] = rows
            else:
                ref[lead, at : at + count, columns] = rows
            at += count


def plan_rows(pieces):
    return sum(count for _, count in pieces)


def project_kernel(ring, plan, by_unit, amount, place_ref, *refs):
    parts, refs = refs[: max(1, 2 * ring)], refs[max(1, 2 * ring) :]
    weights, masks, rows_ref, outs = refs[:amount], refs[amount : 2 * amount], refs[2 * amount], refs[2 * amount + 1 :]
    if not ring:
        rows_ref[...] = parts[0][...]
    else:
        place = place_ref[0]
        unit = parts[0].shape[0]
        for slot in range(ring):
            for source in range(ring):

                @pl.when((place ^ slot) == source)
                def _(slot=slot, source=source):
                    at = 2 * unit * slot
                    rows_ref[at : at + unit, :] = parts[source][...]
                    rows_ref[at + unit : at + 2 * unit, :] = parts[ring + source][...]

    rows = rows_ref[...]
    units = weights[0].shape[0] if by_unit else weights[0].shape[1]
    edge = block_edge(units)
    for lead, (weight, mask) in enumerate(zip(weights, masks)):
        for at in range(0, units, edge):
            columns = slice(at, at + edge)
            if by_unit:
                kept = masked(weight[columns, :], mask[at // BLOCK : (at + edge) // BLOCK, :])
                result = lax.dot_general(rows, kept, (((1,), (1,)), ((), ())), preferred_element_type=F32)
            else:
                kept = masked(weight[:, columns], mask[:, columns])
                result = jnp.dot(rows, kept, preferred_element_type=F32)
            place_rows(result, plan, outs, lead, columns)


def project(place, parts, weights, masks, plan, by_unit):
    ring = len(parts) // 2
    amount = len(weights)
    features = parts[0].shape[1]
    tokens = sum(part.shape[0] for part in parts)
    units = weights[0].shape[0] if by_unit else weights[0].shape[1]
    counts = [plan_rows(pieces) for pieces in plan]
    return pl.pallas_call(
        functools.partial(project_kernel, ring, plan, by_unit, amount),
        in_specs=[IN_SMEM] + [IN_VMEM] * (len(parts) + 2 * amount),
        out_specs=[IN_VMEM] * (1 + len(plan)),
        out_shape=[jax.ShapeDtypeStruct((tokens, features), BF16)]
        + [jax.ShapeDtypeStruct((amount, count, units), BF16) for count in counts],
        compiler_params=kernel_params(),
        cost_estimate=pl.CostEstimate(
            flops=2 * tokens * features * units * amount,
            bytes_accessed=2 * amount * features * units,
            transcendentals=0,
        ),
    )(place, *parts, *weights, *masks)


def contract_kernel(pieces, plan, by_unit, amount, *refs):
    parts, refs = refs[: len(pieces)], refs[len(pieces) :]
    weights, masks, rows_ref, outs = refs[:amount], refs[amount : 2 * amount], refs[2 * amount], refs[2 * amount + 1 :]
    at = 0
    for part, count in zip(parts, pieces):
        rows_ref[:, at : at + count, :] = part[...]
        at += count
    rows = [rows_ref[lead] for lead in range(amount)]
    features = weights[0].shape[1] if by_unit else weights[0].shape[0]
    edge = block_edge(features)
    for at in range(0, features, edge):
        columns = slice(at, at + edge)
        total = None
        for lead, (weight, mask) in enumerate(zip(weights, masks)):
            if by_unit:
                kept = masked(weight[:, columns], mask[:, columns])
                result = jnp.dot(rows[lead], kept, preferred_element_type=F32)
            else:
                kept = masked(weight[columns, :], mask[at // BLOCK : (at + edge) // BLOCK, :])
                result = lax.dot_general(rows[lead], kept, (((1,), (1,)), ((), ())), preferred_element_type=F32)
            total = result if total is None else total + result
        place_rows(total, plan, outs, None, columns)


def contract(parts, weights, masks, plan, types, by_unit):
    amount = len(weights)
    units = parts[0].shape[2]
    pieces = [part.shape[1] for part in parts]
    tokens = sum(pieces)
    features = weights[0].shape[1] if by_unit else weights[0].shape[0]
    counts = [plan_rows(piece) for piece in plan]
    return pl.pallas_call(
        functools.partial(contract_kernel, pieces, plan, by_unit, amount),
        in_specs=[IN_VMEM] * (len(parts) + 2 * amount),
        out_specs=[IN_VMEM] * (1 + len(plan)),
        out_shape=[jax.ShapeDtypeStruct((amount, tokens, units), BF16)]
        + [jax.ShapeDtypeStruct((count, features), kind) for count, kind in zip(counts, types)],
        compiler_params=kernel_params(),
        cost_estimate=pl.CostEstimate(
            flops=2 * tokens * features * units * amount,
            bytes_accessed=2 * amount * features * units,
            transcendentals=0,
        ),
    )(*parts, *weights, *masks)


def outer_kernel(left_ref, right_ref, *refs):
    amount = right_ref.shape[0]
    masks, outs = refs[:amount], refs[amount:]
    edge = outs[0].shape[0]
    left = left_ref[:, pl.ds(pl.multiple_of(pl.program_id(0) * edge, edge), edge)]
    for lead in range(amount):
        result = lax.dot_general(left, right_ref[lead], (((0,), (0,)), ((), ())), preferred_element_type=F32)
        outs[lead][...] = masked(result, masks[lead][0].astype(F32))


def outer(left, right, masks):
    tokens, rows = left.shape
    amount, _, width = right.shape
    edge = block_edge(rows)
    return pl.pallas_call(
        outer_kernel,
        grid=(rows // edge,),
        in_specs=[IN_VMEM, IN_VMEM] + [pl.BlockSpec((1, edge // BLOCK, width), lambda j: (j, 0, 0))] * amount,
        out_specs=[pl.BlockSpec((edge, width), lambda j: (j, 0))] * amount,
        out_shape=[jax.ShapeDtypeStruct((rows, width), F32)] * amount,
        compiler_params=kernel_params(1),
        cost_estimate=pl.CostEstimate(
            flops=2 * tokens * rows * width * amount,
            bytes_accessed=4 * amount * rows * width,
            transcendentals=0,
        ),
    )(left, right, *masks)


def owner_kernel(count, place_ref, own_ref, got_ref, *refs):
    factors, outs, sums = refs[:-count], refs[-count:], ()
    if factors:
        factors, outs, sums = refs[:count], refs[count : 2 * count], refs[2 * count :]
    unit = outs[0].shape[0]
    place = place_ref[0]
    down = None
    for step in range(count):
        rows = pl.ds(pl.multiple_of((place ^ step) * unit, 16), unit)
        part = own_ref[rows, :] + got_ref[rows, :].astype(F32)
        outs[step][...] = part.astype(outs[step].dtype)
        if factors:
            product = part * factors[step][...].astype(F32)
            across = jnp.sum(product, axis=1, keepdims=True)
            sums[0][step * unit : (step + 1) * unit, :] = jnp.broadcast_to(across, (unit, sums[0].shape[1]))
            step_down = jnp.sum(product, axis=0, keepdims=True)
            down = step_down if down is None else down + step_down
    if factors:
        sums[1][...] = down


def owner(place, own, got, count, factors=()):
    total, features = own.shape
    unit = total // count
    outs = [jax.ShapeDtypeStruct((unit, features), F32 if step == 0 else BF16) for step in range(count)]
    if factors:
        outs += [jax.ShapeDtypeStruct((total, 128), F32), jax.ShapeDtypeStruct((1, features), F32)]
    return pl.pallas_call(
        functools.partial(owner_kernel, count),
        in_specs=[IN_SMEM] + [IN_VMEM] * (2 + len(factors)),
        out_specs=[IN_VMEM] * len(outs),
        out_shape=outs,
        compiler_params=kernel_params(),
    )(place, own, got, *factors)


def activation(gate, up_value, hidden_grad):
    sigmoid_gate = 1.0 / (1.0 + jnp.exp(-gate))
    scaled = gate * sigmoid_gate
    hidden = scaled * up_value
    gate_grad = hidden_grad * up_value * sigmoid_gate * (1.0 + gate * (1.0 - sigmoid_gate))
    up_grad = hidden_grad * scaled
    return hidden, gate_grad, up_grad


def activate_kernel(*refs):
    pair, one, (hidden_ref, grads_ref) = refs[:5], refs[5:10], refs[10:]
    half = pair[3].shape[1]
    for second in (False, True):
        at = half if second else 0
        rows = slice(at, at + half)

        def summed(parts, lead):
            own, first_x, first_y, last_y, last_x = parts
            first, last = (first_y, last_x) if second else (first_x, last_y)
            return own[lead, rows].astype(F32) + first[lead, half:].astype(F32) + last[lead].astype(F32)

        results = activation(summed(pair, 0), summed(pair, 1), summed(one, 0))
        hidden_ref[0, rows] = results[0].astype(BF16)
        grads_ref[0, rows] = results[1].astype(BF16)
        grads_ref[1, rows] = results[2].astype(BF16)


def activate(pair, one):
    _, share, units = pair[0].shape
    edge = block_edge(units)
    spec = lambda array: pl.BlockSpec(array.shape[:2] + (edge,), lambda j: (0, 0, j))
    outs = [jax.ShapeDtypeStruct((amount, share, units), BF16) for amount in (1, 2)]
    return pl.pallas_call(
        activate_kernel,
        grid=(units // edge,),
        in_specs=[spec(array) for array in pair + one],
        out_specs=[spec(array) for array in outs],
        out_shape=outs,
        compiler_params=kernel_params(1),
    )(*pair, *one)


def widen(keep):
    return jnp.repeat(keep, BLOCK, axis=1).astype(BF16)


def widen_grouped(keep):
    together = block_edge(keep.shape[0] * BLOCK) // BLOCK
    return widen(keep).reshape(-1, together, keep.shape[1] * BLOCK)


def finish(token_f, inv_rms, norm_gain, normed_grad, inner_sum, gain_sum):
    grad_gain = gain_sum(jnp.sum(normed_grad * token_f * inv_rms, axis=0))
    inner_dot = inner_sum(jnp.sum(norm_gain * normed_grad * token_f, axis=1))
    width = norm_gain.shape[0] * lax.axis_size("row")
    grad_tokens = (
        inv_rms * norm_gain * normed_grad
        - token_f * inv_rms * inv_rms * inv_rms * inner_dot[:, None] / width
    )
    return grad_tokens, grad_gain


def ordered(*groups):
    return lax.optimization_barrier(groups)


def exchange_device(
    tokens, norm_gain, gate_weight, up_weight, down_weight, gate_keep, up_keep, down_keep, cotangent
):
    rows, cols = 4, 4
    unit, features = tokens.shape
    place = lax.axis_index("row")
    place_arg = place.astype(jnp.int32).reshape(1)

    def core_swap(value):
        return swap(value, "dp", 2, 1)

    def row_swap(value, step):
        return swap(value, "row", rows, step)

    def level_swaps(parts):
        return [swap(part, "col", cols, step + 1) for step, part in enumerate(parts)]

    def balanced(value, got):
        return (value + got[0]) + (got[1] + got[2])

    def row_sum(value):
        value = value + row_swap(value, 1)
        return value + row_swap(value, 2)

    def sum_first(x_first, y_first):
        return ordered(row_swap(x_first, 1), row_swap(y_first, 2))

    def sum_middle(x_keep, y_keep, got_x, got_y):
        half = x_keep.shape[1]
        add = lambda a, b: (a.astype(F32) + b[:, :half].astype(F32)).astype(BF16)
        return add(y_keep, got_x), add(x_keep, got_y)

    def sum_last(for_y, for_x):
        return ordered(row_swap(for_y, 2), row_swap(for_x, 1))

    def gather_first(share):
        return ordered(row_swap(share, 1), row_swap(share, 2))

    def gather_middle(got_x, got_y):
        return got_y[:, :unit], got_x[:, unit:]

    def gather_last(for_x, for_y):
        return ordered(row_swap(for_x, 1), row_swap(for_y, 2))

    def owner_total(kept, got):
        return balanced(kept, [part.astype(F32) for part in got])

    def rows_of(slot, second):
        return (2 * unit * slot + (unit if second else 0), unit)

    first_plan = [
        [rows_of(3, False), rows_of(1, False)],
        [rows_of(3, True), rows_of(2, True)],
        [rows_of(1, True)],
        [rows_of(2, False)],
        [(0, 2 * unit)],
    ]
    last_plan = [[rows_of(slot, False) for slot in range(rows)], [rows_of(slot, True) for slot in range(rows)]]

    token_f = tokens.astype(F32)
    squares = jnp.sum(token_f * token_f, axis=1)
    cot_far = level_swaps([cotangent] * 3)
    inv_rms = lax.rsqrt(row_sum(squares)[:, None] / (features * rows) + 1e-05)
    normed = (token_f * inv_rms * norm_gain).astype(BF16)
    gate_mask, up_mask, down_mask = widen(gate_keep), widen(up_keep), widen(down_keep)
    gate_groups, up_groups, down_groups = widen_grouped(gate_keep), widen_grouped(up_keep), widen_grouped(down_keep)
    normed_core = core_swap(normed)
    masks = [gate_mask, up_mask, down_mask, gate_groups, up_groups, down_groups]
    cot_far, normed, normed_core, place, place_arg, masks = ordered(
        cot_far, normed, normed_core, place, place_arg, masks
    )
    gate_mask, up_mask, down_mask, gate_groups, up_groups, down_groups = masks
    cot_own = [cotangent, *cot_far]
    cot_other = [core_swap(part) for part in cot_own]

    normed_far = level_swaps([normed] * 3)
    seen_cot, *one_parts = project(place_arg, cot_own + cot_other, [down_weight], [down_mask], first_plan, True)
    one_x, one_y = sum_first(*one_parts[:2])
    one_keep = one_parts[2:]
    normed_far, one_x, one_y = ordered(normed_far, one_x, one_y)
    normed_own = [normed, *normed_far]
    normed_other = [normed_core] + [core_swap(part) for part in normed_far]
    one_late = sum_middle(*one_keep[:2], one_x, one_y)
    normed_other, one_late = ordered(normed_other, one_late)

    one_last = sum_last(*one_late)
    seen_rows, *pair_parts = project(place_arg, normed_own + normed_other, [gate_weight, up_weight], [gate_mask, up_mask], first_plan, False)
    one_last, pair_parts = ordered(one_last, pair_parts)
    pair_x, pair_y = sum_first(*pair_parts[:2])
    pair_last = sum_last(*sum_middle(*pair_parts[2:4], pair_x, pair_y))
    hidden_share, grads_share = activate(
        [pair_parts[4], pair_x, pair_y, *pair_last], [one_keep[2], one_x, one_y, *one_last]
    )

    hidden_x, hidden_y = gather_first(hidden_share)
    hidden_middle = gather_middle(hidden_x, hidden_y)
    grads_share, hidden_middle = ordered(grads_share, hidden_middle)
    grads_x, grads_y = gather_first(grads_share)
    hidden_last = gather_last(*hidden_middle)
    hidden, branch_own, branch_other = contract(
        [hidden_share, hidden_x, hidden_y, *hidden_last], [down_weight], [down_mask], last_plan, (F32, BF16), True
    )
    grads_x, grads_y, branch_own, branch_other = ordered(grads_x, grads_y, branch_own, branch_other)
    branch_got = core_swap(branch_other)
    grads_middle = gather_middle(grads_x, grads_y)
    grads_last = gather_last(*grads_middle)
    branch_kept, *branch_parts = owner(place_arg, branch_own, branch_got, cols)
    hidden, branch_parts = ordered(hidden, branch_parts)
    branch_far = level_swaps(branch_parts)
    (grad_down,) = outer(hidden[0], seen_cot[None], [down_groups])
    grads_last, grad_down = ordered(grads_last, grad_down)

    grads, normed_mine, normed_theirs = contract(
        [grads_share, grads_x, grads_y, *grads_last], [gate_weight, up_weight], [gate_mask, up_mask], last_plan, (F32, BF16), False
    )
    branch_far, normed_mine, normed_theirs = ordered(branch_far, normed_mine, normed_theirs)
    kept, *parts, across, down_sum = owner(place_arg, normed_mine, core_swap(normed_theirs), cols, normed_own)
    grads, parts, across, down_sum = ordered(grads, parts, across, down_sum)
    far = level_swaps(parts)
    across_x = across + row_swap(across, 1)
    down_both = down_sum + core_swap(down_sum)
    across_x, down_both, grads = ordered(across_x, down_both, grads)
    across_row = across_x + row_swap(across_x, 2)
    grad_gate, grad_up = outer(seen_rows, grads, [gate_groups, up_groups])
    far, across_row, down_both, grad_gate, grad_up = ordered(far, across_row, down_both, grad_gate, grad_up)
    sums = [
        jnp.concatenate([across_row[step * unit : (step + 1) * unit], down_both.reshape(-1, 128)])
        for step in range(cols)
    ]
    sums_total = balanced(sums[0], level_swaps(sums[1:]))
    branch = owner_total(branch_kept, branch_far).astype(BF16)
    normed_grad = owner_total(kept, far)
    grad_gain = sums_total[unit:].reshape(features) / norm_gain
    grad_tokens = (
        inv_rms * norm_gain * normed_grad - token_f * inv_rms * inv_rms * sums_total[:unit, :1] / (features * rows)
    )
    return (branch, grad_tokens, grad_gain, grad_gate, grad_up, grad_down)


def general_device(
    tokens, norm_gain, gate_weight, up_weight, down_weight, gate_keep, up_keep, down_keep, cotangent
):
    owners = ("dp", "col")
    features = tokens.shape[1]
    place_arg = jnp.zeros((1,), jnp.int32)
    token_f = tokens.astype(F32)
    square = lax.psum(jnp.sum(token_f * token_f, axis=1), "row")
    inv_rms = lax.rsqrt(square[:, None] / (features * lax.axis_size("row")) + 1e-05)
    normed = (token_f * inv_rms * norm_gain).astype(BF16)
    gate_mask, up_mask, down_mask = widen(gate_keep), widen(up_keep), widen(down_keep)
    gate_groups, up_groups, down_groups = widen_grouped(gate_keep), widen_grouped(up_keep), widen_grouped(down_keep)
    seen_cot = lax.all_gather(cotangent, owners, axis=0, tiled=True)
    seen_rows = lax.all_gather(normed, owners, axis=0, tiled=True)
    plan = [[(0, seen_cot.shape[0])]]

    def share(value):
        return lax.psum_scatter(value.astype(F32), "row", scatter_dimension=1, tiled=True)

    def collect(value):
        return lax.all_gather(value.astype(BF16), "row", axis=1, tiled=True)

    def owner_sum(value):
        return lax.psum_scatter(value, owners, scatter_dimension=0, tiled=True)

    _, one = project(place_arg, [seen_cot], [down_weight], [down_mask], plan, True)
    _, pair = project(place_arg, [seen_rows], [gate_weight, up_weight], [gate_mask, up_mask], plan, False)
    pair = share(pair)
    hidden, gate_grad, up_grad = activation(pair[0], pair[1], share(one)[0])
    hidden, branch = contract([collect(hidden[None])], [down_weight], [down_mask], plan, (F32,), True)
    branch = owner_sum(branch).astype(BF16)
    grads, normed_grad = contract(
        [collect(jnp.stack([gate_grad, up_grad]))], [gate_weight, up_weight], [gate_mask, up_mask], plan, (F32,), False
    )
    normed_grad = owner_sum(normed_grad)
    (grad_down,) = outer(hidden[0], seen_cot[None], [down_groups])
    grad_gate, grad_up = outer(seen_rows, grads, [gate_groups, up_groups])
    grad_tokens, grad_gain = finish(
        token_f,
        inv_rms,
        norm_gain,
        normed_grad,
        lambda value: lax.psum(value, "row"),
        lambda value: lax.psum(value, owners),
    )
    return (branch, grad_tokens, grad_gain, grad_gate, grad_up, grad_down)


def solution(mesh):
    split = P(("dp", "col"), "row")
    turned = P("row", ("dp", "col"))
    sizes = (mesh.shape["dp"], mesh.shape["row"], mesh.shape["col"])
    on_device = exchange_device if sizes == (2, 4, 4) else general_device
    return jax.shard_map(
        on_device,
        mesh=mesh,
        in_specs=(split, P("row"), turned, turned, split, turned, turned, split, split),
        out_specs=(split, split, P("row"), turned, turned, split),
        check_vma=False,
    )
```

time: 236 us -> 192 us (0.81)
  starting transfers between devices: 72.5 us -> 48.3 us
  Pallas kernels: 60.9 us -> 39.9 us
  waiting for transfers between devices: 85.1 us -> 87.8 us
    ppermute x15 -> x0, starting transfers between devices: 44 us -> none  [shift(): lax.ppermute(value, axis, [(i, (i + step) % size) for i in range(size)])]
    ppermute x33 -> x46, waiting for transfers between devices: 53.7 us -> 87.8 us  [swap(): return lax.ppermute(value, axis, [(i, i ^ step) for i in range(size)])]
    ppermute x15 -> x0, waiting for transfers between devices: 31.4 us -> none  [shift(): lax.ppermute(value, axis, [(i, (i + step) % size) for i in range(size)])]
    ppermute x33 -> x46, starting transfers between devices: 28.5 us -> 48.3 us  [swap(): return lax.ppermute(value, axis, [(i, i ^ step) for i in range(size)])]
    pallas_call x2, Pallas kernels: 19.4 us -> 9 us  [contract(): pl.pallas_call(functools.partial(contract_kernel, pieces, plan, by_unit,...]
    pallas_call x2, Pallas kernels: 18.6 us -> 9.39 us  [project(): pl.pallas_call(functools.partial(project_kernel, ring, plan, by_unit, amo...]
    unnamed x30 -> x18, local copies, waits for them, and re-layouts: 6.15 us -> 7.15 us
    pallas_call x2 -> x4, Pallas kernels: 19.7 us -> 20.2 us  [the longest x2 19.6 us: outer(): pl.pallas_call(outer_kernel, grid=(rows // edge,), in_specs=[IN_VMEM, IN_...]
  transfers between devices with their start and end apart: 48 -> 46, of which waited for: 18 -> 25; matrix products, arithmetic and copies ran while one was open for 3% -> 2% of each run, Pallas kernels for 25% -> 18%
where the time goes in v2:
time: 192 us
  waiting for transfers between devices  87.8 us (46%)
  starting transfers between devices  48.3 us (25%)
  Pallas kernels  39.9 us (21%)
  local copies, waits for them, and re-layouts  7.72 us (4%)
  other arithmetic  6.89 us (4%)
    ppermute x46, waiting for transfers between devices, swap(): return lax.ppermute(value, axis, [(i, i ^ step) for i in range(size)])  87.8 us
    ppermute x46, starting transfers between devices, swap(): return lax.ppermute(value, axis, [(i, i ^ step) for i in range(size)])  48.3 us
    pallas_call x2, Pallas kernels, outer(): pl.pallas_call(outer_kernel, grid=(rows // edge,), in_specs=[IN_VMEM, IN_...  19.6 us
    pallas_call x2, Pallas kernels, project(): pl.pallas_call(functools.partial(project_kernel, ring, plan, by_unit, amo...  9.39 us
    pallas_call x2, Pallas kernels, contract(): pl.pallas_call(functools.partial(contract_kernel, pieces, plan, by_unit,...  9 us
    unnamed x18, local copies, waits for them, and re-layouts  7.15 us
  transfers between devices with their start and end apart: 46, of which 25 were waited for; matrix products, arithmetic and copies ran while one was open for 2% of the time, Pallas kernels for 18%

profile of v2, /device:TPU:0, one launch (start us, length us, event | category | flops | bytes accessed | tf_op | source)
XLA Modules:
  0.0 191.6 jit_solution(5313698092452622664)
XLA Ops:
  1.7 3.0 %collective-permute-start.3 = (f32[48]{0:T(128)S(1)}, f32[48]{0:T(128)S(1)}, u32[]{:S(2)}, u32[]{:S(2)}) collective-permute-start(f32[48]{0:T(128)S(1)} %fusion.6), channel_id=1, source_target_pairs={{0,4},{4,0},{8,12},{12,8},{1,5},{5,1},{9,13},{13,9},{2,6},{6,2},{1... | collective-permute-start | bytes 584 | tf_op jit(solution)/shard_map/ppermute | solution.py:26
  4.7 3.6 %collective-permute-start.2 = (bf16[48,2048]{1,0:T(8,128)(2,1)}, bf16[48,2048]{1,0:T(8,128)(2,1)S(1)}, u32[]{:S(2)}, u32[]{:S(2)}) collective-permute-start(bf16[48,2048]{1,0:T(8,128)(2,1)} %refs_0_.1), channel_id=1, source_target_pairs={{0,3},{1,2},{2,1},{3,0},{4,7},{5,6},{6,5},{7,4},{8,11},{9,10},{10,... | collective-permute-start | bytes 589832 | tf_op jit(solution)/shard_map/ppermute | solution.py:26
  15.0 9.9 %collective-permute-done.1.refs_2_ = bf16[48,2048]{1,0:T(8,128)(2,1)S(1)} collective-permute-done((bf16[48,2048]{1,0:T(8,128)(2,1)}, bf16[48,2048]{1,0:T(8,128)(2,1)S(1)}, u32[]{:S(2)}, u32[]{:S(2)}) %collective-permute-start.1) | collective-permute-done | bytes 196640 | tf_op jit(solution)/shard_map/ppermute | solution.py:26
  26.9 3.1 %copy-done = bf16[1792,2048]{1,0:T(8,128)(2,1)S(1)} copy-done((bf16[1792,2048]{1,0:T(8,128)(2,1)S(1)}, bf16[1792,2048]{1,0:T(8,128)(2,1)}, u32[]{:S(2)}) %copy-start) | copy-done | bytes 7340056
  31.0 3.3 %shard_map.136 = (bf16[384,2048]{1,0:T(8,128)(2,1)S(1)}, bf16[1,96,1792]{2,1,0:T(8,128)(2,1)S(1)}, bf16[1,96,1792]{2,1,0:T(8,128)(2,1)S(1)}, bf16[1,48,1792]{2,1...) custom-call(s32[1]{0:T(128)} %bitcast.place_ref, ...), custom_call_target="tpu_custom_call" | custom-call | flops 2818572288 | bytes 7340032 | tf_op jit(solution)/shard_map/pallas_call | solution.py:94
  36.3 2.5 %collective-permute-start.8 = (bf16[48,2048]{1,0:T(8,128)(2,1)S(1)}, bf16[48,2048]{1,0:T(8,128)(2,1)S(1)}, u32[]{:S(2)}, u32[]{:S(2)}) collective-permute-start(bf16[48,2048]{1,0:T(8,128)(2,1)S(1)} %fusion.2.refs_0_), channel_id=1, source_target_pairs={{0,3},{1,2},{2,1},{3,0},{4,7},{5,6},{6,5},{7,4},{8,11},{9,10},{10,... | collective-permute-start | bytes 589832 | tf_op jit(solution)/shard_map/ppermute | solution.py:26
  40.7 3.8 %collective-permute-done.13.refs_6_ = bf16[1,96,1792]{2,1,0:T(8,128)(2,1)S(1)} collective-permute-done((bf16[1,96,1792]{2,1,0:T(8,128)(2,1)S(1)}, bf16[1,96,1792]{2,1,0:T(8,128)(2,1)S(1)}, u32[]{:S(2)}, u32[]{:S(2)}) %collective-permute-start.13) | collective-permute-done | bytes 344096 | tf_op jit(solution)/shard_map/ppermute | solution.py:26
  46.0 8.6 %collective-permute-done.7.refs_2_ = bf16[48,2048]{1,0:T(8,128)(2,1)S(1)} collective-permute-done((bf16[48,2048]{1,0:T(8,128)(2,1)S(1)}, bf16[48,2048]{1,0:T(8,128)(2,1)S(1)}, u32[]{:S(2)}, u32[]{:S(2)}) %collective-permute-start.7) | collective-permute-done | bytes 196640 | tf_op jit(solution)/shard_map/ppermute | solution.py:26
  58.7 3.1 %copy-done.2 = bf16[2048,1792]{1,0:T(8,128)(2,1)S(1)} copy-done((bf16[2048,1792]{1,0:T(8,128)(2,1)S(1)}, bf16[2048,1792]{1,0:T(8,128)(2,1)}, u32[]{:S(2)}) %copy-start.2) | copy-done | bytes 7340056
  61.8 6.1 %shard_map.137 = (bf16[384,2048]{1,0:T(8,128)(2,1)S(1)}, bf16[2,96,1792]{2,1,0:T(8,128)(2,1)S(1)}, bf16[2,96,1792]{2,1,0:T(8,128)(2,1)S(1)}, bf16[2,48,1792]{2,1...) custom-call(s32[1]{0:T(128)} %bitcast.place_ref, ...), custom_call_target="tpu_custom_call" | custom-call | flops 5637144576 | bytes 14680064 | tf_op jit(solution)/shard_map/pallas_call | solution.py:94
  70.0 15.0 %collective-permute-done.20.refs_1_ = bf16[2,96,1792]{2,1,0:T(8,128)(2,1)S(1)} collective-permute-done((bf16[2,96,1792]{2,1,0:T(8,128)(2,1)S(1)}, bf16[2,96,1792]{2,1,0:T(8,128)(2,1)S(1)}, u32[]{:S(2)}, u32[]{:S(2)}) %collective-permute-start.20) | collective-permute-done | bytes 688160 | tf_op jit(solution)/shard_map/ppermute | solution.py:26
  88.5 6.3 %collective-permute-done.23.refs_4_ = bf16[2,48,1792]{2,1,0:T(8,128)(2,1)S(1)} collective-permute-done((bf16[2,48,1792]{2,1,0:T(8,128)(2,1)S(1)}, bf16[2,48,1792]{2,1,0:T(8,128)(2,1)S(1)}, u32[]{:S(2)}, u32[]{:S(2)}) %collective-permute-start.23) | collective-permute-done | bytes 344096 | tf_op jit(solution)/shard_map/ppermute | solution.py:26
  98.7 5.8 %collective-permute-done.25.refs_2_ = bf16[1,96,1792]{2,1,0:T(8,128)(2,1)S(1)} collective-permute-done((bf16[1,96,1792]{2,1,0:T(8,128)(2,1)S(1)}, bf16[1,96,1792]{2,1,0:T(8,128)(2,1)S(1)}, u32[]{:S(2)}, u32[]{:S(2)}) %collective-permute-start.25) | collective-permute-done | bytes 344096 | tf_op jit(solution)/shard_map/ppermute | solution.py:26
  109.8 14.0 %collective-permute-done.28.refs_3_ = bf16[1,48,1792]{2,1,0:T(8,128)(2,1)S(1)} collective-permute-done((bf16[1,48,1792]{2,1,0:T(8,128)(2,1)S(1)}, bf16[1,48,1792]{2,1,0:T(8,128)(2,1)S(1)}, u32[]{:S(2)}, u32[]{:S(2)}) %collective-permute-start.28) | collective-permute-done | bytes 172064 | tf_op jit(solution)/shard_map/ppermute | solution.py:26
  123.8 3.0 %shard_map.139 = (bf16[1,384,1792]{2,1,0:T(8,128)(2,1)S(1)}, f32[192,2048]{1,0:T(8,128)S(1)}, bf16[192,2048]{1,0:T(8,128)(2,1)S(1)}) custom-call(bf16[1,96,1792]{2,1,0:T(8,128)(2,1)S(1)} %get-tuple-element.165.refs_0_, bf16[1,96,1792]{2,1,0:T(8,128)(2,1)S(1)} %collective-permute-done.24.refs_1_, bf16[1,96,1792]{2,1,0:T(8,128)(2,1)S(1)} %collective-permute-done.25.refs_2_, ...), custom_call_target="tpu_custom_call" | custom-call | flops 2818572288 | bytes 7340032 | tf_op jit(solution)/shard_map/pallas_call | solution.py:140
  129.4 8.1 %collective-permute-done.34.refs_3_ = bf16[2,48,1792]{2,1,0:T(8,128)(2,1)S(1)} collective-permute-done((bf16[2,48,1792]{2,1,0:T(8,128)(2,1)S(1)}, bf16[2,48,1792]{2,1,0:T(8,128)(2,1)S(1)}, u32[]{:S(2)}, u32[]{:S(2)}) %collective-permute-start.34) | collective-permute-done | bytes 344096 | tf_op jit(solution)/shard_map/ppermute | solution.py:26
  140.8 2.5 %collective-permute-start.33 = (bf16[48,2048]{1,0:T(8,128)(2,1)S(1)}, bf16[48,2048]{1,0:T(8,128)(2,1)S(1)}, u32[]{:S(2)}, u32[]{:S(2)}) collective-permute-start(bf16[48,2048]{1,0:T(8,128)(2,1)S(1)} %get-tuple-element.186), channel_id=1, source_target_pairs={{0,3},{1,2},{2,1},{3,0},{4,7},{5,6},{6,5},{7,4},{8,11},{9,10},{10,... | collective-permute-start | bytes 589832 | tf_op jit(solution)/shard_map/ppermute | solution.py:26
  143.3 8.2 %shard_map.141 = f32[1792,2048]{1,0:T(8,128)} custom-call(bf16[384,1792]{1,0:T(8,128)(2,1)S(1)} %bitcast.18, bf16[1,384,2048]{2,1,0:T(8,128)(2,1)S(1)} %bitcast.17, bf16[7,2,2048]{2,1,0:T(2,128)(2,1)S(1)} %convert_element_type.112.refs_0_), custom_call_target="tpu_custom_call" | custom-call | flops 2818572288 | bytes 14680064 | tf_op jit(solution)/shard_map/pallas_call | solution.py:169
  151.5 6.0 %shard_map.142 = (bf16[2,384,1792]{2,1,0:T(8,128)(2,1)S(1)}, f32[192,2048]{1,0:T(8,128)S(1)}, bf16[192,2048]{1,0:T(8,128)(2,1)S(1)}) custom-call(bf16[2,96,1792]{2,1,0:T(8,128)(2,1)S(1)} %get-tuple-element.168.refs_0_, bf16[2,96,1792]{2,1,0:T(8,128)(2,1)S(1)} %collective-permute-done.26.refs_1_, bf16[2,96,1792]{2,1,0:T(8,128)(2,1)S(1)} %collective-permute-done.27.refs_2_, ...), custom_call_target="tpu_custom_call" | custom-call | flops 5637144576 | bytes 14680064 | tf_op jit(solution)/shard_map/pallas_call | solution.py:140
  157.6 2.3 %collective-permute-done.36.got_ref = bf16[192,2048]{1,0:T(8,128)(2,1)S(1)} collective-permute-done((bf16[192,2048]{1,0:T(8,128)(2,1)S(1)}, bf16[192,2048]{1,0:T(8,128)(2,1)S(1)}, u32[]{:S(2)}, u32[]{:S(2)}) %collective-permute-start.36) | collective-permute-done | bytes 786464 | tf_op jit(solution)/shard_map/ppermute | solution.py:26
  162.9 2.5 %collective-permute-start.39 = (bf16[48,2048]{1,0:T(8,128)(2,1)S(1)}, bf16[48,2048]{1,0:T(8,128)(2,1)S(1)}, u32[]{:S(2)}, u32[]{:S(2)}) collective-permute-start(bf16[48,2048]{1,0:T(8,128)(2,1)S(1)} %get-tuple-element.212), channel_id=1, source_target_pairs={{0,3},{1,2},{2,1},{3,0},{4,7},{5,6},{6,5},{7,4},{8,11},{9,10},{10,... | collective-permute-start | bytes 589832 | tf_op jit(solution)/shard_map/ppermute | solution.py:26
  166.3 11.4 %shard_map.144 = (f32[2048,1792]{1,0:T(8,128)}, f32[2048,1792]{1,0:T(8,128)}) custom-call(bf16[384,2048]{1,0:T(8,128)(2,1)S(1)} %get-tuple-element.218.left_ref, bf16[2,384,1792]{2,1,0:T(8,128)(2,1)S(1)} %get-tuple-element.219.right_ref, bf16[8,2,1792]{2,1,0:T(2,128)(2,1)S(1)} %convert_element_type.110.refs_0_, ...), custom_call_target="tpu_custom_call" | custom-call | flops 5637144576 | bytes 29360128 | tf_op jit(solution)/shard_map/pallas_call | solution.py:169
  181.4 3.5 %collective-permute-start.43 = (f32[64,128]{1,0:T(8,128)S(1)}, f32[64,128]{1,0:T(8,128)S(1)}, u32[]{:S(2)}, u32[]{:S(2)}) collective-permute-start(f32[64,128]{1,0:T(8,128)S(1)} %get-tuple-element.237), channel_id=1, source_target_pairs={{0,1},{1,0},{2,3},{3,2},{4,5},{5,4},{6,7},{7,6},{8,9},{9,8},{10,11... | collective-permute-start | bytes 98312 | tf_op jit(solution)/shard_map/ppermute | solution.py:26
  186.8 3.1 %collective-permute-done.44 = f32[64,128]{1,0:T(8,128)S(1)} collective-permute-done((f32[64,128]{1,0:T(8,128)S(1)}, f32[64,128]{1,0:T(8,128)S(1)}, u32[]{:S(2)}, u32[]{:S(2)}) %collective-permute-start.44) | collective-permute-done | bytes 32800 | tf_op jit(solution)/shard_map/ppermute | solution.py:26
  (128 shorter events, 52.1 us)
Async XLA Ops:
  4.7 10.3 %collective-permute-start.2 = (bf16[48,2048]{1,0:T(8,128)(2,1)}, bf16[48,2048]{1,0:T(8,128)(2,1)S(1)}, u32[]{:S(2)}, u32[]{:S(2)}) collective-permute-start(bf16[48,2048]{1,0:T(8,128)(2,1)} %refs_0_.1), channel_id=1, source_target_pairs={{0,3},{1,2},{2,1},{3,0},{4,7},{5,6},{6,5},{7,4},{8,11},{9,10},{10,... | collective-permute-start | bytes 589832 | tf_op jit(solution)/shard_map/ppermute | solution.py:26
  8.3 16.6 %collective-permute-start.1 = (bf16[48,2048]{1,0:T(8,128)(2,1)}, bf16[48,2048]{1,0:T(8,128)(2,1)S(1)}, u32[]{:S(2)}, u32[]{:S(2)}) collective-permute-start(bf16[48,2048]{1,0:T(8,128)(2,1)} %refs_0_.1), channel_id=1, source_target_pairs={{0,2},{1,3},{2,0},{3,1},{4,6},{5,7},{6,4},{7,5},{8,10},{9,11},{10,... | collective-permute-start | bytes 589832 | tf_op jit(solution)/shard_map/ppermute | solution.py:26
  8.3 16.6 %collective-permute-start = (bf16[48,2048]{1,0:T(8,128)(2,1)}, bf16[48,2048]{1,0:T(8,128)(2,1)S(1)}, u32[]{:S(2)}, u32[]{:S(2)}) collective-permute-start(bf16[48,2048]{1,0:T(8,128)(2,1)} %refs_0_.1), channel_id=1, source_target_pairs={{0,1},{1,0},{2,3},{3,2},{4,5},{5,4},{6,7},{7,6},{8,9},{9,8},{10,11... | collective-permute-start | bytes 589832 | tf_op jit(solution)/shard_map/ppermute | solution.py:26
  9.1 16.4 %collective-permute-start.9 = (bf16[48,2048]{1,0:T(8,128)(2,1)}, bf16[48,2048]{1,0:T(8,128)(2,1)S(1)}, u32[]{:S(2)}, u32[]{:S(2)}) collective-permute-start(bf16[48,2048]{1,0:T(8,128)(2,1)} %refs_0_.1), channel_id=1, source_target_pairs={{0,16},{16,0},{1,17},{17,1},{2,18},{18,2},{3,19},{19,3},{4,20},{20... | collective-permute-start | bytes 589832 | tf_op jit(solution)/shard_map/ppermute | solution.py:26
  13.8 11.2 %collective-permute-start.5 = (bf16[48,2048]{1,0:T(8,128)(2,1)S(1)}, bf16[48,2048]{1,0:T(8,128)(2,1)S(1)}, u32[]{:S(2)}, u32[]{:S(2)}) collective-permute-start(bf16[48,2048]{1,0:T(8,128)(2,1)S(1)} %fusion.2.refs_0_), channel_id=1, source_target_pairs={{0,16},{16,0},{1,17},{17,1},{2,18},{18,2},{3,19},{19,3},{4,20},{20... | collective-permute-start | bytes 589832 | tf_op jit(solution)/shard_map/ppermute | solution.py:26
  38.8 15.8 %collective-permute-start.7 = (bf16[48,2048]{1,0:T(8,128)(2,1)S(1)}, bf16[48,2048]{1,0:T(8,128)(2,1)S(1)}, u32[]{:S(2)}, u32[]{:S(2)}) collective-permute-start(bf16[48,2048]{1,0:T(8,128)(2,1)S(1)} %fusion.2.refs_0_), channel_id=1, source_target_pairs={{0,2},{1,3},{2,0},{3,1},{4,6},{5,7},{6,4},{7,5},{8,10},{9,11},{10,... | collective-permute-start | bytes 589832 | tf_op jit(solution)/shard_map/ppermute | solution.py:26
  38.8 15.8 %collective-permute-start.6 = (bf16[48,2048]{1,0:T(8,128)(2,1)S(1)}, bf16[48,2048]{1,0:T(8,128)(2,1)S(1)}, u32[]{:S(2)}, u32[]{:S(2)}) collective-permute-start(bf16[48,2048]{1,0:T(8,128)(2,1)S(1)} %fusion.2.refs_0_), channel_id=1, source_target_pairs={{0,1},{1,0},{2,3},{3,2},{4,5},{5,4},{6,7},{7,6},{8,9},{9,8},{10,11... | collective-permute-start | bytes 589832 | tf_op jit(solution)/shard_map/ppermute | solution.py:26
  56.7 11.2 %collective-permute-start.18 = (bf16[1,48,1792]{2,1,0:T(8,128)(2,1)S(1)}, bf16[1,48,1792]{2,1,0:T(8,128)(2,1)S(1)}, u32[]{:S(2)}, u32[]{:S(2)}) collective-permute-start(bf16[1,48,1792]{2,1,0:T(8,128)(2,1)S(1)} %add_convert_fusion.4), channel_id=1, source_target_pairs={{0,8},{4,12},{8,0},{12,4},{1,9},{5,13},{9,1},{13,5},{2,10},{6,14},... | collective-permute-start | bytes 516104 | tf_op jit(solution)/shard_map/ppermute | solution.py:26
  57.2 10.7 %collective-permute-start.19 = (bf16[1,48,1792]{2,1,0:T(8,128)(2,1)S(1)}, bf16[1,48,1792]{2,1,0:T(8,128)(2,1)S(1)}, u32[]{:S(2)}, u32[]{:S(2)}) collective-permute-start(bf16[1,48,1792]{2,1,0:T(8,128)(2,1)S(1)} %add_convert_fusion.3), channel_id=1, source_target_pairs={{0,4},{4,0},{8,12},{12,8},{1,5},{5,1},{9,13},{13,9},{2,6},{6,2},{1... | collective-permute-start | bytes 516104 | tf_op jit(solution)/shard_map/ppermute | solution.py:26
  67.9 17.1 %collective-permute-start.20 = (bf16[2,96,1792]{2,1,0:T(8,128)(2,1)S(1)}, bf16[2,96,1792]{2,1,0:T(8,128)(2,1)S(1)}, u32[]{:S(2)}, u32[]{:S(2)}) collective-permute-start(bf16[2,96,1792]{2,1,0:T(8,128)(2,1)S(1)} %get-tuple-element.153), channel_id=1, source_target_pairs={{0,4},{4,0},{8,12},{12,8},{1,5},{5,1},{9,13},{13,9},{2,6},{6,2},{1... | collective-permute-start | bytes 2064392 | tf_op jit(solution)/shard_map/ppermute | solution.py:26
  68.5 17.2 %collective-permute-start.21 = (bf16[2,96,1792]{2,1,0:T(8,128)(2,1)S(1)}, bf16[2,96,1792]{2,1,0:T(8,128)(2,1)S(1)}, u32[]{:S(2)}, u32[]{:S(2)}) collective-permute-start(bf16[2,96,1792]{2,1,0:T(8,128)(2,1)S(1)} %get-tuple-element.154), channel_id=1, source_target_pairs={{0,8},{4,12},{8,0},{12,4},{1,9},{5,13},{9,1},{13,5},{2,10},{6,14},... | collective-permute-start | bytes 2064392 | tf_op jit(solution)/shard_map/ppermute | solution.py:26
  105.7 21.2 %collective-permute-start.27 = (bf16[2,96,1792]{2,1,0:T(8,128)(2,1)S(1)}, bf16[2,96,1792]{2,1,0:T(8,128)(2,1)S(1)}, u32[]{:S(2)}, u32[]{:S(2)}) collective-permute-start(bf16[2,96,1792]{2,1,0:T(8,128)(2,1)S(1)} %get-tuple-element.168.refs_0_), channel_id=1, source_target_pairs={{0,8},{4,12},{8,0},{12,4},{1,9},{5,13},{9,1},{13,5},{2,10},{6,14},... | collective-permute-start | bytes 2064392 | tf_op jit(solution)/shard_map/ppermute | solution.py:26
  106.3 20.6 %collective-permute-start.26 = (bf16[2,96,1792]{2,1,0:T(8,128)(2,1)S(1)}, bf16[2,96,1792]{2,1,0:T(8,128)(2,1)S(1)}, u32[]{:S(2)}, u32[]{:S(2)}) collective-permute-start(bf16[2,96,1792]{2,1,0:T(8,128)(2,1)S(1)} %get-tuple-element.168.refs_0_), channel_id=1, source_target_pairs={{0,4},{4,0},{8,12},{12,8},{1,5},{5,1},{9,13},{13,9},{2,6},{6,2},{1... | collective-permute-start | bytes 2064392 | tf_op jit(solution)/shard_map/ppermute | solution.py:26
  108.1 15.6 %collective-permute-start.28 = (bf16[1,48,1792]{2,1,0:T(8,128)(2,1)S(1)}, bf16[1,48,1792]{2,1,0:T(8,128)(2,1)S(1)}, u32[]{:S(2)}, u32[]{:S(2)}) collective-permute-start(bf16[1,48,1792]{2,1,0:T(8,128)(2,1)S(1)} %slice.46), channel_id=1, source_target_pairs={{0,4},{4,0},{8,12},{12,8},{1,5},{5,1},{9,13},{13,9},{2,6},{6,2},{1... | collective-permute-start | bytes 516104 | tf_op jit(solution)/shard_map/ppermute | solution.py:26
  108.3 15.5 %collective-permute-start.29 = (bf16[1,48,1792]{2,1,0:T(8,128)(2,1)S(1)}, bf16[1,48,1792]{2,1,0:T(8,128)(2,1)S(1)}, u32[]{:S(2)}, u32[]{:S(2)}) collective-permute-start(bf16[1,48,1792]{2,1,0:T(8,128)(2,1)S(1)} %slice.47), channel_id=1, source_target_pairs={{0,8},{4,12},{8,0},{12,4},{1,9},{5,13},{9,1},{13,5},{2,10},{6,14},... | collective-permute-start | bytes 516104 | tf_op jit(solution)/shard_map/ppermute | solution.py:26
  126.9 11.8 %collective-permute-start.30 = (bf16[192,2048]{1,0:T(8,128)(2,1)S(1)}, bf16[192,2048]{1,0:T(8,128)(2,1)S(1)}, u32[]{:S(2)}, u32[]{:S(2)}) collective-permute-start(bf16[192,2048]{1,0:T(8,128)(2,1)S(1)} %get-tuple-element.178), channel_id=1, source_target_pairs={{0,16},{16,0},{1,17},{17,1},{2,18},{18,2},{3,19},{19,3},{4,20},{20... | collective-permute-start | bytes 2359304 | tf_op jit(solution)/shard_map/ppermute | solution.py:26
  127.0 10.5 %collective-permute-start.34 = (bf16[2,48,1792]{2,1,0:T(8,128)(2,1)S(1)}, bf16[2,48,1792]{2,1,0:T(8,128)(2,1)S(1)}, u32[]{:S(2)}, u32[]{:S(2)}) collective-permute-start(bf16[2,48,1792]{2,1,0:T(8,128)(2,1)S(1)} %slice.48), channel_id=1, source_target_pairs={{0,4},{4,0},{8,12},{12,8},{1,5},{5,1},{9,13},{13,9},{2,6},{6,2},{1... | collective-permute-start | bytes 1032200 | tf_op jit(solution)/shard_map/ppermute | solution.py:26
  138.9 18.6 %collective-permute-start.31 = (bf16[48,2048]{1,0:T(8,128)(2,1)S(1)}, bf16[48,2048]{1,0:T(8,128)(2,1)S(1)}, u32[]{:S(2)}, u32[]{:S(2)}) collective-permute-start(bf16[48,2048]{1,0:T(8,128)(2,1)S(1)} %get-tuple-element.184), channel_id=1, source_target_pairs={{0,1},{1,0},{2,3},{3,2},{4,5},{5,4},{6,7},{7,6},{8,9},{9,8},{10,11... | collective-permute-start | bytes 589832 | tf_op jit(solution)/shard_map/ppermute | solution.py:26
  138.9 18.6 %collective-permute-start.32 = (bf16[48,2048]{1,0:T(8,128)(2,1)S(1)}, bf16[48,2048]{1,0:T(8,128)(2,1)S(1)}, u32[]{:S(2)}, u32[]{:S(2)}) collective-permute-start(bf16[48,2048]{1,0:T(8,128)(2,1)S(1)} %get-tuple-element.185), channel_id=1, source_target_pairs={{0,2},{1,3},{2,0},{3,1},{4,6},{5,7},{6,4},{7,5},{8,10},{9,11},{10,... | collective-permute-start | bytes 589832 | tf_op jit(solution)/shard_map/ppermute | solution.py:26
  140.8 16.7 %collective-permute-start.33 = (bf16[48,2048]{1,0:T(8,128)(2,1)S(1)}, bf16[48,2048]{1,0:T(8,128)(2,1)S(1)}, u32[]{:S(2)}, u32[]{:S(2)}) collective-permute-start(bf16[48,2048]{1,0:T(8,128)(2,1)S(1)} %get-tuple-element.186), channel_id=1, source_target_pairs={{0,3},{1,2},{2,1},{3,0},{4,7},{5,6},{6,5},{7,4},{8,11},{9,10},{10,... | collective-permute-start | bytes 589832 | tf_op jit(solution)/shard_map/ppermute | solution.py:26
  161.0 16.6 %collective-permute-start.37 = (bf16[48,2048]{1,0:T(8,128)(2,1)S(1)}, bf16[48,2048]{1,0:T(8,128)(2,1)S(1)}, u32[]{:S(2)}, u32[]{:S(2)}) collective-permute-start(bf16[48,2048]{1,0:T(8,128)(2,1)S(1)} %get-tuple-element.210), channel_id=1, source_target_pairs={{0,1},{1,0},{2,3},{3,2},{4,5},{5,4},{6,7},{7,6},{8,9},{9,8},{10,11... | collective-permute-start | bytes 589832 | tf_op jit(solution)/shard_map/ppermute | solution.py:26
  162.8 17.1 %collective-permute-start.38 = (bf16[48,2048]{1,0:T(8,128)(2,1)S(1)}, bf16[48,2048]{1,0:T(8,128)(2,1)S(1)}, u32[]{:S(2)}, u32[]{:S(2)}) collective-permute-start(bf16[48,2048]{1,0:T(8,128)(2,1)S(1)} %get-tuple-element.211), channel_id=1, source_target_pairs={{0,2},{1,3},{2,0},{3,1},{4,6},{5,7},{6,4},{7,5},{8,10},{9,11},{10,... | collective-permute-start | bytes 589832 | tf_op jit(solution)/shard_map/ppermute | solution.py:26
  162.9 17.0 %collective-permute-start.39 = (bf16[48,2048]{1,0:T(8,128)(2,1)S(1)}, bf16[48,2048]{1,0:T(8,128)(2,1)S(1)}, u32[]{:S(2)}, u32[]{:S(2)}) collective-permute-start(bf16[48,2048]{1,0:T(8,128)(2,1)S(1)} %get-tuple-element.212), channel_id=1, source_target_pairs={{0,3},{1,2},{2,1},{3,0},{4,7},{5,6},{6,5},{7,4},{8,11},{9,10},{10,... | collective-permute-start | bytes 589832 | tf_op jit(solution)/shard_map/ppermute | solution.py:26
  165.5 12.2 %collective-permute-start.42 = (f32[192,128]{1,0:T(8,128)S(1)}, f32[192,128]{1,0:T(8,128)S(1)}, u32[]{:S(2)}, u32[]{:S(2)}) collective-permute-start(f32[192,128]{1,0:T(8,128)S(1)} %add.72), channel_id=1, source_target_pairs={{0,8},{4,12},{8,0},{12,4},{1,9},{5,13},{9,1},{13,5},{2,10},{6,14},... | collective-permute-start | bytes 294920 | tf_op jit(solution)/shard_map/ppermute | solution.py:26
  (30 other events, 342.2 us)

commit v3 on v2

--- a/solution.py
+++ b/solution.py
@@ -50,6 +50,21 @@
 
 def plan_rows(pieces):
     return sum(count for _, count in pieces)
+
+
+def bring_kernel(place_ref, *refs):
+    refs[-1][0] = place_ref[0]
+
+
+def bring(place, weights):
+    return pl.pallas_call(
+        bring_kernel,
+        in_specs=[IN_SMEM] + [IN_VMEM] * len(weights),
+        out_specs=IN_SMEM,
+        out_shape=jax.ShapeDtypeStruct((1,), jnp.int32),
+        compiler_params=kernel_params(),
+        cost_estimate=pl.CostEstimate(flops=0, bytes_accessed=0, transcendentals=0),
+    )(place, *weights)
 
 
 def project_kernel(ring, plan, by_unit, amount, place_ref, *refs):
@@ -84,7 +99,7 @@
             place_rows(result, plan, outs, lead, columns)
 
 
-def project(place, parts, weights, masks, plan, by_unit):
+def project(place, parts, weights, masks, plan, by_unit, weigh=0):
     ring = len(parts) // 2
     amount = len(weights)
     features = parts[0].shape[1]
@@ -99,8 +114,8 @@
         + [jax.ShapeDtypeStruct((amount, count, units), BF16) for count in counts],
         compiler_params=kernel_params(),
         cost_estimate=pl.CostEstimate(
-            flops=2 * tokens * features * units * amount,
-            bytes_accessed=2 * amount * features * units,
+            flops=2 * tokens * features * units * amount * weigh,
+            bytes_accessed=2 * amount * features * units * weigh,
             transcendentals=0,
         ),
     )(place, *parts, *weights, *masks)
@@ -130,7 +145,7 @@
         place_rows(total, plan, outs, None, columns)
 
 
-def contract(parts, weights, masks, plan, types, by_unit):
+def contract(parts, weights, masks, plan, types, by_unit, weigh=0):
     amount = len(weights)
     units = parts[0].shape[2]
     pieces = [part.shape[1] for part in parts]
@@ -145,8 +160,8 @@
         + [jax.ShapeDtypeStruct((count, features), kind) for count, kind in zip(counts, types)],
         compiler_params=kernel_params(),
         cost_estimate=pl.CostEstimate(
-            flops=2 * tokens * features * units * amount,
-            bytes_accessed=2 * amount * features * units,
+            flops=2 * tokens * features * units * amount * weigh,
+            bytes_accessed=2 * amount * features * units * weigh,
             transcendentals=0,
         ),
     )(*parts, *weights, *masks)
@@ -174,9 +189,7 @@
         out_shape=[jax.ShapeDtypeStruct((rows, width), F32)] * amount,
         compiler_params=kernel_params(1),
         cost_estimate=pl.CostEstimate(
-            flops=2 * tokens * rows * width * amount,
-            bytes_accessed=4 * amount * rows * width,
-            transcendentals=0,
+            flops=0, bytes_accessed=0, transcendentals=0
         ),
     )(left, right, *masks)
 
@@ -349,29 +362,28 @@
     normed = (token_f * inv_rms * norm_gain).astype(BF16)
     gate_mask, up_mask, down_mask = widen(gate_keep), widen(up_keep), widen(down_keep)
     gate_groups, up_groups, down_groups = widen_grouped(gate_keep), widen_grouped(up_keep), widen_grouped(down_keep)
-    normed_core = core_swap(normed)
+    cot_core, normed_core = core_swap(cotangent), core_swap(normed)
     masks = [gate_mask, up_mask, down_mask, gate_groups, up_groups, down_groups]
-    cot_far, normed, normed_core, place, place_arg, masks = ordered(
-        cot_far, normed, normed_core, place, place_arg, masks
-    )
+    place, place_arg, masks = ordered(place, place_arg, masks)
     gate_mask, up_mask, down_mask, gate_groups, up_groups, down_groups = masks
+    place_arg = bring(place_arg, [down_weight, gate_weight, up_weight])
+    cot_far, cot_core, normed, normed_core, place_arg = ordered(cot_far, cot_core, normed, normed_core, place_arg)
     cot_own = [cotangent, *cot_far]
-    cot_other = [core_swap(part) for part in cot_own]
+    cot_other = [cot_core] + [core_swap(part) for part in cot_far]
 
     normed_far = level_swaps([normed] * 3)
-    seen_cot, *one_parts = project(place_arg, cot_own + cot_other, [down_weight], [down_mask], first_plan, True)
+    seen_cot, *one_parts = project(
+        place_arg, cot_own + cot_other, [down_weight], [down_mask], first_plan, True
+    )
     one_x, one_y = sum_first(*one_parts[:2])
-    one_keep = one_parts[2:]
-    normed_far, one_x, one_y = ordered(normed_far, one_x, one_y)
+    normed_far, one_keep = ordered(normed_far, one_parts[2:])
     normed_own = [normed, *normed_far]
     normed_other = [normed_core] + [core_swap(part) for part in normed_far]
-    one_late = sum_middle(*one_keep[:2], one_x, one_y)
-    normed_other, one_late = ordered(normed_other, one_late)
-
-    one_last = sum_last(*one_late)
+
     seen_rows, *pair_parts = project(place_arg, normed_own + normed_other, [gate_weight, up_weight], [gate_mask, up_mask], first_plan, False)
-    one_last, pair_parts = ordered(one_last, pair_parts)
+    one_x, one_y, pair_parts = ordered(one_x, one_y, pair_parts)
     pair_x, pair_y = sum_first(*pair_parts[:2])
+    one_last = sum_last(*sum_middle(*one_keep[:2], one_x, one_y))
     pair_last = sum_last(*sum_middle(*pair_parts[2:4], pair_x, pair_y))
     hidden_share, grads_share = activate(
         [pair_parts[4], pair_x, pair_y, *pair_last], [one_keep[2], one_x, one_y, *one_last]
@@ -383,15 +395,15 @@
     grads_x, grads_y = gather_first(grads_share)
     hidden_last = gather_last(*hidden_middle)
     hidden, branch_own, branch_other = contract(
-        [hidden_share, hidden_x, hidden_y, *hidden_last], [down_weight], [down_mask], last_plan, (F32, BF16), True
+        [hidden_share, hidden_x, hidden_y, *hidden_last], [down_weight], [down_mask], last_plan, (F32, BF16), True, 10
     )
     grads_x, grads_y, branch_own, branch_other = ordered(grads_x, grads_y, branch_own, branch_other)
     branch_got = core_swap(branch_other)
     grads_middle = gather_middle(grads_x, grads_y)
     grads_last = gather_last(*grads_middle)
     branch_kept, *branch_parts = owner(place_arg, branch_own, branch_got, cols)
-    hidden, branch_parts = ordered(hidden, branch_parts)
     branch_far = level_swaps(branch_parts)
+    hidden, grads_middle = ordered(hidden, grads_middle)
     (grad_down,) = outer(hidden[0], seen_cot[None], [down_groups])
     grads_last, grad_down = ordered(grads_last, grad_down)
 
@@ -399,6 +411,7 @@
         [grads_share, grads_x, grads_y, *grads_last], [gate_weight, up_weight], [gate_mask, up_mask], last_plan, (F32, BF16), False
     )
     branch_far, normed_mine, normed_theirs = ordered(branch_far, normed_mine, normed_theirs)
+
     kept, *parts, across, down_sum = owner(place_arg, normed_mine, core_swap(normed_theirs), cols, normed_own)
     grads, parts, across, down_sum = ordered(grads, parts, across, down_sum)
     far = level_swaps(parts)
@@ -406,13 +419,15 @@
     down_both = down_sum + core_swap(down_sum)
     across_x, down_both, grads = ordered(across_x, down_both, grads)
     across_row = across_x + row_swap(across_x, 2)
-    grad_gate, grad_up = outer(seen_rows, grads, [gate_groups, up_groups])
-    far, across_row, down_both, grad_gate, grad_up = ordered(far, across_row, down_both, grad_gate, grad_up)
     sums = [
         jnp.concatenate([across_row[step * unit : (step + 1) * unit], down_both.reshape(-1, 128)])
         for step in range(cols)
     ]
-    sums_total = balanced(sums[0], level_swaps(sums[1:]))
+    grads, sums = ordered(grads, sums)
+    sums_far = level_swaps(sums[1:])
+    grad_gate, grad_up = outer(seen_rows, grads, [gate_groups, up_groups])
+    far, sums_far, grad_gate, grad_up = ordered(far, sums_far, grad_gate, grad_up)
+    sums_total = balanced(sums[0], sums_far)
     branch = owner_total(branch_kept, branch_far).astype(BF16)
     normed_grad = owner_total(kept, far)
     grad_gain = sums_total[unit:].reshape(features) / norm_gain

time: 192 us -> 173 us (0.901)
  waiting for transfers between devices: 87.8 us -> 63.1 us
  Pallas kernels: 39.9 us -> 43 us
  local copies, waits for them, and re-layouts: 7.72 us -> 9.88 us
    ppermute x46, waiting for transfers between devices: 87.8 us -> 63.1 us  [swap(): return lax.ppermute(value, axis, [(i, i ^ step) for i in range(size)])]
    unnamed x18 -> x20, local copies, waits for them, and re-layouts: 7.15 us -> 9.3 us
  transfers between devices with their start and end apart: 46 -> 46, of which waited for: 25 -> 20; matrix products, arithmetic and copies ran while one was open for 2% -> 3% of each run, Pallas kernels for 18% -> 23%
where the time goes in v3:
time: 173 us
  waiting for transfers between devices  63.1 us (36%)
  starting transfers between devices  49 us (28%)
  Pallas kernels  43 us (25%)
  local copies, waits for them, and re-layouts  9.88 us (6%)
  other arithmetic  6.9 us (4%)
    ppermute x46, waiting for transfers between devices, swap(): return lax.ppermute(value, axis, [(i, i ^ step) for i in range(size)])  63.1 us
    ppermute x46, starting transfers between devices, swap(): return lax.ppermute(value, axis, [(i, i ^ step) for i in range(size)])  49 us
    pallas_call x2, Pallas kernels, outer(): pl.pallas_call(outer_kernel, grid=(rows // edge,), in_specs=[IN_VMEM, IN_...  19.6 us
    pallas_call x2, Pallas kernels, project(): pl.pallas_call(functools.partial(project_kernel, ring, plan, by_unit, amo...  10.8 us
    unnamed x20, local copies, waits for them, and re-layouts  9.3 us
    pallas_call x2, Pallas kernels, contract(): pl.pallas_call(functools.partial(contract_kernel, pieces, plan, by_unit,...  8.91 us
  transfers between devices with their start and end apart: 46, of which 20 were waited for; matrix products, arithmetic and copies ran while one was open for 3% of the time, Pallas kernels for 23%

profile of v3, /device:TPU:0, one launch (start us, length us, event | category | flops | bytes accessed | tf_op | source)
XLA Modules:
  0.0 172.9 jit_solution(10916511243231895294)
XLA Ops:
  1.7 3.0 %collective-permute-start.4 = (f32[48]{0:T(128)S(1)}, f32[48]{0:T(128)S(1)}, u32[]{:S(2)}, u32[]{:S(2)}) collective-permute-start(f32[48]{0:T(128)S(1)} %fusion.6), channel_id=1, source_target_pairs={{0,4},{4,0},{8,12},{12,8},{1,5},{5,1},{9,13},{13,9},{2,6},{6,2},{1... | collective-permute-start | bytes 584 | tf_op jit(solution)/shard_map/ppermute | solution.py:26
  4.7 3.6 %collective-permute-start.2 = (bf16[48,2048]{1,0:T(8,128)(2,1)}, bf16[48,2048]{1,0:T(8,128)(2,1)S(1)}, u32[]{:S(2)}, u32[]{:S(2)}) collective-permute-start(bf16[48,2048]{1,0:T(8,128)(2,1)} %refs_0_.3), channel_id=1, source_target_pairs={{0,3},{1,2},{2,1},{3,0},{4,7},{5,6},{6,5},{7,4},{8,11},{9,10},{10,... | collective-permute-start | bytes 589832 | tf_op jit(solution)/shard_map/ppermute | solution.py:26
  15.0 3.1 %copy-done = bf16[2048,1792]{1,0:T(8,128)(2,1)S(1)} copy-done((bf16[2048,1792]{1,0:T(8,128)(2,1)S(1)}, bf16[2048,1792]{1,0:T(8,128)(2,1)}, u32[]{:S(2)}) %copy-start) | copy-done | bytes 7340056
  18.1 3.1 %copy-done.2 = bf16[2048,1792]{1,0:T(8,128)(2,1)S(1)} copy-done((bf16[2048,1792]{1,0:T(8,128)(2,1)S(1)}, bf16[2048,1792]{1,0:T(8,128)(2,1)}, u32[]{:S(2)}) %copy-start.2) | copy-done | bytes 7340056
  21.2 3.1 %copy-done.4 = bf16[1792,2048]{1,0:T(8,128)(2,1)S(1)} copy-done((bf16[1792,2048]{1,0:T(8,128)(2,1)S(1)}, bf16[1792,2048]{1,0:T(8,128)(2,1)}, u32[]{:S(2)}) %copy-start.4) | copy-done | bytes 7340056
  26.0 3.6 %collective-permute-start.14 = (bf16[48,2048]{1,0:T(8,128)(2,1)S(1)}, bf16[48,2048]{1,0:T(8,128)(2,1)S(1)}, u32[]{:S(2)}, u32[]{:S(2)}) collective-permute-start(bf16[48,2048]{1,0:T(8,128)(2,1)S(1)} %fusion.2.refs_0_), channel_id=1, source_target_pairs={{0,3},{1,2},{2,1},{3,0},{4,7},{5,6},{6,5},{7,4},{8,11},{9,10},{10,... | collective-permute-start | bytes 589832 | tf_op jit(solution)/shard_map/ppermute | solution.py:26
  30.4 4.2 %shard_map.137 = (bf16[384,2048]{1,0:T(8,128)(2,1)S(1)}, bf16[1,96,1792]{2,1,0:T(8,128)(2,1)S(1)}, bf16[1,96,1792]{2,1,0:T(8,128)(2,1)S(1)}, bf16[1,48,1792]{2,1...) custom-call(s32[1]{0:T(128)} %shard_map.136.place_ref, ...), custom_call_target="tpu_custom_call" | custom-call | tf_op jit(solution)/shard_map/pallas_call | solution.py:109
  36.7 9.5 %collective-permute-done.13.refs_2_ = bf16[48,2048]{1,0:T(8,128)(2,1)S(1)} collective-permute-done((bf16[48,2048]{1,0:T(8,128)(2,1)S(1)}, bf16[48,2048]{1,0:T(8,128)(2,1)S(1)}, u32[]{:S(2)}, u32[]{:S(2)}) %collective-permute-start.13) | collective-permute-done | bytes 196640 | tf_op jit(solution)/shard_map/ppermute | solution.py:26
  48.2 6.7 %shard_map.138 = (bf16[384,2048]{1,0:T(8,128)(2,1)S(1)}, bf16[2,96,1792]{2,1,0:T(8,128)(2,1)S(1)}, bf16[2,96,1792]{2,1,0:T(8,128)(2,1)S(1)}, bf16[2,48,1792]{2,1...) custom-call(s32[1]{0:T(128)} %shard_map.136.place_ref, ...), custom_call_target="tpu_custom_call" | custom-call | tf_op jit(solution)/shard_map/pallas_call | solution.py:109
  58.6 14.6 %collective-permute-done.18.refs_1_ = bf16[2,96,1792]{2,1,0:T(8,128)(2,1)S(1)} collective-permute-done((bf16[2,96,1792]{2,1,0:T(8,128)(2,1)S(1)}, bf16[2,96,1792]{2,1,0:T(8,128)(2,1)S(1)}, u32[]{:S(2)}, u32[]{:S(2)}) %collective-permute-start.18) | collective-permute-done | bytes 688160 | tf_op jit(solution)/shard_map/ppermute | solution.py:26
  76.9 10.2 %collective-permute-done.22.refs_8_ = bf16[1,48,1792]{2,1,0:T(8,128)(2,1)S(1)} collective-permute-done((bf16[1,48,1792]{2,1,0:T(8,128)(2,1)S(1)}, bf16[1,48,1792]{2,1,0:T(8,128)(2,1)S(1)}, u32[]{:S(2)}, u32[]{:S(2)}) %collective-permute-start.22) | collective-permute-done | bytes 172064 | tf_op jit(solution)/shard_map/ppermute | solution.py:26
  90.6 5.7 %collective-permute-done.25.refs_2_ = bf16[1,96,1792]{2,1,0:T(8,128)(2,1)S(1)} collective-permute-done((bf16[1,96,1792]{2,1,0:T(8,128)(2,1)S(1)}, bf16[1,96,1792]{2,1,0:T(8,128)(2,1)S(1)}, u32[]{:S(2)}, u32[]{:S(2)}) %collective-permute-start.25) | collective-permute-done | bytes 344096 | tf_op jit(solution)/shard_map/ppermute | solution.py:26
  96.3 1.8 %collective-permute-done.24.refs_1_ = bf16[1,96,1792]{2,1,0:T(8,128)(2,1)S(1)} collective-permute-done((bf16[1,96,1792]{2,1,0:T(8,128)(2,1)S(1)}, bf16[1,96,1792]{2,1,0:T(8,128)(2,1)S(1)}, u32[]{:S(2)}, u32[]{:S(2)}) %collective-permute-start.24) | collective-permute-done | bytes 344096 | tf_op jit(solution)/shard_map/ppermute | solution.py:26
  102.3 3.3 %collective-permute-done.28.refs_3_ = bf16[1,48,1792]{2,1,0:T(8,128)(2,1)S(1)} collective-permute-done((bf16[1,48,1792]{2,1,0:T(8,128)(2,1)S(1)}, bf16[1,48,1792]{2,1,0:T(8,128)(2,1)S(1)}, u32[]{:S(2)}, u32[]{:S(2)}) %collective-permute-start.28) | collective-permute-done | bytes 172064 | tf_op jit(solution)/shard_map/ppermute | solution.py:26
  105.8 3.0 %shard_map.140 = (bf16[1,384,1792]{2,1,0:T(8,128)(2,1)S(1)}, f32[192,2048]{1,0:T(8,128)S(1)}, bf16[192,2048]{1,0:T(8,128)(2,1)S(1)}) custom-call(bf16[1,96,1792]{2,1,0:T(8,128)(2,1)S(1)} %get-tuple-element.162.refs_0_, bf16[1,96,1792]{2,1,0:T(8,128)(2,1)S(1)} %collective-permute-done.24.refs_1_, bf16[1,96,1792]{2,1,0:T(8,128)(2,1)S(1)} %collective-permute-done.25.refs_2_, ...), custom_call_target="tpu_custom_call" | custom-call | flops 28185722880 | bytes 73400320 | tf_op jit(solution)/shard_map/pallas_call | solution.py:155
  108.8 6.6 %collective-permute-done.27.refs_2_ = bf16[2,96,1792]{2,1,0:T(8,128)(2,1)S(1)} collective-permute-done((bf16[2,96,1792]{2,1,0:T(8,128)(2,1)S(1)}, bf16[2,96,1792]{2,1,0:T(8,128)(2,1)S(1)}, u32[]{:S(2)}, u32[]{:S(2)}) %collective-permute-start.27) | collective-permute-done | bytes 688160 | tf_op jit(solution)/shard_map/ppermute | solution.py:26
  119.1 2.9 %collective-permute-start.32 = (bf16[48,2048]{1,0:T(8,128)(2,1)S(1)}, bf16[48,2048]{1,0:T(8,128)(2,1)S(1)}, u32[]{:S(2)}, u32[]{:S(2)}) collective-permute-start(bf16[48,2048]{1,0:T(8,128)(2,1)S(1)} %get-tuple-element.178), channel_id=1, source_target_pairs={{0,2},{1,3},{2,0},{3,1},{4,6},{5,7},{6,4},{7,5},{8,10},{9,11},{10,... | collective-permute-start | bytes 589832 | tf_op jit(solution)/shard_map/ppermute | solution.py:26
  123.5 8.2 %shard_map.142 = f32[1792,2048]{1,0:T(8,128)} custom-call(bf16[384,1792]{1,0:T(8,128)(2,1)S(1)} %bitcast.18, bf16[1,384,2048]{2,1,0:T(8,128)(2,1)S(1)} %bitcast.17, bf16[7,2,2048]{2,1,0:T(2,128)(2,1)S(1)} %convert_element_type.112.refs_0_), custom_call_target="tpu_custom_call" | custom-call | tf_op jit(solution)/shard_map/pallas_call | solution.py:184
  131.7 5.9 %shard_map.143 = (bf16[2,384,1792]{2,1,0:T(8,128)(2,1)S(1)}, f32[192,2048]{1,0:T(8,128)S(1)}, bf16[192,2048]{1,0:T(8,128)(2,1)S(1)}) custom-call(bf16[2,96,1792]{2,1,0:T(8,128)(2,1)S(1)} %get-tuple-element.165.refs_0_, bf16[2,96,1792]{2,1,0:T(8,128)(2,1)S(1)} %collective-permute-done.26.refs_1_, bf16[2,96,1792]{2,1,0:T(8,128)(2,1)S(1)} %collective-permute-done.27.refs_2_, ...), custom_call_target="tpu_custom_call" | custom-call | tf_op jit(solution)/shard_map/pallas_call | solution.py:155
  137.8 2.3 %collective-permute-done.36.got_ref = bf16[192,2048]{1,0:T(8,128)(2,1)S(1)} collective-permute-done((bf16[192,2048]{1,0:T(8,128)(2,1)S(1)}, bf16[192,2048]{1,0:T(8,128)(2,1)S(1)}, u32[]{:S(2)}, u32[]{:S(2)}) %collective-permute-start.36) | collective-permute-done | bytes 786464 | tf_op jit(solution)/shard_map/ppermute | solution.py:26
  143.5 2.5 %collective-permute-done.40 = f32[192,128]{1,0:T(8,128)S(1)} collective-permute-done((f32[192,128]{1,0:T(8,128)S(1)}, f32[192,128]{1,0:T(8,128)S(1)}, u32[]{:S(2)}, u32[]{:S(2)}) %collective-permute-start.40) | collective-permute-done | bytes 98336 | tf_op jit(solution)/shard_map/ppermute | solution.py:26
  147.1 2.3 %collective-permute-start.37 = (bf16[48,2048]{1,0:T(8,128)(2,1)S(1)}, bf16[48,2048]{1,0:T(8,128)(2,1)S(1)}, u32[]{:S(2)}, u32[]{:S(2)}) collective-permute-start(bf16[48,2048]{1,0:T(8,128)(2,1)S(1)} %get-tuple-element.204), channel_id=1, source_target_pairs={{0,1},{1,0},{2,3},{3,2},{4,5},{5,4},{6,7},{7,6},{8,9},{9,8},{10,11... | collective-permute-start | bytes 589832 | tf_op jit(solution)/shard_map/ppermute | solution.py:26
  156.7 2.4 %collective-permute-start.45 = (f32[64,128]{1,0:T(8,128)S(1)}, f32[64,128]{1,0:T(8,128)S(1)}, u32[]{:S(2)}, u32[]{:S(2)}) collective-permute-start(f32[64,128]{1,0:T(8,128)S(1)} %get-tuple-element.215), channel_id=1, source_target_pairs={{0,3},{1,2},{2,1},{3,0},{4,7},{5,6},{6,5},{7,4},{8,11},{9,10},{10,... | collective-permute-start | bytes 98312 | tf_op jit(solution)/shard_map/ppermute | solution.py:26
  159.9 11.4 %shard_map.145 = (f32[2048,1792]{1,0:T(8,128)}, f32[2048,1792]{1,0:T(8,128)}) custom-call(bf16[384,2048]{1,0:T(8,128)(2,1)S(1)} %get-tuple-element.216.left_ref, bf16[2,384,1792]{2,1,0:T(8,128)(2,1)S(1)} %get-tuple-element.217.right_ref, bf16[8,2,1792]{2,1,0:T(2,128)(2,1)S(1)} %convert_element_type.110.refs_0_, ...), custom_call_target="tpu_custom_call" | custom-call | tf_op jit(solution)/shard_map/pallas_call | solution.py:184
  (130 shorter events, 49.0 us)
Async XLA Ops:
  4.7 20.1 %collective-permute-start.2 = (bf16[48,2048]{1,0:T(8,128)(2,1)}, bf16[48,2048]{1,0:T(8,128)(2,1)S(1)}, u32[]{:S(2)}, u32[]{:S(2)}) collective-permute-start(bf16[48,2048]{1,0:T(8,128)(2,1)} %refs_0_.3), channel_id=1, source_target_pairs={{0,3},{1,2},{2,1},{3,0},{4,7},{5,6},{6,5},{7,4},{8,11},{9,10},{10,... | collective-permute-start | bytes 589832 | tf_op jit(solution)/shard_map/ppermute | solution.py:26
  8.3 16.6 %collective-permute-start.1 = (bf16[48,2048]{1,0:T(8,128)(2,1)}, bf16[48,2048]{1,0:T(8,128)(2,1)S(1)}, u32[]{:S(2)}, u32[]{:S(2)}) collective-permute-start(bf16[48,2048]{1,0:T(8,128)(2,1)} %refs_0_.3), channel_id=1, source_target_pairs={{0,2},{1,3},{2,0},{3,1},{4,6},{5,7},{6,4},{7,5},{8,10},{9,11},{10,... | collective-permute-start | bytes 589832 | tf_op jit(solution)/shard_map/ppermute | solution.py:26
  8.3 16.6 %collective-permute-start = (bf16[48,2048]{1,0:T(8,128)(2,1)}, bf16[48,2048]{1,0:T(8,128)(2,1)S(1)}, u32[]{:S(2)}, u32[]{:S(2)}) collective-permute-start(bf16[48,2048]{1,0:T(8,128)(2,1)} %refs_0_.3), channel_id=1, source_target_pairs={{0,1},{1,0},{2,3},{3,2},{4,5},{5,4},{6,7},{7,6},{8,9},{9,8},{10,11... | collective-permute-start | bytes 589832 | tf_op jit(solution)/shard_map/ppermute | solution.py:26
  9.1 15.8 %collective-permute-start.3 = (bf16[48,2048]{1,0:T(8,128)(2,1)}, bf16[48,2048]{1,0:T(8,128)(2,1)S(1)}, u32[]{:S(2)}, u32[]{:S(2)}) collective-permute-start(bf16[48,2048]{1,0:T(8,128)(2,1)} %refs_0_.3), channel_id=1, source_target_pairs={{0,16},{16,0},{1,17},{17,1},{2,18},{18,2},{3,19},{19,3},{4,20},{20... | collective-permute-start | bytes 589832 | tf_op jit(solution)/shard_map/ppermute | solution.py:26
  29.6 16.6 %collective-permute-start.13 = (bf16[48,2048]{1,0:T(8,128)(2,1)S(1)}, bf16[48,2048]{1,0:T(8,128)(2,1)S(1)}, u32[]{:S(2)}, u32[]{:S(2)}) collective-permute-start(bf16[48,2048]{1,0:T(8,128)(2,1)S(1)} %fusion.2.refs_0_), channel_id=1, source_target_pairs={{0,2},{1,3},{2,0},{3,1},{4,6},{5,7},{6,4},{7,5},{8,10},{9,11},{10,... | collective-permute-start | bytes 589832 | tf_op jit(solution)/shard_map/ppermute | solution.py:26
  29.6 16.6 %collective-permute-start.12 = (bf16[48,2048]{1,0:T(8,128)(2,1)S(1)}, bf16[48,2048]{1,0:T(8,128)(2,1)S(1)}, u32[]{:S(2)}, u32[]{:S(2)}) collective-permute-start(bf16[48,2048]{1,0:T(8,128)(2,1)S(1)} %fusion.2.refs_0_), channel_id=1, source_target_pairs={{0,1},{1,0},{2,3},{3,2},{4,5},{5,4},{6,7},{7,6},{8,9},{9,8},{10,11... | collective-permute-start | bytes 589832 | tf_op jit(solution)/shard_map/ppermute | solution.py:26
  34.5 20.3 %collective-permute-start.10 = (bf16[1,96,1792]{2,1,0:T(8,128)(2,1)S(1)}, bf16[1,96,1792]{2,1,0:T(8,128)(2,1)S(1)}, u32[]{:S(2)}, u32[]{:S(2)}) collective-permute-start(bf16[1,96,1792]{2,1,0:T(8,128)(2,1)S(1)} %get-tuple-element.126), channel_id=1, source_target_pairs={{0,4},{4,0},{8,12},{12,8},{1,5},{5,1},{9,13},{13,9},{2,6},{6,2},{1... | collective-permute-start | bytes 1032200 | tf_op jit(solution)/shard_map/ppermute | solution.py:26
  34.9 20.0 %collective-permute-start.11 = (bf16[1,96,1792]{2,1,0:T(8,128)(2,1)S(1)}, bf16[1,96,1792]{2,1,0:T(8,128)(2,1)S(1)}, u32[]{:S(2)}, u32[]{:S(2)}) collective-permute-start(bf16[1,96,1792]{2,1,0:T(8,128)(2,1)S(1)} %get-tuple-element.127), channel_id=1, source_target_pairs={{0,8},{4,12},{8,0},{12,4},{1,9},{5,13},{9,1},{13,5},{2,10},{6,14},... | collective-permute-start | bytes 1032200 | tf_op jit(solution)/shard_map/ppermute | solution.py:26
  54.9 18.3 %collective-permute-start.18 = (bf16[2,96,1792]{2,1,0:T(8,128)(2,1)S(1)}, bf16[2,96,1792]{2,1,0:T(8,128)(2,1)S(1)}, u32[]{:S(2)}, u32[]{:S(2)}) collective-permute-start(bf16[2,96,1792]{2,1,0:T(8,128)(2,1)S(1)} %get-tuple-element.146), channel_id=1, source_target_pairs={{0,4},{4,0},{8,12},{12,8},{1,5},{5,1},{9,13},{13,9},{2,6},{6,2},{1... | collective-permute-start | bytes 2064392 | tf_op jit(solution)/shard_map/ppermute | solution.py:26
  55.5 17.7 %collective-permute-start.19 = (bf16[2,96,1792]{2,1,0:T(8,128)(2,1)S(1)}, bf16[2,96,1792]{2,1,0:T(8,128)(2,1)S(1)}, u32[]{:S(2)}, u32[]{:S(2)}) collective-permute-start(bf16[2,96,1792]{2,1,0:T(8,128)(2,1)S(1)} %get-tuple-element.147), channel_id=1, source_target_pairs={{0,8},{4,12},{8,0},{12,4},{1,9},{5,13},{9,1},{13,5},{2,10},{6,14},... | collective-permute-start | bytes 2064392 | tf_op jit(solution)/shard_map/ppermute | solution.py:26
  57.1 19.8 %collective-permute-start.23 = (bf16[1,48,1792]{2,1,0:T(8,128)(2,1)S(1)}, bf16[1,48,1792]{2,1,0:T(8,128)(2,1)S(1)}, u32[]{:S(2)}, u32[]{:S(2)}) collective-permute-start(bf16[1,48,1792]{2,1,0:T(8,128)(2,1)S(1)} %add_convert_fusion.3), channel_id=1, source_target_pairs={{0,4},{4,0},{8,12},{12,8},{1,5},{5,1},{9,13},{13,9},{2,6},{6,2},{1... | collective-permute-start | bytes 516104 | tf_op jit(solution)/shard_map/ppermute | solution.py:26
  73.3 13.7 %collective-permute-start.21 = (bf16[2,48,1792]{2,1,0:T(8,128)(2,1)S(1)}, bf16[2,48,1792]{2,1,0:T(8,128)(2,1)S(1)}, u32[]{:S(2)}, u32[]{:S(2)}) collective-permute-start(bf16[2,48,1792]{2,1,0:T(8,128)(2,1)S(1)} %add_convert_fusion), channel_id=1, source_target_pairs={{0,4},{4,0},{8,12},{12,8},{1,5},{5,1},{9,13},{13,9},{2,6},{6,2},{1... | collective-permute-start | bytes 1032200 | tf_op jit(solution)/shard_map/ppermute | solution.py:26
  99.0 16.5 %collective-permute-start.27 = (bf16[2,96,1792]{2,1,0:T(8,128)(2,1)S(1)}, bf16[2,96,1792]{2,1,0:T(8,128)(2,1)S(1)}, u32[]{:S(2)}, u32[]{:S(2)}) collective-permute-start(bf16[2,96,1792]{2,1,0:T(8,128)(2,1)S(1)} %get-tuple-element.165.refs_0_), channel_id=1, source_target_pairs={{0,8},{4,12},{8,0},{12,4},{1,9},{5,13},{9,1},{13,5},{2,10},{6,14},... | collective-permute-start | bytes 2064392 | tf_op jit(solution)/shard_map/ppermute | solution.py:26
  100.5 15.5 %collective-permute-start.26 = (bf16[2,96,1792]{2,1,0:T(8,128)(2,1)S(1)}, bf16[2,96,1792]{2,1,0:T(8,128)(2,1)S(1)}, u32[]{:S(2)}, u32[]{:S(2)}) collective-permute-start(bf16[2,96,1792]{2,1,0:T(8,128)(2,1)S(1)} %get-tuple-element.165.refs_0_), channel_id=1, source_target_pairs={{0,4},{4,0},{8,12},{12,8},{1,5},{5,1},{9,13},{13,9},{2,6},{6,2},{1... | collective-permute-start | bytes 2064392 | tf_op jit(solution)/shard_map/ppermute | solution.py:26
  116.0 15.7 %collective-permute-start.34 = (bf16[2,48,1792]{2,1,0:T(8,128)(2,1)S(1)}, bf16[2,48,1792]{2,1,0:T(8,128)(2,1)S(1)}, u32[]{:S(2)}, u32[]{:S(2)}) collective-permute-start(bf16[2,48,1792]{2,1,0:T(8,128)(2,1)S(1)} %slice.48), channel_id=1, source_target_pairs={{0,4},{4,0},{8,12},{12,8},{1,5},{5,1},{9,13},{13,9},{2,6},{6,2},{1... | collective-permute-start | bytes 1032200 | tf_op jit(solution)/shard_map/ppermute | solution.py:26
  117.2 14.5 %collective-permute-start.35 = (bf16[2,48,1792]{2,1,0:T(8,128)(2,1)S(1)}, bf16[2,48,1792]{2,1,0:T(8,128)(2,1)S(1)}, u32[]{:S(2)}, u32[]{:S(2)}) collective-permute-start(bf16[2,48,1792]{2,1,0:T(8,128)(2,1)S(1)} %slice.49), channel_id=1, source_target_pairs={{0,8},{4,12},{8,0},{12,4},{1,9},{5,13},{9,1},{13,5},{2,10},{6,14},... | collective-permute-start | bytes 1032200 | tf_op jit(solution)/shard_map/ppermute | solution.py:26
  119.1 18.6 %collective-permute-start.31 = (bf16[48,2048]{1,0:T(8,128)(2,1)S(1)}, bf16[48,2048]{1,0:T(8,128)(2,1)S(1)}, u32[]{:S(2)}, u32[]{:S(2)}) collective-permute-start(bf16[48,2048]{1,0:T(8,128)(2,1)S(1)} %get-tuple-element.177), channel_id=1, source_target_pairs={{0,1},{1,0},{2,3},{3,2},{4,5},{5,4},{6,7},{7,6},{8,9},{9,8},{10,11... | collective-permute-start | bytes 589832 | tf_op jit(solution)/shard_map/ppermute | solution.py:26
  119.1 18.5 %collective-permute-start.32 = (bf16[48,2048]{1,0:T(8,128)(2,1)S(1)}, bf16[48,2048]{1,0:T(8,128)(2,1)S(1)}, u32[]{:S(2)}, u32[]{:S(2)}) collective-permute-start(bf16[48,2048]{1,0:T(8,128)(2,1)S(1)} %get-tuple-element.178), channel_id=1, source_target_pairs={{0,2},{1,3},{2,0},{3,1},{4,6},{5,7},{6,4},{7,5},{8,10},{9,11},{10,... | collective-permute-start | bytes 589832 | tf_op jit(solution)/shard_map/ppermute | solution.py:26
  122.1 15.6 %collective-permute-start.33 = (bf16[48,2048]{1,0:T(8,128)(2,1)S(1)}, bf16[48,2048]{1,0:T(8,128)(2,1)S(1)}, u32[]{:S(2)}, u32[]{:S(2)}) collective-permute-start(bf16[48,2048]{1,0:T(8,128)(2,1)S(1)} %get-tuple-element.179), channel_id=1, source_target_pairs={{0,3},{1,2},{2,1},{3,0},{4,7},{5,6},{6,5},{7,4},{8,11},{9,10},{10,... | collective-permute-start | bytes 589832 | tf_op jit(solution)/shard_map/ppermute | solution.py:26
  149.5 21.7 %collective-permute-start.38 = (bf16[48,2048]{1,0:T(8,128)(2,1)S(1)}, bf16[48,2048]{1,0:T(8,128)(2,1)S(1)}, u32[]{:S(2)}, u32[]{:S(2)}) collective-permute-start(bf16[48,2048]{1,0:T(8,128)(2,1)S(1)} %get-tuple-element.205), channel_id=1, source_target_pairs={{0,2},{1,3},{2,0},{3,1},{4,6},{5,7},{6,4},{7,5},{8,10},{9,11},{10,... | collective-permute-start | bytes 589832 | tf_op jit(solution)/shard_map/ppermute | solution.py:26
  150.4 20.8 %collective-permute-start.39 = (bf16[48,2048]{1,0:T(8,128)(2,1)S(1)}, bf16[48,2048]{1,0:T(8,128)(2,1)S(1)}, u32[]{:S(2)}, u32[]{:S(2)}) collective-permute-start(bf16[48,2048]{1,0:T(8,128)(2,1)S(1)} %get-tuple-element.206), channel_id=1, source_target_pairs={{0,3},{1,2},{2,1},{3,0},{4,7},{5,6},{6,5},{7,4},{8,11},{9,10},{10,... | collective-permute-start | bytes 589832 | tf_op jit(solution)/shard_map/ppermute | solution.py:26
  151.9 19.3 %collective-permute-start.43 = (f32[64,128]{1,0:T(8,128)S(1)}, f32[64,128]{1,0:T(8,128)S(1)}, u32[]{:S(2)}, u32[]{:S(2)}) collective-permute-start(f32[64,128]{1,0:T(8,128)S(1)} %get-tuple-element.213), channel_id=1, source_target_pairs={{0,1},{1,0},{2,3},{3,2},{4,5},{5,4},{6,7},{7,6},{8,9},{9,8},{10,11... | collective-permute-start | bytes 98312 | tf_op jit(solution)/shard_map/ppermute | solution.py:26
  153.4 17.8 %collective-permute-start.44 = (f32[64,128]{1,0:T(8,128)S(1)}, f32[64,128]{1,0:T(8,128)S(1)}, u32[]{:S(2)}, u32[]{:S(2)}) collective-permute-start(f32[64,128]{1,0:T(8,128)S(1)} %get-tuple-element.214), channel_id=1, source_target_pairs={{0,2},{1,3},{2,0},{3,1},{4,6},{5,7},{6,4},{7,5},{8,10},{9,11},{10,... | collective-permute-start | bytes 98312 | tf_op jit(solution)/shard_map/ppermute | solution.py:26
  156.7 14.5 %collective-permute-start.45 = (f32[64,128]{1,0:T(8,128)S(1)}, f32[64,128]{1,0:T(8,128)S(1)}, u32[]{:S(2)}, u32[]{:S(2)}) collective-permute-start(f32[64,128]{1,0:T(8,128)S(1)} %get-tuple-element.215), channel_id=1, source_target_pairs={{0,3},{1,2},{2,1},{3,0},{4,7},{5,6},{6,5},{7,4},{8,11},{9,10},{10,... | collective-permute-start | bytes 98312 | tf_op jit(solution)/shard_map/ppermute | solution.py:26
  (31 other events, 268.9 us)

commit v4 on v3

--- a/solution.py
+++ b/solution.py
@@ -195,9 +195,8 @@
 
 
 def owner_kernel(count, place_ref, own_ref, got_ref, *refs):
-    factors, outs, sums = refs[:-count], refs[-count:], ()
-    if factors:
-        factors, outs, sums = refs[:count], refs[count : 2 * count], refs[2 * count :]
+    factors = refs[:count] if len(refs) > count else ()
+    outs = refs[len(factors) : len(factors) + count]
     unit = outs[0].shape[0]
     place = place_ref[0]
     down = None
@@ -206,13 +205,10 @@
         part = own_ref[rows, :] + got_ref[rows, :].astype(F32)
         outs[step][...] = part.astype(outs[step].dtype)
         if factors:
-            product = part * factors[step][...].astype(F32)
-            across = jnp.sum(product, axis=1, keepdims=True)
-            sums[0][step * unit : (step + 1) * unit, :] = jnp.broadcast_to(across, (unit, sums[0].shape[1]))
-            step_down = jnp.sum(product, axis=0, keepdims=True)
+            step_down = jnp.sum(part * factors[step][...].astype(F32), axis=0, keepdims=True)
             down = step_down if down is None else down + step_down
     if factors:
-        sums[1][...] = down
+        refs[-1][...] = down
 
 
 def owner(place, own, got, count, factors=()):
@@ -220,7 +216,7 @@
     unit = total // count
     outs = [jax.ShapeDtypeStruct((unit, features), F32 if step == 0 else BF16) for step in range(count)]
     if factors:
-        outs += [jax.ShapeDtypeStruct((total, 128), F32), jax.ShapeDtypeStruct((1, features), F32)]
+        outs += [jax.ShapeDtypeStruct((1, features), F32)]
     return pl.pallas_call(
         functools.partial(owner_kernel, count),
         in_specs=[IN_SMEM] + [IN_VMEM] * (2 + len(factors)),
@@ -240,7 +236,7 @@
 
 
 def activate_kernel(*refs):
-    pair, one, (hidden_ref, grads_ref) = refs[:5], refs[5:10], refs[10:]
+    pair, one, (hidden_ref, grads_ref, sums_ref, held_ref) = refs[:5], refs[5:10], refs[10:]
     half = pair[3].shape[1]
     for second in (False, True):
         at = half if second else 0
@@ -251,10 +247,26 @@
             first, last = (first_y, last_x) if second else (first_x, last_y)
             return own[lead, rows].astype(F32) + first[lead, half:].astype(F32) + last[lead].astype(F32)
 
-        results = activation(summed(pair, 0), summed(pair, 1), summed(one, 0))
-        hidden_ref[0, rows] = results[0].astype(BF16)
-        grads_ref[0, rows] = results[1].astype(BF16)
-        grads_ref[1, rows] = results[2].astype(BF16)
+        gate, up_value = summed(pair, 0), summed(pair, 1)
+        hidden, *grads = activation(gate, up_value, summed(one, 0))
+        hidden_ref[0, rows] = hidden.astype(BF16)
+        products = 0.0
+        for lead, (grad, value) in enumerate(zip(grads, (gate, up_value))):
+            rounded = grad.astype(BF16)
+            grads_ref[lead, rows] = rounded
+            products = products + rounded.astype(F32) * value
+
+        @pl.when(pl.program_id(0) == 0)
+        def _():
+            held_ref[rows] = products
+
+        @pl.when(pl.program_id(0) > 0)
+        def _():
+            held_ref[rows] = held_ref[rows] + products
+
+    @pl.when(pl.program_id(0) == pl.num_programs(0) - 1)
+    def _():
+        sums_ref[...] = jnp.broadcast_to(jnp.sum(held_ref[...], axis=1, keepdims=True), sums_ref.shape)
 
 
 def activate(pair, one):
@@ -266,8 +278,9 @@
         activate_kernel,
         grid=(units // edge,),
         in_specs=[spec(array) for array in pair + one],
-        out_specs=[spec(array) for array in outs],
-        out_shape=outs,
+        out_specs=[spec(array) for array in outs] + [pl.BlockSpec((share, BLOCK), lambda j: (0, 0))],
+        out_shape=outs + [jax.ShapeDtypeStruct((share, BLOCK), F32)],
+        scratch_shapes=[pltpu.VMEM((share, edge), F32)],
         compiler_params=kernel_params(1),
     )(*pair, *one)
 
@@ -385,7 +398,7 @@
     pair_x, pair_y = sum_first(*pair_parts[:2])
     one_last = sum_last(*sum_middle(*one_keep[:2], one_x, one_y))
     pair_last = sum_last(*sum_middle(*pair_parts[2:4], pair_x, pair_y))
-    hidden_share, grads_share = activate(
+    hidden_share, grads_share, inner_share = activate(
         [pair_parts[4], pair_x, pair_y, *pair_last], [one_keep[2], one_x, one_y, *one_last]
     )
 
@@ -397,7 +410,11 @@
     hidden, branch_own, branch_other = contract(
         [hidden_share, hidden_x, hidden_y, *hidden_last], [down_weight], [down_mask], last_plan, (F32, BF16), True, 10
     )
-    grads_x, grads_y, branch_own, branch_other = ordered(grads_x, grads_y, branch_own, branch_other)
+    inner_share, branch_own = ordered(inner_share, branch_own)
+    inner = inner_share[:unit] + core_swap(inner_share[unit:])
+    to_owner = [(r * cols + z, r * cols + (z ^ r)) for r in range(rows) for z in range(cols)]
+    inner = lax.ppermute(inner, ("row", "col"), to_owner)
+    grads_x, grads_y, branch_own, branch_other, inner = ordered(grads_x, grads_y, branch_own, branch_other, inner)
     branch_got = core_swap(branch_other)
     grads_middle = gather_middle(grads_x, grads_y)
     grads_last = gather_last(*grads_middle)
@@ -412,27 +429,24 @@
     )
     branch_far, normed_mine, normed_theirs = ordered(branch_far, normed_mine, normed_theirs)
 
-    kept, *parts, across, down_sum = owner(place_arg, normed_mine, core_swap(normed_theirs), cols, normed_own)
-    grads, parts, across, down_sum = ordered(grads, parts, across, down_sum)
+    kept, *parts, down_sum = owner(place_arg, normed_mine, core_swap(normed_theirs), cols, normed_own)
+    grads, parts, down_sum, inner = ordered(grads, parts, down_sum, inner)
     far = level_swaps(parts)
-    across_x = across + row_swap(across, 1)
-    down_both = down_sum + core_swap(down_sum)
-    across_x, down_both, grads = ordered(across_x, down_both, grads)
-    across_row = across_x + row_swap(across_x, 2)
-    sums = [
-        jnp.concatenate([across_row[step * unit : (step + 1) * unit], down_both.reshape(-1, 128)])
-        for step in range(cols)
-    ]
-    grads, sums = ordered(grads, sums)
-    sums_far = level_swaps(sums[1:])
+    down_pair = down_sum + swap(down_sum, "col", cols, 1)
+    inner_pair = inner + row_swap(inner, 1)
+    grads, down_pair, inner_pair = ordered(grads, down_pair, inner_pair)
+    down_got = swap(down_pair, "col", cols, 2)
+    inner_got = row_swap(inner_pair, 2)
     grad_gate, grad_up = outer(seen_rows, grads, [gate_groups, up_groups])
-    far, sums_far, grad_gate, grad_up = ordered(far, sums_far, grad_gate, grad_up)
-    sums_total = balanced(sums[0], sums_far)
+    far, down_got, inner_got, grad_gate, grad_up = ordered(far, down_got, inner_got, grad_gate, grad_up)
+    inner = inner_pair + inner_got
+    down_levels = down_pair + down_got
+    down_total = down_levels + core_swap(down_levels)
     branch = owner_total(branch_kept, branch_far).astype(BF16)
     normed_grad = owner_total(kept, far)
-    grad_gain = sums_total[unit:].reshape(features) / norm_gain
+    grad_gain = down_total.reshape(features) / norm_gain
     grad_tokens = (
-        inv_rms * norm_gain * normed_grad - token_f * inv_rms * inv_rms * sums_total[:unit, :1] / (features * rows)
+        inv_rms * norm_gain * normed_grad - token_f * inv_rms * inv_rms * inner[:, :1] / (features * rows)
     )
     return (branch, grad_tokens, grad_gain, grad_gate, grad_up, grad_down)
 

time: 173 us -> 169 us (0.977)
  waiting for transfers between devices: 63.1 us -> 57.9 us
    ppermute x46, waiting for transfers between devices: 63.1 us -> 57.9 us  [swap(): return lax.ppermute(value, axis, [(i, i ^ step) for i in range(size)])]
  transfers between devices with their start and end apart: 46 -> 47, of which waited for: 20 -> 19; matrix products, arithmetic and copies ran while one was open for 3% -> 3% of each run, Pallas kernels for 23% -> 24%
where the time goes in v4:
time: 169 us; the launch traced here: 168 us
  waiting for transfers between devices  57.9 us (34%)
  starting transfers between devices  49.2 us (29%)
  Pallas kernels  43.5 us (26%)
  local copies, waits for them, and re-layouts  9.77 us (6%)
  other arithmetic  7 us (4%)
    ppermute x46, waiting for transfers between devices, swap(): return lax.ppermute(value, axis, [(i, i ^ step) for i in range(size)])  57.9 us
    ppermute x46, starting transfers between devices, swap(): return lax.ppermute(value, axis, [(i, i ^ step) for i in range(size)])  48.3 us
    pallas_call x2, Pallas kernels, outer(): pl.pallas_call(outer_kernel, grid=(rows // edge,), in_specs=[IN_VMEM, IN_...  19.6 us
    pallas_call x2, Pallas kernels, project(): pl.pallas_call(functools.partial(project_kernel, ring, plan, by_unit, amo...  11 us
    unnamed x20, local copies, waits for them, and re-layouts  9.3 us
    pallas_call x2, Pallas kernels, contract(): pl.pallas_call(functools.partial(contract_kernel, pieces, plan, by_unit,...  8.91 us
  transfers between devices with their start and end apart: 47, of which 19 were waited for; matrix products, arithmetic and copies ran while one was open for 3% of the time, Pallas kernels for 24%

profile of v4, /device:TPU:0, one launch (start us, length us, event | category | flops | bytes accessed | tf_op | source)
XLA Modules:
  0.0 168.4 jit_solution(277858908229356923)
XLA Ops:
  1.7 3.0 %collective-permute-start.4 = (f32[48]{0:T(128)S(1)}, f32[48]{0:T(128)S(1)}, u32[]{:S(2)}, u32[]{:S(2)}) collective-permute-start(f32[48]{0:T(128)S(1)} %fusion.6), channel_id=1, source_target_pairs={{0,4},{4,0},{8,12},{12,8},{1,5},{5,1},{9,13},{13,9},{2,6},{6,2},{1... | collective-permute-start | bytes 584 | tf_op jit(solution)/shard_map/ppermute | solution.py:26
  4.7 3.6 %collective-permute-start.2 = (bf16[48,2048]{1,0:T(8,128)(2,1)}, bf16[48,2048]{1,0:T(8,128)(2,1)S(1)}, u32[]{:S(2)}, u32[]{:S(2)}) collective-permute-start(bf16[48,2048]{1,0:T(8,128)(2,1)} %refs_0_.3), channel_id=1, source_target_pairs={{0,3},{1,2},{2,1},{3,0},{4,7},{5,6},{6,5},{7,4},{8,11},{9,10},{10,... | collective-permute-start | bytes 589832 | tf_op jit(solution)/shard_map/ppermute | solution.py:26
  15.0 3.1 %copy-done = bf16[2048,1792]{1,0:T(8,128)(2,1)S(1)} copy-done((bf16[2048,1792]{1,0:T(8,128)(2,1)S(1)}, bf16[2048,1792]{1,0:T(8,128)(2,1)}, u32[]{:S(2)}) %copy-start) | copy-done | bytes 7340056
  18.1 3.1 %copy-done.2 = bf16[2048,1792]{1,0:T(8,128)(2,1)S(1)} copy-done((bf16[2048,1792]{1,0:T(8,128)(2,1)S(1)}, bf16[2048,1792]{1,0:T(8,128)(2,1)}, u32[]{:S(2)}) %copy-start.2) | copy-done | bytes 7340056
  21.2 3.1 %copy-done.4 = bf16[1792,2048]{1,0:T(8,128)(2,1)S(1)} copy-done((bf16[1792,2048]{1,0:T(8,128)(2,1)S(1)}, bf16[1792,2048]{1,0:T(8,128)(2,1)}, u32[]{:S(2)}) %copy-start.4) | copy-done | bytes 7340056
  26.0 3.6 %collective-permute-start.14 = (bf16[48,2048]{1,0:T(8,128)(2,1)S(1)}, bf16[48,2048]{1,0:T(8,128)(2,1)S(1)}, u32[]{:S(2)}, u32[]{:S(2)}) collective-permute-start(bf16[48,2048]{1,0:T(8,128)(2,1)S(1)} %fusion.2.refs_0_), channel_id=1, source_target_pairs={{0,3},{1,2},{2,1},{3,0},{4,7},{5,6},{6,5},{7,4},{8,11},{9,10},{10,... | collective-permute-start | bytes 589832 | tf_op jit(solution)/shard_map/ppermute | solution.py:26
  30.4 4.2 %shard_map.137 = (bf16[384,2048]{1,0:T(8,128)(2,1)S(1)}, bf16[1,96,1792]{2,1,0:T(8,128)(2,1)S(1)}, bf16[1,96,1792]{2,1,0:T(8,128)(2,1)S(1)}, bf16[1,48,1792]{2,1...) custom-call(s32[1]{0:T(128)} %shard_map.136.place_ref, ...), custom_call_target="tpu_custom_call" | custom-call | tf_op jit(solution)/shard_map/pallas_call | solution.py:109
  36.7 9.5 %collective-permute-done.13.refs_2_ = bf16[48,2048]{1,0:T(8,128)(2,1)S(1)} collective-permute-done((bf16[48,2048]{1,0:T(8,128)(2,1)S(1)}, bf16[48,2048]{1,0:T(8,128)(2,1)S(1)}, u32[]{:S(2)}, u32[]{:S(2)}) %collective-permute-start.13) | collective-permute-done | bytes 196640 | tf_op jit(solution)/shard_map/ppermute | solution.py:26
  48.2 6.9 %shard_map.138 = (bf16[384,2048]{1,0:T(8,128)(2,1)S(1)}, bf16[2,96,1792]{2,1,0:T(8,128)(2,1)S(1)}, bf16[2,96,1792]{2,1,0:T(8,128)(2,1)S(1)}, bf16[2,48,1792]{2,1...) custom-call(s32[1]{0:T(128)} %shard_map.136.place_ref, ...), custom_call_target="tpu_custom_call" | custom-call | tf_op jit(solution)/shard_map/pallas_call | solution.py:109
  58.8 14.6 %collective-permute-done.18.refs_1_ = bf16[2,96,1792]{2,1,0:T(8,128)(2,1)S(1)} collective-permute-done((bf16[2,96,1792]{2,1,0:T(8,128)(2,1)S(1)}, bf16[2,96,1792]{2,1,0:T(8,128)(2,1)S(1)}, u32[]{:S(2)}, u32[]{:S(2)}) %collective-permute-start.18) | collective-permute-done | bytes 688160 | tf_op jit(solution)/shard_map/ppermute | solution.py:26
  77.1 10.2 %collective-permute-done.22.refs_8_ = bf16[1,48,1792]{2,1,0:T(8,128)(2,1)S(1)} collective-permute-done((bf16[1,48,1792]{2,1,0:T(8,128)(2,1)S(1)}, bf16[1,48,1792]{2,1,0:T(8,128)(2,1)S(1)}, u32[]{:S(2)}, u32[]{:S(2)}) %collective-permute-start.22) | collective-permute-done | bytes 172064 | tf_op jit(solution)/shard_map/ppermute | solution.py:26
  91.1 5.7 %collective-permute-done.25.refs_2_ = bf16[1,96,1792]{2,1,0:T(8,128)(2,1)S(1)} collective-permute-done((bf16[1,96,1792]{2,1,0:T(8,128)(2,1)S(1)}, bf16[1,96,1792]{2,1,0:T(8,128)(2,1)S(1)}, u32[]{:S(2)}, u32[]{:S(2)}) %collective-permute-start.25) | collective-permute-done | bytes 344096 | tf_op jit(solution)/shard_map/ppermute | solution.py:26
  102.8 3.3 %collective-permute-done.28.refs_3_ = bf16[1,48,1792]{2,1,0:T(8,128)(2,1)S(1)} collective-permute-done((bf16[1,48,1792]{2,1,0:T(8,128)(2,1)S(1)}, bf16[1,48,1792]{2,1,0:T(8,128)(2,1)S(1)}, u32[]{:S(2)}, u32[]{:S(2)}) %collective-permute-start.28) | collective-permute-done | bytes 172064 | tf_op jit(solution)/shard_map/ppermute | solution.py:26
  106.3 3.0 %shard_map.140 = (bf16[1,384,1792]{2,1,0:T(8,128)(2,1)S(1)}, f32[192,2048]{1,0:T(8,128)S(1)}, bf16[192,2048]{1,0:T(8,128)(2,1)S(1)}) custom-call(bf16[1,96,1792]{2,1,0:T(8,128)(2,1)S(1)} %get-tuple-element.159.refs_0_, bf16[1,96,1792]{2,1,0:T(8,128)(2,1)S(1)} %collective-permute-done.24.refs_1_, bf16[1,96,1792]{2,1,0:T(8,128)(2,1)S(1)} %collective-permute-done.25.refs_2_, ...), custom_call_target="tpu_custom_call" | custom-call | flops 28185722880 | bytes 73400320 | tf_op jit(solution)/shard_map/pallas_call | solution.py:155
  111.5 4.5 %collective-permute-done.27.refs_2_ = bf16[2,96,1792]{2,1,0:T(8,128)(2,1)S(1)} collective-permute-done((bf16[2,96,1792]{2,1,0:T(8,128)(2,1)S(1)}, bf16[2,96,1792]{2,1,0:T(8,128)(2,1)S(1)}, u32[]{:S(2)}, u32[]{:S(2)}) %collective-permute-start.27) | collective-permute-done | bytes 688160 | tf_op jit(solution)/shard_map/ppermute | solution.py:26
  118.2 2.3 %collective-permute-start.37 = (bf16[2,48,1792]{2,1,0:T(8,128)(2,1)S(1)}, bf16[2,48,1792]{2,1,0:T(8,128)(2,1)S(1)}, u32[]{:S(2)}, u32[]{:S(2)}) collective-permute-start(bf16[2,48,1792]{2,1,0:T(8,128)(2,1)S(1)} %slice.42), channel_id=1, source_target_pairs={{0,8},{4,12},{8,0},{12,4},{1,9},{5,13},{9,1},{13,5},{2,10},{6,14},... | collective-permute-start | bytes 1032200 | tf_op jit(solution)/shard_map/ppermute | solution.py:26
  121.4 2.9 %collective-permute-start.34 = (bf16[48,2048]{1,0:T(8,128)(2,1)S(1)}, bf16[48,2048]{1,0:T(8,128)(2,1)S(1)}, u32[]{:S(2)}, u32[]{:S(2)}) collective-permute-start(bf16[48,2048]{1,0:T(8,128)(2,1)S(1)} %get-tuple-element.178), channel_id=1, source_target_pairs={{0,2},{1,3},{2,0},{3,1},{4,6},{5,7},{6,4},{7,5},{8,10},{9,11},{10,... | collective-permute-start | bytes 589832 | tf_op jit(solution)/shard_map/ppermute | solution.py:26
  125.7 8.2 %shard_map.142 = f32[1792,2048]{1,0:T(8,128)} custom-call(bf16[384,1792]{1,0:T(8,128)(2,1)S(1)} %bitcast.14, bf16[1,384,2048]{2,1,0:T(8,128)(2,1)S(1)} %bitcast.13, bf16[7,2,2048]{2,1,0:T(2,128)(2,1)S(1)} %convert_element_type.112.refs_0_), custom_call_target="tpu_custom_call" | custom-call | tf_op jit(solution)/shard_map/pallas_call | solution.py:184
  134.0 5.9 %shard_map.143 = (bf16[2,384,1792]{2,1,0:T(8,128)(2,1)S(1)}, f32[192,2048]{1,0:T(8,128)S(1)}, bf16[192,2048]{1,0:T(8,128)(2,1)S(1)}) custom-call(bf16[2,96,1792]{2,1,0:T(8,128)(2,1)S(1)} %get-tuple-element.162.refs_0_, bf16[2,96,1792]{2,1,0:T(8,128)(2,1)S(1)} %collective-permute-done.26.refs_1_, bf16[2,96,1792]{2,1,0:T(8,128)(2,1)S(1)} %collective-permute-done.27.refs_2_, ...), custom_call_target="tpu_custom_call" | custom-call | tf_op jit(solution)/shard_map/pallas_call | solution.py:155
  140.0 2.3 %collective-permute-done.38.got_ref = bf16[192,2048]{1,0:T(8,128)(2,1)S(1)} collective-permute-done((bf16[192,2048]{1,0:T(8,128)(2,1)S(1)}, bf16[192,2048]{1,0:T(8,128)(2,1)S(1)}, u32[]{:S(2)}, u32[]{:S(2)}) %collective-permute-start.38) | collective-permute-done | bytes 786464 | tf_op jit(solution)/shard_map/ppermute | solution.py:26
  143.4 2.6 %collective-permute-start.42 = (f32[1,2048]{1,0:T(1,128)S(1)}, f32[1,2048]{1,0:T(1,128)S(1)}, u32[]{:S(2)}, u32[]{:S(2)}) collective-permute-start(f32[1,2048]{1,0:T(1,128)S(1)} %get-tuple-element.208), channel_id=1, source_target_pairs={{0,1},{1,0},{2,3},{3,2},{4,5},{5,4},{6,7},{7,6},{8,9},{9,8},{10,11... | collective-permute-start | bytes 24584 | tf_op jit(solution)/shard_map/ppermute | solution.py:26
  146.1 2.9 %collective-permute-start.40 = (bf16[48,2048]{1,0:T(8,128)(2,1)S(1)}, bf16[48,2048]{1,0:T(8,128)(2,1)S(1)}, u32[]{:S(2)}, u32[]{:S(2)}) collective-permute-start(bf16[48,2048]{1,0:T(8,128)(2,1)S(1)} %get-tuple-element.205), channel_id=1, source_target_pairs={{0,2},{1,3},{2,0},{3,1},{4,6},{5,7},{6,4},{7,5},{8,10},{9,11},{10,... | collective-permute-start | bytes 589832 | tf_op jit(solution)/shard_map/ppermute | solution.py:26
  150.8 2.0 %collective-permute-start.45 = (f32[48,128]{1,0:T(8,128)S(1)}, f32[48,128]{1,0:T(8,128)S(1)}, u32[]{:S(2)}, u32[]{:S(2)}) collective-permute-start(f32[48,128]{1,0:T(8,128)S(1)} %add.74), channel_id=1, source_target_pairs={{0,8},{4,12},{8,0},{12,4},{1,9},{5,13},{9,1},{13,5},{2,10},{6,14},... | collective-permute-start | bytes 73736 | tf_op jit(solution)/shard_map/ppermute | solution.py:26
  153.5 11.4 %shard_map.145 = (f32[2048,1792]{1,0:T(8,128)}, f32[2048,1792]{1,0:T(8,128)}) custom-call(bf16[384,2048]{1,0:T(8,128)(2,1)S(1)} %get-tuple-element.212.left_ref, bf16[2,384,1792]{2,1,0:T(8,128)(2,1)S(1)} %get-tuple-element.213.right_ref, bf16[8,2,1792]{2,1,0:T(2,128)(2,1)S(1)} %convert_element_type.110.refs_0_, ...), custom_call_target="tpu_custom_call" | custom-call | tf_op jit(solution)/shard_map/pallas_call | solution.py:184
  (132 shorter events, 45.8 us)
Async XLA Ops:
  4.7 20.1 %collective-permute-start.2 = (bf16[48,2048]{1,0:T(8,128)(2,1)}, bf16[48,2048]{1,0:T(8,128)(2,1)S(1)}, u32[]{:S(2)}, u32[]{:S(2)}) collective-permute-start(bf16[48,2048]{1,0:T(8,128)(2,1)} %refs_0_.3), channel_id=1, source_target_pairs={{0,3},{1,2},{2,1},{3,0},{4,7},{5,6},{6,5},{7,4},{8,11},{9,10},{10,... | collective-permute-start | bytes 589832 | tf_op jit(solution)/shard_map/ppermute | solution.py:26
  8.3 16.6 %collective-permute-start.1 = (bf16[48,2048]{1,0:T(8,128)(2,1)}, bf16[48,2048]{1,0:T(8,128)(2,1)S(1)}, u32[]{:S(2)}, u32[]{:S(2)}) collective-permute-start(bf16[48,2048]{1,0:T(8,128)(2,1)} %refs_0_.3), channel_id=1, source_target_pairs={{0,2},{1,3},{2,0},{3,1},{4,6},{5,7},{6,4},{7,5},{8,10},{9,11},{10,... | collective-permute-start | bytes 589832 | tf_op jit(solution)/shard_map/ppermute | solution.py:26
  8.3 16.6 %collective-permute-start = (bf16[48,2048]{1,0:T(8,128)(2,1)}, bf16[48,2048]{1,0:T(8,128)(2,1)S(1)}, u32[]{:S(2)}, u32[]{:S(2)}) collective-permute-start(bf16[48,2048]{1,0:T(8,128)(2,1)} %refs_0_.3), channel_id=1, source_target_pairs={{0,1},{1,0},{2,3},{3,2},{4,5},{5,4},{6,7},{7,6},{8,9},{9,8},{10,11... | collective-permute-start | bytes 589832 | tf_op jit(solution)/shard_map/ppermute | solution.py:26
  9.1 15.8 %collective-permute-start.3 = (bf16[48,2048]{1,0:T(8,128)(2,1)}, bf16[48,2048]{1,0:T(8,128)(2,1)S(1)}, u32[]{:S(2)}, u32[]{:S(2)}) collective-permute-start(bf16[48,2048]{1,0:T(8,128)(2,1)} %refs_0_.3), channel_id=1, source_target_pairs={{0,16},{16,0},{1,17},{17,1},{2,18},{18,2},{3,19},{19,3},{4,20},{20... | collective-permute-start | bytes 589832 | tf_op jit(solution)/shard_map/ppermute | solution.py:26
  29.6 16.6 %collective-permute-start.13 = (bf16[48,2048]{1,0:T(8,128)(2,1)S(1)}, bf16[48,2048]{1,0:T(8,128)(2,1)S(1)}, u32[]{:S(2)}, u32[]{:S(2)}) collective-permute-start(bf16[48,2048]{1,0:T(8,128)(2,1)S(1)} %fusion.2.refs_0_), channel_id=1, source_target_pairs={{0,2},{1,3},{2,0},{3,1},{4,6},{5,7},{6,4},{7,5},{8,10},{9,11},{10,... | collective-permute-start | bytes 589832 | tf_op jit(solution)/shard_map/ppermute | solution.py:26
  29.6 16.6 %collective-permute-start.12 = (bf16[48,2048]{1,0:T(8,128)(2,1)S(1)}, bf16[48,2048]{1,0:T(8,128)(2,1)S(1)}, u32[]{:S(2)}, u32[]{:S(2)}) collective-permute-start(bf16[48,2048]{1,0:T(8,128)(2,1)S(1)} %fusion.2.refs_0_), channel_id=1, source_target_pairs={{0,1},{1,0},{2,3},{3,2},{4,5},{5,4},{6,7},{7,6},{8,9},{9,8},{10,11... | collective-permute-start | bytes 589832 | tf_op jit(solution)/shard_map/ppermute | solution.py:26
  34.5 20.5 %collective-permute-start.10 = (bf16[1,96,1792]{2,1,0:T(8,128)(2,1)S(1)}, bf16[1,96,1792]{2,1,0:T(8,128)(2,1)S(1)}, u32[]{:S(2)}, u32[]{:S(2)}) collective-permute-start(bf16[1,96,1792]{2,1,0:T(8,128)(2,1)S(1)} %get-tuple-element.123), channel_id=1, source_target_pairs={{0,4},{4,0},{8,12},{12,8},{1,5},{5,1},{9,13},{13,9},{2,6},{6,2},{1... | collective-permute-start | bytes 1032200 | tf_op jit(solution)/shard_map/ppermute | solution.py:26
  34.9 20.1 %collective-permute-start.11 = (bf16[1,96,1792]{2,1,0:T(8,128)(2,1)S(1)}, bf16[1,96,1792]{2,1,0:T(8,128)(2,1)S(1)}, u32[]{:S(2)}, u32[]{:S(2)}) collective-permute-start(bf16[1,96,1792]{2,1,0:T(8,128)(2,1)S(1)} %get-tuple-element.124), channel_id=1, source_target_pairs={{0,8},{4,12},{8,0},{12,4},{1,9},{5,13},{9,1},{13,5},{2,10},{6,14},... | collective-permute-start | bytes 1032200 | tf_op jit(solution)/shard_map/ppermute | solution.py:26
  55.1 18.3 %collective-permute-start.18 = (bf16[2,96,1792]{2,1,0:T(8,128)(2,1)S(1)}, bf16[2,96,1792]{2,1,0:T(8,128)(2,1)S(1)}, u32[]{:S(2)}, u32[]{:S(2)}) collective-permute-start(bf16[2,96,1792]{2,1,0:T(8,128)(2,1)S(1)} %get-tuple-element.143), channel_id=1, source_target_pairs={{0,4},{4,0},{8,12},{12,8},{1,5},{5,1},{9,13},{13,9},{2,6},{6,2},{1... | collective-permute-start | bytes 2064392 | tf_op jit(solution)/shard_map/ppermute | solution.py:26
  55.7 17.7 %collective-permute-start.19 = (bf16[2,96,1792]{2,1,0:T(8,128)(2,1)S(1)}, bf16[2,96,1792]{2,1,0:T(8,128)(2,1)S(1)}, u32[]{:S(2)}, u32[]{:S(2)}) collective-permute-start(bf16[2,96,1792]{2,1,0:T(8,128)(2,1)S(1)} %get-tuple-element.144), channel_id=1, source_target_pairs={{0,8},{4,12},{8,0},{12,4},{1,9},{5,13},{9,1},{13,5},{2,10},{6,14},... | collective-permute-start | bytes 2064392 | tf_op jit(solution)/shard_map/ppermute | solution.py:26
  57.2 19.8 %collective-permute-start.23 = (bf16[1,48,1792]{2,1,0:T(8,128)(2,1)S(1)}, bf16[1,48,1792]{2,1,0:T(8,128)(2,1)S(1)}, u32[]{:S(2)}, u32[]{:S(2)}) collective-permute-start(bf16[1,48,1792]{2,1,0:T(8,128)(2,1)S(1)} %add_convert_fusion.3), channel_id=1, source_target_pairs={{0,4},{4,0},{8,12},{12,8},{1,5},{5,1},{9,13},{13,9},{2,6},{6,2},{1... | collective-permute-start | bytes 516104 | tf_op jit(solution)/shard_map/ppermute | solution.py:26
  73.5 13.7 %collective-permute-start.21 = (bf16[2,48,1792]{2,1,0:T(8,128)(2,1)S(1)}, bf16[2,48,1792]{2,1,0:T(8,128)(2,1)S(1)}, u32[]{:S(2)}, u32[]{:S(2)}) collective-permute-start(bf16[2,48,1792]{2,1,0:T(8,128)(2,1)S(1)} %add_convert_fusion), channel_id=1, source_target_pairs={{0,4},{4,0},{8,12},{12,8},{1,5},{5,1},{9,13},{13,9},{2,6},{6,2},{1... | collective-permute-start | bytes 1032200 | tf_op jit(solution)/shard_map/ppermute | solution.py:26
  99.5 16.5 %collective-permute-start.27 = (bf16[2,96,1792]{2,1,0:T(8,128)(2,1)S(1)}, bf16[2,96,1792]{2,1,0:T(8,128)(2,1)S(1)}, u32[]{:S(2)}, u32[]{:S(2)}) collective-permute-start(bf16[2,96,1792]{2,1,0:T(8,128)(2,1)S(1)} %get-tuple-element.162.refs_0_), channel_id=1, source_target_pairs={{0,8},{4,12},{8,0},{12,4},{1,9},{5,13},{9,1},{13,5},{2,10},{6,14},... | collective-permute-start | bytes 2064392 | tf_op jit(solution)/shard_map/ppermute | solution.py:26
  101.1 15.5 %collective-permute-start.26 = (bf16[2,96,1792]{2,1,0:T(8,128)(2,1)S(1)}, bf16[2,96,1792]{2,1,0:T(8,128)(2,1)S(1)}, u32[]{:S(2)}, u32[]{:S(2)}) collective-permute-start(bf16[2,96,1792]{2,1,0:T(8,128)(2,1)S(1)} %get-tuple-element.162.refs_0_), channel_id=1, source_target_pairs={{0,4},{4,0},{8,12},{12,8},{1,5},{5,1},{9,13},{13,9},{2,6},{6,2},{1... | collective-permute-start | bytes 2064392 | tf_op jit(solution)/shard_map/ppermute | solution.py:26
  116.6 17.3 %collective-permute-start.36 = (bf16[2,48,1792]{2,1,0:T(8,128)(2,1)S(1)}, bf16[2,48,1792]{2,1,0:T(8,128)(2,1)S(1)}, u32[]{:S(2)}, u32[]{:S(2)}) collective-permute-start(bf16[2,48,1792]{2,1,0:T(8,128)(2,1)S(1)} %slice.41), channel_id=1, source_target_pairs={{0,4},{4,0},{8,12},{12,8},{1,5},{5,1},{9,13},{13,9},{2,6},{6,2},{1... | collective-permute-start | bytes 1032200 | tf_op jit(solution)/shard_map/ppermute | solution.py:26
  118.2 15.7 %collective-permute-start.37 = (bf16[2,48,1792]{2,1,0:T(8,128)(2,1)S(1)}, bf16[2,48,1792]{2,1,0:T(8,128)(2,1)S(1)}, u32[]{:S(2)}, u32[]{:S(2)}) collective-permute-start(bf16[2,48,1792]{2,1,0:T(8,128)(2,1)S(1)} %slice.42), channel_id=1, source_target_pairs={{0,8},{4,12},{8,0},{12,4},{1,9},{5,13},{9,1},{13,5},{2,10},{6,14},... | collective-permute-start | bytes 1032200 | tf_op jit(solution)/shard_map/ppermute | solution.py:26
  121.3 18.6 %collective-permute-start.33 = (bf16[48,2048]{1,0:T(8,128)(2,1)S(1)}, bf16[48,2048]{1,0:T(8,128)(2,1)S(1)}, u32[]{:S(2)}, u32[]{:S(2)}) collective-permute-start(bf16[48,2048]{1,0:T(8,128)(2,1)S(1)} %get-tuple-element.177), channel_id=1, source_target_pairs={{0,1},{1,0},{2,3},{3,2},{4,5},{5,4},{6,7},{7,6},{8,9},{9,8},{10,11... | collective-permute-start | bytes 589832 | tf_op jit(solution)/shard_map/ppermute | solution.py:26
  121.4 18.5 %collective-permute-start.34 = (bf16[48,2048]{1,0:T(8,128)(2,1)S(1)}, bf16[48,2048]{1,0:T(8,128)(2,1)S(1)}, u32[]{:S(2)}, u32[]{:S(2)}) collective-permute-start(bf16[48,2048]{1,0:T(8,128)(2,1)S(1)} %get-tuple-element.178), channel_id=1, source_target_pairs={{0,2},{1,3},{2,0},{3,1},{4,6},{5,7},{6,4},{7,5},{8,10},{9,11},{10,... | collective-permute-start | bytes 589832 | tf_op jit(solution)/shard_map/ppermute | solution.py:26
  124.3 15.6 %collective-permute-start.35 = (bf16[48,2048]{1,0:T(8,128)(2,1)S(1)}, bf16[48,2048]{1,0:T(8,128)(2,1)S(1)}, u32[]{:S(2)}, u32[]{:S(2)}) collective-permute-start(bf16[48,2048]{1,0:T(8,128)(2,1)S(1)} %get-tuple-element.179), channel_id=1, source_target_pairs={{0,3},{1,2},{2,1},{3,0},{4,7},{5,6},{6,5},{7,4},{8,11},{9,10},{10,... | collective-permute-start | bytes 589832 | tf_op jit(solution)/shard_map/ppermute | solution.py:26
  146.0 20.4 %collective-permute-start.39 = (bf16[48,2048]{1,0:T(8,128)(2,1)S(1)}, bf16[48,2048]{1,0:T(8,128)(2,1)S(1)}, u32[]{:S(2)}, u32[]{:S(2)}) collective-permute-start(bf16[48,2048]{1,0:T(8,128)(2,1)S(1)} %get-tuple-element.204), channel_id=1, source_target_pairs={{0,1},{1,0},{2,3},{3,2},{4,5},{5,4},{6,7},{7,6},{8,9},{9,8},{10,11... | collective-permute-start | bytes 589832 | tf_op jit(solution)/shard_map/ppermute | solution.py:26
  146.1 20.4 %collective-permute-start.40 = (bf16[48,2048]{1,0:T(8,128)(2,1)S(1)}, bf16[48,2048]{1,0:T(8,128)(2,1)S(1)}, u32[]{:S(2)}, u32[]{:S(2)}) collective-permute-start(bf16[48,2048]{1,0:T(8,128)(2,1)S(1)} %get-tuple-element.205), channel_id=1, source_target_pairs={{0,2},{1,3},{2,0},{3,1},{4,6},{5,7},{6,4},{7,5},{8,10},{9,11},{10,... | collective-permute-start | bytes 589832 | tf_op jit(solution)/shard_map/ppermute | solution.py:26
  148.9 17.5 %collective-permute-start.41 = (bf16[48,2048]{1,0:T(8,128)(2,1)S(1)}, bf16[48,2048]{1,0:T(8,128)(2,1)S(1)}, u32[]{:S(2)}, u32[]{:S(2)}) collective-permute-start(bf16[48,2048]{1,0:T(8,128)(2,1)S(1)} %get-tuple-element.206), channel_id=1, source_target_pairs={{0,3},{1,2},{2,1},{3,0},{4,7},{5,6},{6,5},{7,4},{8,11},{9,10},{10,... | collective-permute-start | bytes 589832 | tf_op jit(solution)/shard_map/ppermute | solution.py:26
  150.5 16.0 %collective-permute-start.44 = (f32[1,2048]{1,0:T(1,128)S(1)}, f32[1,2048]{1,0:T(1,128)S(1)}, u32[]{:S(2)}, u32[]{:S(2)}) collective-permute-start(f32[1,2048]{1,0:T(1,128)S(1)} %add.73), channel_id=1, source_target_pairs={{0,2},{1,3},{2,0},{3,1},{4,6},{5,7},{6,4},{7,5},{8,10},{9,11},{10,... | collective-permute-start | bytes 24584 | tf_op jit(solution)/shard_map/ppermute | solution.py:26
  150.8 15.7 %collective-permute-start.45 = (f32[48,128]{1,0:T(8,128)S(1)}, f32[48,128]{1,0:T(8,128)S(1)}, u32[]{:S(2)}, u32[]{:S(2)}) collective-permute-start(f32[48,128]{1,0:T(8,128)S(1)} %add.74), channel_id=1, source_target_pairs={{0,8},{4,12},{8,0},{12,4},{1,9},{5,13},{9,1},{13,5},{2,10},{6,14},... | collective-permute-start | bytes 73736 | tf_op jit(solution)/shard_map/ppermute | solution.py:26
  (32 other events, 257.2 us)

commit v5 on v4

--- a/solution.py
+++ b/solution.py
@@ -236,19 +236,19 @@
 
 
 def activate_kernel(*refs):
-    pair, one, (hidden_ref, grads_ref, sums_ref, held_ref) = refs[:5], refs[5:10], refs[10:]
-    half = pair[3].shape[1]
+    gates, ups, ones, (hidden_ref, grads_ref, sums_ref, held_ref) = refs[:5], refs[5:10], refs[10:15], refs[15:]
+    half = gates[3].shape[1]
     for second in (False, True):
         at = half if second else 0
         rows = slice(at, at + half)
 
-        def summed(parts, lead):
+        def summed(parts):
             own, first_x, first_y, last_y, last_x = parts
             first, last = (first_y, last_x) if second else (first_x, last_y)
-            return own[lead, rows].astype(F32) + first[lead, half:].astype(F32) + last[lead].astype(F32)
-
-        gate, up_value = summed(pair, 0), summed(pair, 1)
-        hidden, *grads = activation(gate, up_value, summed(one, 0))
+            return own[0, rows].astype(F32) + first[0, half:].astype(F32) + last[0].astype(F32)
+
+        gate, up_value = summed(gates), summed(ups)
+        hidden, *grads = activation(gate, up_value, summed(ones))
         hidden_ref[0, rows] = hidden.astype(BF16)
         products = 0.0
         for lead, (grad, value) in enumerate(zip(grads, (gate, up_value))):
@@ -269,20 +269,20 @@
         sums_ref[...] = jnp.broadcast_to(jnp.sum(held_ref[...], axis=1, keepdims=True), sums_ref.shape)
 
 
-def activate(pair, one):
-    _, share, units = pair[0].shape
+def activate(gates, ups, ones):
+    _, share, units = gates[0].shape
     edge = block_edge(units)
     spec = lambda array: pl.BlockSpec(array.shape[:2] + (edge,), lambda j: (0, 0, j))
     outs = [jax.ShapeDtypeStruct((amount, share, units), BF16) for amount in (1, 2)]
     return pl.pallas_call(
         activate_kernel,
         grid=(units // edge,),
-        in_specs=[spec(array) for array in pair + one],
+        in_specs=[spec(array) for array in gates + ups + ones],
         out_specs=[spec(array) for array in outs] + [pl.BlockSpec((share, BLOCK), lambda j: (0, 0))],
         out_shape=outs + [jax.ShapeDtypeStruct((share, BLOCK), F32)],
         scratch_shapes=[pltpu.VMEM((share, edge), F32)],
         compiler_params=kernel_params(1),
-    )(*pair, *one)
+    )(*gates, *ups, *ones)
 
 
 def widen(keep):
@@ -393,13 +393,23 @@
     normed_own = [normed, *normed_far]
     normed_other = [normed_core] + [core_swap(part) for part in normed_far]
 
-    seen_rows, *pair_parts = project(place_arg, normed_own + normed_other, [gate_weight, up_weight], [gate_mask, up_mask], first_plan, False)
-    one_x, one_y, pair_parts = ordered(one_x, one_y, pair_parts)
-    pair_x, pair_y = sum_first(*pair_parts[:2])
-    one_last = sum_last(*sum_middle(*one_keep[:2], one_x, one_y))
-    pair_last = sum_last(*sum_middle(*pair_parts[2:4], pair_x, pair_y))
+    seen_rows, *gate_parts = project(
+        place_arg, normed_own + normed_other, [gate_weight], [gate_mask], first_plan, False
+    )
+    gate_x, gate_y = sum_first(*gate_parts[:2])
+    _, *up_parts = project(place_arg, [seen_rows], [up_weight], [up_mask], first_plan, False)
+    one_x, one_y, up_parts = ordered(one_x, one_y, up_parts)
+    up_x, up_y = sum_first(*up_parts[:2])
+    one_middle = sum_middle(*one_keep[:2], one_x, one_y)
+    gate_x, gate_y, up_parts, one_middle = ordered(gate_x, gate_y, up_parts, one_middle)
+    gate_last = sum_last(*sum_middle(*gate_parts[2:4], gate_x, gate_y))
+    up_x, up_y, one_middle = ordered(up_x, up_y, one_middle)
+    one_last = sum_last(*one_middle)
+    up_last = sum_last(*sum_middle(*up_parts[2:4], up_x, up_y))
     hidden_share, grads_share, inner_share = activate(
-        [pair_parts[4], pair_x, pair_y, *pair_last], [one_keep[2], one_x, one_y, *one_last]
+        [gate_parts[4], gate_x, gate_y, *gate_last],
+        [up_parts[4], up_x, up_y, *up_last],
+        [one_keep[2], one_x, one_y, *one_last],
     )
 
     hidden_x, hidden_y = gather_first(hidden_share)

time: 169 us -> 165 us (0.976)
  waiting for transfers between devices: 57.9 us -> 49.8 us
  starting transfers between devices: 49.2 us -> 52.2 us
    ppermute x46 -> x50, waiting for transfers between devices: 57.9 us -> 49.8 us  [swap(): return lax.ppermute(value, axis, [(i, i ^ step) for i in range(size)])]
    ppermute x46 -> x50, starting transfers between devices: 48.3 us -> 51.4 us  [swap(): return lax.ppermute(value, axis, [(i, i ^ step) for i in range(size)])]
    pallas_call x2 -> x3, Pallas kernels: 11 us -> 11.7 us  [project(): pl.pallas_call(functools.partial(project_kernel, ring, plan, by_unit, amo...]
    unnamed x20 -> x22, local copies, waits for them, and re-layouts: 9.3 us -> 9.3 us
  transfers between devices with their start and end apart: 47 -> 51, of which waited for: 19 -> 24; matrix products, arithmetic and copies ran while one was open for 3% -> 3% of each run, Pallas kernels for 24% -> 25%
where the time goes in v5:
time: 165 us; the launch traced here: 164 us
  starting transfers between devices  52.2 us (32%)
  waiting for transfers between devices  49.8 us (30%)
  Pallas kernels  44.3 us (27%)
  local copies, waits for them, and re-layouts  9.77 us (6%)
  other arithmetic  6.98 us (4%)
    ppermute x50, starting transfers between devices, swap(): return lax.ppermute(value, axis, [(i, i ^ step) for i in range(size)])  51.4 us
    ppermute x50, waiting for transfers between devices, swap(): return lax.ppermute(value, axis, [(i, i ^ step) for i in range(size)])  49.8 us
    pallas_call x2, Pallas kernels, outer(): pl.pallas_call(outer_kernel, grid=(rows // edge,), in_specs=[IN_VMEM, IN_...  19.6 us
    pallas_call x3, Pallas kernels, project(): pl.pallas_call(functools.partial(project_kernel, ring, plan, by_unit, amo...  11.7 us
    unnamed x22, local copies, waits for them, and re-layouts  9.3 us
    pallas_call x2, Pallas kernels, contract(): pl.pallas_call(functools.partial(contract_kernel, pieces, plan, by_unit,...  8.94 us
  transfers between devices with their start and end apart: 51, of which 24 were waited for; matrix products, arithmetic and copies ran while one was open for 3% of the time, Pallas kernels for 25%

profile of v5, /device:TPU:0, one launch (start us, length us, event | category | flops | bytes accessed | tf_op | source)
XLA Modules:
  0.0 164.2 jit_solution(15505390295864731085)
XLA Ops:
  1.7 3.0 %collective-permute-start.4 = (f32[48]{0:T(128)S(1)}, f32[48]{0:T(128)S(1)}, u32[]{:S(2)}, u32[]{:S(2)}) collective-permute-start(f32[48]{0:T(128)S(1)} %fusion.6), channel_id=1, source_target_pairs={{0,4},{4,0},{8,12},{12,8},{1,5},{5,1},{9,13},{13,9},{2,6},{6,2},{1... | collective-permute-start | bytes 584 | tf_op jit(solution)/shard_map/ppermute | solution.py:26
  4.7 3.6 %collective-permute-start.2 = (bf16[48,2048]{1,0:T(8,128)(2,1)}, bf16[48,2048]{1,0:T(8,128)(2,1)S(1)}, u32[]{:S(2)}, u32[]{:S(2)}) collective-permute-start(bf16[48,2048]{1,0:T(8,128)(2,1)} %refs_0_.3), channel_id=1, source_target_pairs={{0,3},{1,2},{2,1},{3,0},{4,7},{5,6},{6,5},{7,4},{8,11},{9,10},{10,... | collective-permute-start | bytes 589832 | tf_op jit(solution)/shard_map/ppermute | solution.py:26
  15.0 3.1 %copy-done = bf16[2048,1792]{1,0:T(8,128)(2,1)S(1)} copy-done((bf16[2048,1792]{1,0:T(8,128)(2,1)S(1)}, bf16[2048,1792]{1,0:T(8,128)(2,1)}, u32[]{:S(2)}) %copy-start) | copy-done | bytes 7340056
  18.1 3.1 %copy-done.2 = bf16[2048,1792]{1,0:T(8,128)(2,1)S(1)} copy-done((bf16[2048,1792]{1,0:T(8,128)(2,1)S(1)}, bf16[2048,1792]{1,0:T(8,128)(2,1)}, u32[]{:S(2)}) %copy-start.2) | copy-done | bytes 7340056
  21.2 3.1 %copy-done.3 = bf16[1792,2048]{1,0:T(8,128)(2,1)S(1)} copy-done((bf16[1792,2048]{1,0:T(8,128)(2,1)S(1)}, bf16[1792,2048]{1,0:T(8,128)(2,1)}, u32[]{:S(2)}) %copy-start.3) | copy-done | bytes 7340056
  26.0 3.6 %collective-permute-start.9 = (bf16[48,2048]{1,0:T(8,128)(2,1)S(1)}, bf16[48,2048]{1,0:T(8,128)(2,1)S(1)}, u32[]{:S(2)}, u32[]{:S(2)}) collective-permute-start(bf16[48,2048]{1,0:T(8,128)(2,1)S(1)} %fusion.2.refs_0_), channel_id=1, source_target_pairs={{0,3},{1,2},{2,1},{3,0},{4,7},{5,6},{6,5},{7,4},{8,11},{9,10},{10,... | collective-permute-start | bytes 589832 | tf_op jit(solution)/shard_map/ppermute | solution.py:26
  30.4 3.9 %shard_map.137 = (bf16[384,2048]{1,0:T(8,128)(2,1)S(1)}, bf16[1,96,1792]{2,1,0:T(8,128)(2,1)S(1)}, bf16[1,96,1792]{2,1,0:T(8,128)(2,1)S(1)}, bf16[1,48,1792]{2,1...) custom-call(s32[1]{0:T(128)} %shard_map.136.place_ref, ...), custom_call_target="tpu_custom_call" | custom-call | tf_op jit(solution)/shard_map/pallas_call | solution.py:109
  36.4 9.8 %collective-permute-done.8.refs_2_ = bf16[48,2048]{1,0:T(8,128)(2,1)S(1)} collective-permute-done((bf16[48,2048]{1,0:T(8,128)(2,1)S(1)}, bf16[48,2048]{1,0:T(8,128)(2,1)S(1)}, u32[]{:S(2)}, u32[]{:S(2)}) %collective-permute-start.8) | collective-permute-done | bytes 196640 | tf_op jit(solution)/shard_map/ppermute | solution.py:26
  48.2 4.0 %shard_map.138 = (bf16[384,2048]{1,0:T(8,128)(2,1)S(1)}, bf16[1,96,1792]{2,1,0:T(8,128)(2,1)S(1)}, bf16[1,96,1792]{2,1,0:T(8,128)(2,1)S(1)}, bf16[1,48,1792]{2,1...) custom-call(s32[1]{0:T(128)} %shard_map.136.place_ref, ...), custom_call_target="tpu_custom_call" | custom-call | tf_op jit(solution)/shard_map/pallas_call | solution.py:109
  54.3 3.8 %shard_map.139 = (bf16[384,2048]{1,0:T(8,128)(2,1)}, bf16[1,96,1792]{2,1,0:T(8,128)(2,1)S(1)}, bf16[1,96,1792]{2,1,0:T(8,128)(2,1)S(1)}, bf16[1,48,1792]{2,1,0:T...) custom-call(s32[1]{0:T(128)} %shard_map.136.place_ref, ...), custom_call_target="tpu_custom_call" | custom-call | tf_op jit(solution)/shard_map/pallas_call | solution.py:109
  60.3 2.9 %collective-permute-done.16.refs_1_ = bf16[1,96,1792]{2,1,0:T(8,128)(2,1)S(1)} collective-permute-done((bf16[1,96,1792]{2,1,0:T(8,128)(2,1)S(1)}, bf16[1,96,1792]{2,1,0:T(8,128)(2,1)S(1)}, u32[]{:S(2)}, u32[]{:S(2)}) %collective-permute-start.16) | collective-permute-done | bytes 344096 | tf_op jit(solution)/shard_map/ppermute | solution.py:26
  67.0 3.6 %collective-permute-done.22.refs_6_ = bf16[1,96,1792]{2,1,0:T(8,128)(2,1)S(1)} collective-permute-done((bf16[1,96,1792]{2,1,0:T(8,128)(2,1)S(1)}, bf16[1,96,1792]{2,1,0:T(8,128)(2,1)S(1)}, u32[]{:S(2)}, u32[]{:S(2)}) %collective-permute-start.22) | collective-permute-done | bytes 344096 | tf_op jit(solution)/shard_map/ppermute | solution.py:26
  75.7 2.7 %collective-permute-done.26.refs_13_ = bf16[1,48,1792]{2,1,0:T(8,128)(2,1)S(1)} collective-permute-done((bf16[1,48,1792]{2,1,0:T(8,128)(2,1)S(1)}, bf16[1,48,1792]{2,1,0:T(8,128)(2,1)S(1)}, u32[]{:S(2)}, u32[]{:S(2)}) %collective-permute-start.26) | collective-permute-done | bytes 172064 | tf_op jit(solution)/shard_map/ppermute | solution.py:26
  86.1 6.0 %collective-permute-done.29.refs_2_ = bf16[1,96,1792]{2,1,0:T(8,128)(2,1)S(1)} collective-permute-done((bf16[1,96,1792]{2,1,0:T(8,128)(2,1)S(1)}, bf16[1,96,1792]{2,1,0:T(8,128)(2,1)S(1)}, u32[]{:S(2)}, u32[]{:S(2)}) %collective-permute-start.29) | collective-permute-done | bytes 344096 | tf_op jit(solution)/shard_map/ppermute | solution.py:26
  97.5 3.1 %collective-permute-done.32.refs_3_ = bf16[1,48,1792]{2,1,0:T(8,128)(2,1)S(1)} collective-permute-done((bf16[1,48,1792]{2,1,0:T(8,128)(2,1)S(1)}, bf16[1,48,1792]{2,1,0:T(8,128)(2,1)S(1)}, u32[]{:S(2)}, u32[]{:S(2)}) %collective-permute-start.32) | collective-permute-done | bytes 172064 | tf_op jit(solution)/shard_map/ppermute | solution.py:26
  102.3 3.0 %shard_map.141 = (bf16[1,384,1792]{2,1,0:T(8,128)(2,1)S(1)}, f32[192,2048]{1,0:T(8,128)S(1)}, bf16[192,2048]{1,0:T(8,128)(2,1)S(1)}) custom-call(bf16[1,96,1792]{2,1,0:T(8,128)(2,1)S(1)} %get-tuple-element.200.refs_0_, bf16[1,96,1792]{2,1,0:T(8,128)(2,1)S(1)} %collective-permute-done.28.refs_1_, bf16[1,96,1792]{2,1,0:T(8,128)(2,1)S(1)} %collective-permute-done.29.refs_2_, ...), custom_call_target="tpu_custom_call" | custom-call | flops 28185722880 | bytes 73400320 | tf_op jit(solution)/shard_map/pallas_call | solution.py:155
  107.5 6.1 %collective-permute-done.31.refs_2_ = bf16[2,96,1792]{2,1,0:T(8,128)(2,1)S(1)} collective-permute-done((bf16[2,96,1792]{2,1,0:T(8,128)(2,1)S(1)}, bf16[2,96,1792]{2,1,0:T(8,128)(2,1)S(1)}, u32[]{:S(2)}, u32[]{:S(2)}) %collective-permute-start.31) | collective-permute-done | bytes 688160 | tf_op jit(solution)/shard_map/ppermute | solution.py:26
  116.8 2.9 %collective-permute-start.38 = (bf16[48,2048]{1,0:T(8,128)(2,1)S(1)}, bf16[48,2048]{1,0:T(8,128)(2,1)S(1)}, u32[]{:S(2)}, u32[]{:S(2)}) collective-permute-start(bf16[48,2048]{1,0:T(8,128)(2,1)S(1)} %get-tuple-element.219), channel_id=1, source_target_pairs={{0,2},{1,3},{2,0},{3,1},{4,6},{5,7},{6,4},{7,5},{8,10},{9,11},{10,... | collective-permute-start | bytes 589832 | tf_op jit(solution)/shard_map/ppermute | solution.py:26
  121.1 8.2 %shard_map.143 = f32[1792,2048]{1,0:T(8,128)} custom-call(bf16[384,1792]{1,0:T(8,128)(2,1)S(1)} %bitcast.16, bf16[1,384,2048]{2,1,0:T(8,128)(2,1)S(1)} %bitcast.15, bf16[7,2,2048]{2,1,0:T(2,128)(2,1)S(1)} %convert_element_type.130.refs_0_), custom_call_target="tpu_custom_call" | custom-call | tf_op jit(solution)/shard_map/pallas_call | solution.py:184
  129.4 5.9 %shard_map.144 = (bf16[2,384,1792]{2,1,0:T(8,128)(2,1)S(1)}, f32[192,2048]{1,0:T(8,128)S(1)}, bf16[192,2048]{1,0:T(8,128)(2,1)S(1)}) custom-call(bf16[2,96,1792]{2,1,0:T(8,128)(2,1)S(1)} %get-tuple-element.203.refs_0_, bf16[2,96,1792]{2,1,0:T(8,128)(2,1)S(1)} %collective-permute-done.30.refs_1_, bf16[2,96,1792]{2,1,0:T(8,128)(2,1)S(1)} %collective-permute-done.31.refs_2_, ...), custom_call_target="tpu_custom_call" | custom-call | tf_op jit(solution)/shard_map/pallas_call | solution.py:155
  139.3 2.5 %collective-permute-start.46 = (f32[1,2048]{1,0:T(1,128)S(1)}, f32[1,2048]{1,0:T(1,128)S(1)}, u32[]{:S(2)}, u32[]{:S(2)}) collective-permute-start(f32[1,2048]{1,0:T(1,128)S(1)} %get-tuple-element.249), channel_id=1, source_target_pairs={{0,1},{1,0},{2,3},{3,2},{4,5},{5,4},{6,7},{7,6},{8,9},{9,8},{10,11... | collective-permute-start | bytes 24584 | tf_op jit(solution)/shard_map/ppermute | solution.py:26
  141.9 2.9 %collective-permute-start.44 = (bf16[48,2048]{1,0:T(8,128)(2,1)S(1)}, bf16[48,2048]{1,0:T(8,128)(2,1)S(1)}, u32[]{:S(2)}, u32[]{:S(2)}) collective-permute-start(bf16[48,2048]{1,0:T(8,128)(2,1)S(1)} %get-tuple-element.246), channel_id=1, source_target_pairs={{0,2},{1,3},{2,0},{3,1},{4,6},{5,7},{6,4},{7,5},{8,10},{9,11},{10,... | collective-permute-start | bytes 589832 | tf_op jit(solution)/shard_map/ppermute | solution.py:26
  148.5 11.4 %shard_map.146 = (f32[2048,1792]{1,0:T(8,128)}, f32[2048,1792]{1,0:T(8,128)}) custom-call(bf16[384,2048]{1,0:T(8,128)(2,1)S(1)} %get-tuple-element.161.refs_0_.left_ref, bf16[2,384,1792]{2,1,0:T(8,128)(2,1)S(1)} %get-tuple-element.253.right_ref, bf16[8,2,1792]{2,1,0:T(2,128)(2,1)S(1)} %convert_element_type.128.refs_0_, ...), custom_call_target="tpu_custom_call" | custom-call | tf_op jit(solution)/shard_map/pallas_call | solution.py:184
  159.9 2.3 %collective-permute-done.48 = f32[1,2048]{1,0:T(1,128)S(1)} collective-permute-done((f32[1,2048]{1,0:T(1,128)S(1)}, f32[1,2048]{1,0:T(1,128)S(1)}, u32[]{:S(2)}, u32[]{:S(2)}) %collective-permute-start.48) | collective-permute-done | bytes 8224 | tf_op jit(solution)/shard_map/ppermute | solution.py:26
  (146 shorter events, 58.6 us)
Async XLA Ops:
  4.7 20.1 %collective-permute-start.2 = (bf16[48,2048]{1,0:T(8,128)(2,1)}, bf16[48,2048]{1,0:T(8,128)(2,1)S(1)}, u32[]{:S(2)}, u32[]{:S(2)}) collective-permute-start(bf16[48,2048]{1,0:T(8,128)(2,1)} %refs_0_.3), channel_id=1, source_target_pairs={{0,3},{1,2},{2,1},{3,0},{4,7},{5,6},{6,5},{7,4},{8,11},{9,10},{10,... | collective-permute-start | bytes 589832 | tf_op jit(solution)/shard_map/ppermute | solution.py:26
  8.3 16.6 %collective-permute-start.1 = (bf16[48,2048]{1,0:T(8,128)(2,1)}, bf16[48,2048]{1,0:T(8,128)(2,1)S(1)}, u32[]{:S(2)}, u32[]{:S(2)}) collective-permute-start(bf16[48,2048]{1,0:T(8,128)(2,1)} %refs_0_.3), channel_id=1, source_target_pairs={{0,2},{1,3},{2,0},{3,1},{4,6},{5,7},{6,4},{7,5},{8,10},{9,11},{10,... | collective-permute-start | bytes 589832 | tf_op jit(solution)/shard_map/ppermute | solution.py:26
  8.3 16.6 %collective-permute-start = (bf16[48,2048]{1,0:T(8,128)(2,1)}, bf16[48,2048]{1,0:T(8,128)(2,1)S(1)}, u32[]{:S(2)}, u32[]{:S(2)}) collective-permute-start(bf16[48,2048]{1,0:T(8,128)(2,1)} %refs_0_.3), channel_id=1, source_target_pairs={{0,1},{1,0},{2,3},{3,2},{4,5},{5,4},{6,7},{7,6},{8,9},{9,8},{10,11... | collective-permute-start | bytes 589832 | tf_op jit(solution)/shard_map/ppermute | solution.py:26
  9.1 15.8 %collective-permute-start.3 = (bf16[48,2048]{1,0:T(8,128)(2,1)}, bf16[48,2048]{1,0:T(8,128)(2,1)S(1)}, u32[]{:S(2)}, u32[]{:S(2)}) collective-permute-start(bf16[48,2048]{1,0:T(8,128)(2,1)} %refs_0_.3), channel_id=1, source_target_pairs={{0,16},{16,0},{1,17},{17,1},{2,18},{18,2},{3,19},{19,3},{4,20},{20... | collective-permute-start | bytes 589832 | tf_op jit(solution)/shard_map/ppermute | solution.py:26
  13.8 11.2 %collective-permute-start.6 = (bf16[48,2048]{1,0:T(8,128)(2,1)S(1)}, bf16[48,2048]{1,0:T(8,128)(2,1)S(1)}, u32[]{:S(2)}, u32[]{:S(2)}) collective-permute-start(bf16[48,2048]{1,0:T(8,128)(2,1)S(1)} %fusion.2.refs_0_), channel_id=1, source_target_pairs={{0,16},{16,0},{1,17},{17,1},{2,18},{18,2},{3,19},{19,3},{4,20},{20... | collective-permute-start | bytes 589832 | tf_op jit(solution)/shard_map/ppermute | solution.py:26
  29.6 16.6 %collective-permute-start.8 = (bf16[48,2048]{1,0:T(8,128)(2,1)S(1)}, bf16[48,2048]{1,0:T(8,128)(2,1)S(1)}, u32[]{:S(2)}, u32[]{:S(2)}) collective-permute-start(bf16[48,2048]{1,0:T(8,128)(2,1)S(1)} %fusion.2.refs_0_), channel_id=1, source_target_pairs={{0,2},{1,3},{2,0},{3,1},{4,6},{5,7},{6,4},{7,5},{8,10},{9,11},{10,... | collective-permute-start | bytes 589832 | tf_op jit(solution)/shard_map/ppermute | solution.py:26
  29.6 16.6 %collective-permute-start.7 = (bf16[48,2048]{1,0:T(8,128)(2,1)S(1)}, bf16[48,2048]{1,0:T(8,128)(2,1)S(1)}, u32[]{:S(2)}, u32[]{:S(2)}) collective-permute-start(bf16[48,2048]{1,0:T(8,128)(2,1)S(1)} %fusion.2.refs_0_), channel_id=1, source_target_pairs={{0,1},{1,0},{2,3},{3,2},{4,5},{5,4},{6,7},{7,6},{8,9},{9,8},{10,11... | collective-permute-start | bytes 589832 | tf_op jit(solution)/shard_map/ppermute | solution.py:26
  34.3 23.8 %collective-permute-start.18 = (bf16[1,96,1792]{2,1,0:T(8,128)(2,1)S(1)}, bf16[1,96,1792]{2,1,0:T(8,128)(2,1)S(1)}, u32[]{:S(2)}, u32[]{:S(2)}) collective-permute-start(bf16[1,96,1792]{2,1,0:T(8,128)(2,1)S(1)} %get-tuple-element.157), channel_id=1, source_target_pairs={{0,4},{4,0},{8,12},{12,8},{1,5},{5,1},{9,13},{13,9},{2,6},{6,2},{1... | collective-permute-start | bytes 1032200 | tf_op jit(solution)/shard_map/ppermute | solution.py:26
  34.6 23.5 %collective-permute-start.19 = (bf16[1,96,1792]{2,1,0:T(8,128)(2,1)S(1)}, bf16[1,96,1792]{2,1,0:T(8,128)(2,1)S(1)}, u32[]{:S(2)}, u32[]{:S(2)}) collective-permute-start(bf16[1,96,1792]{2,1,0:T(8,128)(2,1)S(1)} %get-tuple-element.158), channel_id=1, source_target_pairs={{0,8},{4,12},{8,0},{12,4},{1,9},{5,13},{9,1},{13,5},{2,10},{6,14},... | collective-permute-start | bytes 1032200 | tf_op jit(solution)/shard_map/ppermute | solution.py:26
  58.1 12.4 %collective-permute-start.22 = (bf16[1,96,1792]{2,1,0:T(8,128)(2,1)S(1)}, bf16[1,96,1792]{2,1,0:T(8,128)(2,1)S(1)}, u32[]{:S(2)}, u32[]{:S(2)}) collective-permute-start(bf16[1,96,1792]{2,1,0:T(8,128)(2,1)S(1)} %get-tuple-element.168), channel_id=1, source_target_pairs={{0,4},{4,0},{8,12},{12,8},{1,5},{5,1},{9,13},{13,9},{2,6},{6,2},{1... | collective-permute-start | bytes 1032200 | tf_op jit(solution)/shard_map/ppermute | solution.py:26
  59.7 11.4 %collective-permute-start.23 = (bf16[1,96,1792]{2,1,0:T(8,128)(2,1)S(1)}, bf16[1,96,1792]{2,1,0:T(8,128)(2,1)S(1)}, u32[]{:S(2)}, u32[]{:S(2)}) collective-permute-start(bf16[1,96,1792]{2,1,0:T(8,128)(2,1)S(1)} %get-tuple-element.169), channel_id=1, source_target_pairs={{0,8},{4,12},{8,0},{12,4},{1,9},{5,13},{9,1},{13,5},{2,10},{6,14},... | collective-permute-start | bytes 1032200 | tf_op jit(solution)/shard_map/ppermute | solution.py:26
  63.8 11.0 %collective-permute-start.21 = (bf16[1,48,1792]{2,1,0:T(8,128)(2,1)S(1)}, bf16[1,48,1792]{2,1,0:T(8,128)(2,1)S(1)}, u32[]{:S(2)}, u32[]{:S(2)}) collective-permute-start(bf16[1,48,1792]{2,1,0:T(8,128)(2,1)S(1)} %add_convert_fusion.3), channel_id=1, source_target_pairs={{0,4},{4,0},{8,12},{12,8},{1,5},{5,1},{9,13},{13,9},{2,6},{6,2},{1... | collective-permute-start | bytes 516104 | tf_op jit(solution)/shard_map/ppermute | solution.py:26
  95.5 18.1 %collective-permute-start.31 = (bf16[2,96,1792]{2,1,0:T(8,128)(2,1)S(1)}, bf16[2,96,1792]{2,1,0:T(8,128)(2,1)S(1)}, u32[]{:S(2)}, u32[]{:S(2)}) collective-permute-start(bf16[2,96,1792]{2,1,0:T(8,128)(2,1)S(1)} %get-tuple-element.203.refs_0_), channel_id=1, source_target_pairs={{0,8},{4,12},{8,0},{12,4},{1,9},{5,13},{9,1},{13,5},{2,10},{6,14},... | collective-permute-start | bytes 2064392 | tf_op jit(solution)/shard_map/ppermute | solution.py:26
  97.0 16.6 %collective-permute-start.30 = (bf16[2,96,1792]{2,1,0:T(8,128)(2,1)S(1)}, bf16[2,96,1792]{2,1,0:T(8,128)(2,1)S(1)}, u32[]{:S(2)}, u32[]{:S(2)}) collective-permute-start(bf16[2,96,1792]{2,1,0:T(8,128)(2,1)S(1)} %get-tuple-element.203.refs_0_), channel_id=1, source_target_pairs={{0,4},{4,0},{8,12},{12,8},{1,5},{5,1},{9,13},{13,9},{2,6},{6,2},{1... | collective-permute-start | bytes 2064392 | tf_op jit(solution)/shard_map/ppermute | solution.py:26
  113.7 15.7 %collective-permute-start.40 = (bf16[2,48,1792]{2,1,0:T(8,128)(2,1)S(1)}, bf16[2,48,1792]{2,1,0:T(8,128)(2,1)S(1)}, u32[]{:S(2)}, u32[]{:S(2)}) collective-permute-start(bf16[2,48,1792]{2,1,0:T(8,128)(2,1)S(1)} %slice.49), channel_id=1, source_target_pairs={{0,4},{4,0},{8,12},{12,8},{1,5},{5,1},{9,13},{13,9},{2,6},{6,2},{1... | collective-permute-start | bytes 1032200 | tf_op jit(solution)/shard_map/ppermute | solution.py:26
  114.3 15.1 %collective-permute-start.41 = (bf16[2,48,1792]{2,1,0:T(8,128)(2,1)S(1)}, bf16[2,48,1792]{2,1,0:T(8,128)(2,1)S(1)}, u32[]{:S(2)}, u32[]{:S(2)}) collective-permute-start(bf16[2,48,1792]{2,1,0:T(8,128)(2,1)S(1)} %slice.50), channel_id=1, source_target_pairs={{0,8},{4,12},{8,0},{12,4},{1,9},{5,13},{9,1},{13,5},{2,10},{6,14},... | collective-permute-start | bytes 1032200 | tf_op jit(solution)/shard_map/ppermute | solution.py:26
  116.7 18.6 %collective-permute-start.37 = (bf16[48,2048]{1,0:T(8,128)(2,1)S(1)}, bf16[48,2048]{1,0:T(8,128)(2,1)S(1)}, u32[]{:S(2)}, u32[]{:S(2)}) collective-permute-start(bf16[48,2048]{1,0:T(8,128)(2,1)S(1)} %get-tuple-element.218), channel_id=1, source_target_pairs={{0,1},{1,0},{2,3},{3,2},{4,5},{5,4},{6,7},{7,6},{8,9},{9,8},{10,11... | collective-permute-start | bytes 589832 | tf_op jit(solution)/shard_map/ppermute | solution.py:26
  116.8 18.6 %collective-permute-start.38 = (bf16[48,2048]{1,0:T(8,128)(2,1)S(1)}, bf16[48,2048]{1,0:T(8,128)(2,1)S(1)}, u32[]{:S(2)}, u32[]{:S(2)}) collective-permute-start(bf16[48,2048]{1,0:T(8,128)(2,1)S(1)} %get-tuple-element.219), channel_id=1, source_target_pairs={{0,2},{1,3},{2,0},{3,1},{4,6},{5,7},{6,4},{7,5},{8,10},{9,11},{10,... | collective-permute-start | bytes 589832 | tf_op jit(solution)/shard_map/ppermute | solution.py:26
  119.7 15.7 %collective-permute-start.39 = (bf16[48,2048]{1,0:T(8,128)(2,1)S(1)}, bf16[48,2048]{1,0:T(8,128)(2,1)S(1)}, u32[]{:S(2)}, u32[]{:S(2)}) collective-permute-start(bf16[48,2048]{1,0:T(8,128)(2,1)S(1)} %get-tuple-element.220), channel_id=1, source_target_pairs={{0,3},{1,2},{2,1},{3,0},{4,7},{5,6},{6,5},{7,4},{8,11},{9,10},{10,... | collective-permute-start | bytes 589832 | tf_op jit(solution)/shard_map/ppermute | solution.py:26
  141.8 20.4 %collective-permute-start.43 = (bf16[48,2048]{1,0:T(8,128)(2,1)S(1)}, bf16[48,2048]{1,0:T(8,128)(2,1)S(1)}, u32[]{:S(2)}, u32[]{:S(2)}) collective-permute-start(bf16[48,2048]{1,0:T(8,128)(2,1)S(1)} %get-tuple-element.245), channel_id=1, source_target_pairs={{0,1},{1,0},{2,3},{3,2},{4,5},{5,4},{6,7},{7,6},{8,9},{9,8},{10,11... | collective-permute-start | bytes 589832 | tf_op jit(solution)/shard_map/ppermute | solution.py:26
  141.9 20.3 %collective-permute-start.44 = (bf16[48,2048]{1,0:T(8,128)(2,1)S(1)}, bf16[48,2048]{1,0:T(8,128)(2,1)S(1)}, u32[]{:S(2)}, u32[]{:S(2)}) collective-permute-start(bf16[48,2048]{1,0:T(8,128)(2,1)S(1)} %get-tuple-element.246), channel_id=1, source_target_pairs={{0,2},{1,3},{2,0},{3,1},{4,6},{5,7},{6,4},{7,5},{8,10},{9,11},{10,... | collective-permute-start | bytes 589832 | tf_op jit(solution)/shard_map/ppermute | solution.py:26
  144.8 17.4 %collective-permute-start.45 = (bf16[48,2048]{1,0:T(8,128)(2,1)S(1)}, bf16[48,2048]{1,0:T(8,128)(2,1)S(1)}, u32[]{:S(2)}, u32[]{:S(2)}) collective-permute-start(bf16[48,2048]{1,0:T(8,128)(2,1)S(1)} %get-tuple-element.247), channel_id=1, source_target_pairs={{0,3},{1,2},{2,1},{3,0},{4,7},{5,6},{6,5},{7,4},{8,11},{9,10},{10,... | collective-permute-start | bytes 589832 | tf_op jit(solution)/shard_map/ppermute | solution.py:26
  146.3 15.9 %collective-permute-start.48 = (f32[1,2048]{1,0:T(1,128)S(1)}, f32[1,2048]{1,0:T(1,128)S(1)}, u32[]{:S(2)}, u32[]{:S(2)}) collective-permute-start(f32[1,2048]{1,0:T(1,128)S(1)} %add.81), channel_id=1, source_target_pairs={{0,2},{1,3},{2,0},{3,1},{4,6},{5,7},{6,4},{7,5},{8,10},{9,11},{10,... | collective-permute-start | bytes 24584 | tf_op jit(solution)/shard_map/ppermute | solution.py:26
  146.6 15.6 %collective-permute-start.49 = (f32[48,128]{1,0:T(8,128)S(1)}, f32[48,128]{1,0:T(8,128)S(1)}, u32[]{:S(2)}, u32[]{:S(2)}) collective-permute-start(f32[48,128]{1,0:T(8,128)S(1)} %add.82), channel_id=1, source_target_pairs={{0,8},{4,12},{8,0},{12,4},{1,9},{5,13},{9,1},{13,5},{2,10},{6,14},... | collective-permute-start | bytes 73736 | tf_op jit(solution)/shard_map/ppermute | solution.py:26
  (37 other events, 251.1 us)

commit v6 on v5

--- a/solution.py
+++ b/solution.py
@@ -194,6 +194,38 @@
     )(left, right, *masks)
 
 
+def outer_one_kernel(left_ref, right_ref, mask_ref, out_ref, held_ref, sems):
+    slots, edge, _ = held_ref.shape
+    copies = []
+    for block in range(left_ref.shape[1] // edge):
+        rows = slice(block * edge, (block + 1) * edge)
+        slot = block % slots
+        if block >= slots:
+            copies[block - slots].wait()
+        result = lax.dot_general(
+            left_ref[:, rows], right_ref[...], (((0,), (0,)), ((), ())), preferred_element_type=F32
+        )
+        held_ref[slot] = masked(result, mask_ref[block].astype(F32))
+        copies.append(pltpu.make_async_copy(held_ref.at[slot], out_ref.at[rows], sems.at[slot]))
+        copies[-1].start()
+    for copy in copies[-slots:]:
+        copy.wait()
+
+
+def outer_one(left, right, mask):
+    rows, width = left.shape[1], right.shape[1]
+    edge = block_edge(rows)
+    return pl.pallas_call(
+        outer_one_kernel,
+        in_specs=[IN_VMEM] * 3,
+        out_specs=pl.BlockSpec(memory_space=pl.ANY),
+        out_shape=jax.ShapeDtypeStruct((rows, width), F32),
+        scratch_shapes=[pltpu.VMEM((3, edge, width), F32), pltpu.SemaphoreType.DMA((3,))],
+        compiler_params=kernel_params(),
+        cost_estimate=pl.CostEstimate(flops=0, bytes_accessed=0, transcendentals=0),
+    )(left, right, mask)
+
+
 def owner_kernel(count, place_ref, own_ref, got_ref, *refs):
     factors = refs[:count] if len(refs) > count else ()
     outs = refs[len(factors) : len(factors) + count]
@@ -431,7 +463,7 @@
     branch_kept, *branch_parts = owner(place_arg, branch_own, branch_got, cols)
     branch_far = level_swaps(branch_parts)
     hidden, grads_middle = ordered(hidden, grads_middle)
-    (grad_down,) = outer(hidden[0], seen_cot[None], [down_groups])
+    grad_down = outer_one(hidden[0], seen_cot, down_groups)
     grads_last, grad_down = ordered(grads_last, grad_down)
 
     grads, normed_mine, normed_theirs = contract(
@@ -496,7 +528,7 @@
         [collect(jnp.stack([gate_grad, up_grad]))], [gate_weight, up_weight], [gate_mask, up_mask], plan, (F32,), False
     )
     normed_grad = owner_sum(normed_grad)
-    (grad_down,) = outer(hidden[0], seen_cot[None], [down_groups])
+    grad_down = outer_one(hidden[0], seen_cot, down_groups)
     grad_gate, grad_up = outer(seen_rows, grads, [gate_groups, up_groups])
     grad_tokens, grad_gain = finish(
         token_f,

time: 165 us -> 165 us (level)
    pallas_call x2 -> x1, Pallas kernels: 19.6 us -> 11.4 us  [outer(): pl.pallas_call(outer_kernel, grid=(rows // edge,), in_specs=[IN_VMEM, IN_...]
    pallas_call x0 -> x1, Pallas kernels: none -> 7.02 us  [outer_one(): pl.pallas_call(outer_one_kernel, in_specs=[IN_VMEM] * 3, out_specs=pl.Blo...]
where the time goes in v6:
time: 165 us; the launch traced here: 164 us
  starting transfers between devices  53.4 us (32%)
  waiting for transfers between devices  49.8 us (30%)
  Pallas kernels  43.1 us (26%)
  local copies, waits for them, and re-layouts  9.77 us (6%)
  other arithmetic  6.98 us (4%)
    ppermute x50, starting transfers between devices, swap(): return lax.ppermute(value, axis, [(i, i ^ step) for i in range(size)])  52.5 us
    ppermute x50, waiting for transfers between devices, swap(): return lax.ppermute(value, axis, [(i, i ^ step) for i in range(size)])  49.8 us
    pallas_call x3, Pallas kernels, project(): pl.pallas_call(functools.partial(project_kernel, ring, plan, by_unit, amo...  11.7 us
    pallas_call x1, Pallas kernels, outer(): pl.pallas_call(outer_kernel, grid=(rows // edge,), in_specs=[IN_VMEM, IN_...  11.4 us
    unnamed x22, local copies, waits for them, and re-layouts  9.3 us
    pallas_call x2, Pallas kernels, contract(): pl.pallas_call(functools.partial(contract_kernel, pieces, plan, by_unit,...  8.94 us
    pallas_call x1, Pallas kernels, outer_one(): pl.pallas_call(outer_one_kernel, in_specs=[IN_VMEM] * 3, out_specs=pl.Blo...  7.02 us
  transfers between devices with their start and end apart: 51, of which 24 were waited for; matrix products, arithmetic and copies ran while one was open for 3% of the time, Pallas kernels for 25%

profile of v6, /device:TPU:0, one launch (start us, length us, event | category | flops | bytes accessed | tf_op | source)
XLA Modules:
  0.0 164.2 jit_solution(15608164721355190231)
XLA Ops:
  1.7 3.0 %collective-permute-start.4 = (f32[48]{0:T(128)S(1)}, f32[48]{0:T(128)S(1)}, u32[]{:S(2)}, u32[]{:S(2)}) collective-permute-start(f32[48]{0:T(128)S(1)} %fusion.6), channel_id=1, source_target_pairs={{0,4},{4,0},{8,12},{12,8},{1,5},{5,1},{9,13},{13,9},{2,6},{6,2},{1... | collective-permute-start | bytes 584 | tf_op jit(solution)/shard_map/ppermute | solution.py:26
  4.7 3.6 %collective-permute-start.2 = (bf16[48,2048]{1,0:T(8,128)(2,1)}, bf16[48,2048]{1,0:T(8,128)(2,1)S(1)}, u32[]{:S(2)}, u32[]{:S(2)}) collective-permute-start(bf16[48,2048]{1,0:T(8,128)(2,1)} %refs_0_.3), channel_id=1, source_target_pairs={{0,3},{1,2},{2,1},{3,0},{4,7},{5,6},{6,5},{7,4},{8,11},{9,10},{10,... | collective-permute-start | bytes 589832 | tf_op jit(solution)/shard_map/ppermute | solution.py:26
  15.0 3.1 %copy-done = bf16[2048,1792]{1,0:T(8,128)(2,1)S(1)} copy-done((bf16[2048,1792]{1,0:T(8,128)(2,1)S(1)}, bf16[2048,1792]{1,0:T(8,128)(2,1)}, u32[]{:S(2)}) %copy-start) | copy-done | bytes 7340056
  18.1 3.1 %copy-done.2 = bf16[2048,1792]{1,0:T(8,128)(2,1)S(1)} copy-done((bf16[2048,1792]{1,0:T(8,128)(2,1)S(1)}, bf16[2048,1792]{1,0:T(8,128)(2,1)}, u32[]{:S(2)}) %copy-start.2) | copy-done | bytes 7340056
  21.2 3.1 %copy-done.3 = bf16[1792,2048]{1,0:T(8,128)(2,1)S(1)} copy-done((bf16[1792,2048]{1,0:T(8,128)(2,1)S(1)}, bf16[1792,2048]{1,0:T(8,128)(2,1)}, u32[]{:S(2)}) %copy-start.3) | copy-done | bytes 7340056
  26.0 3.6 %collective-permute-start.9 = (bf16[48,2048]{1,0:T(8,128)(2,1)S(1)}, bf16[48,2048]{1,0:T(8,128)(2,1)S(1)}, u32[]{:S(2)}, u32[]{:S(2)}) collective-permute-start(bf16[48,2048]{1,0:T(8,128)(2,1)S(1)} %fusion.2.refs_0_), channel_id=1, source_target_pairs={{0,3},{1,2},{2,1},{3,0},{4,7},{5,6},{6,5},{7,4},{8,11},{9,10},{10,... | collective-permute-start | bytes 589832 | tf_op jit(solution)/shard_map/ppermute | solution.py:26
  30.4 3.9 %shard_map.137 = (bf16[384,2048]{1,0:T(8,128)(2,1)S(1)}, bf16[1,96,1792]{2,1,0:T(8,128)(2,1)S(1)}, bf16[1,96,1792]{2,1,0:T(8,128)(2,1)S(1)}, bf16[1,48,1792]{2,1...) custom-call(s32[1]{0:T(128)} %shard_map.136.place_ref, ...), custom_call_target="tpu_custom_call" | custom-call | tf_op jit(solution)/shard_map/pallas_call | solution.py:109
  36.4 9.8 %collective-permute-done.8.refs_2_ = bf16[48,2048]{1,0:T(8,128)(2,1)S(1)} collective-permute-done((bf16[48,2048]{1,0:T(8,128)(2,1)S(1)}, bf16[48,2048]{1,0:T(8,128)(2,1)S(1)}, u32[]{:S(2)}, u32[]{:S(2)}) %collective-permute-start.8) | collective-permute-done | bytes 196640 | tf_op jit(solution)/shard_map/ppermute | solution.py:26
  48.2 4.0 %shard_map.138 = (bf16[384,2048]{1,0:T(8,128)(2,1)S(1)}, bf16[1,96,1792]{2,1,0:T(8,128)(2,1)S(1)}, bf16[1,96,1792]{2,1,0:T(8,128)(2,1)S(1)}, bf16[1,48,1792]{2,1...) custom-call(s32[1]{0:T(128)} %shard_map.136.place_ref, ...), custom_call_target="tpu_custom_call" | custom-call | tf_op jit(solution)/shard_map/pallas_call | solution.py:109
  54.3 3.8 %shard_map.139 = (bf16[384,2048]{1,0:T(8,128)(2,1)}, bf16[1,96,1792]{2,1,0:T(8,128)(2,1)S(1)}, bf16[1,96,1792]{2,1,0:T(8,128)(2,1)S(1)}, bf16[1,48,1792]{2,1,0:T...) custom-call(s32[1]{0:T(128)} %shard_map.136.place_ref, ...), custom_call_target="tpu_custom_call" | custom-call | tf_op jit(solution)/shard_map/pallas_call | solution.py:109
  60.3 2.9 %collective-permute-done.16.refs_1_ = bf16[1,96,1792]{2,1,0:T(8,128)(2,1)S(1)} collective-permute-done((bf16[1,96,1792]{2,1,0:T(8,128)(2,1)S(1)}, bf16[1,96,1792]{2,1,0:T(8,128)(2,1)S(1)}, u32[]{:S(2)}, u32[]{:S(2)}) %collective-permute-start.16) | collective-permute-done | bytes 344096 | tf_op jit(solution)/shard_map/ppermute | solution.py:26
  67.0 3.6 %collective-permute-done.22.refs_6_ = bf16[1,96,1792]{2,1,0:T(8,128)(2,1)S(1)} collective-permute-done((bf16[1,96,1792]{2,1,0:T(8,128)(2,1)S(1)}, bf16[1,96,1792]{2,1,0:T(8,128)(2,1)S(1)}, u32[]{:S(2)}, u32[]{:S(2)}) %collective-permute-start.22) | collective-permute-done | bytes 344096 | tf_op jit(solution)/shard_map/ppermute | solution.py:26
  75.7 2.7 %collective-permute-done.26.refs_13_ = bf16[1,48,1792]{2,1,0:T(8,128)(2,1)S(1)} collective-permute-done((bf16[1,48,1792]{2,1,0:T(8,128)(2,1)S(1)}, bf16[1,48,1792]{2,1,0:T(8,128)(2,1)S(1)}, u32[]{:S(2)}, u32[]{:S(2)}) %collective-permute-start.26) | collective-permute-done | bytes 172064 | tf_op jit(solution)/shard_map/ppermute | solution.py:26
  86.1 6.0 %collective-permute-done.29.refs_2_ = bf16[1,96,1792]{2,1,0:T(8,128)(2,1)S(1)} collective-permute-done((bf16[1,96,1792]{2,1,0:T(8,128)(2,1)S(1)}, bf16[1,96,1792]{2,1,0:T(8,128)(2,1)S(1)}, u32[]{:S(2)}, u32[]{:S(2)}) %collective-permute-start.29) | collective-permute-done | bytes 344096 | tf_op jit(solution)/shard_map/ppermute | solution.py:26
  97.5 3.1 %collective-permute-done.32.refs_3_ = bf16[1,48,1792]{2,1,0:T(8,128)(2,1)S(1)} collective-permute-done((bf16[1,48,1792]{2,1,0:T(8,128)(2,1)S(1)}, bf16[1,48,1792]{2,1,0:T(8,128)(2,1)S(1)}, u32[]{:S(2)}, u32[]{:S(2)}) %collective-permute-start.32) | collective-permute-done | bytes 172064 | tf_op jit(solution)/shard_map/ppermute | solution.py:26
  102.3 3.0 %shard_map.141 = (bf16[1,384,1792]{2,1,0:T(8,128)(2,1)S(1)}, f32[192,2048]{1,0:T(8,128)S(1)}, bf16[192,2048]{1,0:T(8,128)(2,1)S(1)}) custom-call(bf16[1,96,1792]{2,1,0:T(8,128)(2,1)S(1)} %get-tuple-element.200.refs_0_, bf16[1,96,1792]{2,1,0:T(8,128)(2,1)S(1)} %collective-permute-done.28.refs_1_, bf16[1,96,1792]{2,1,0:T(8,128)(2,1)S(1)} %collective-permute-done.29.refs_2_, ...), custom_call_target="tpu_custom_call" | custom-call | flops 28185722880 | bytes 73400320 | tf_op jit(solution)/shard_map/pallas_call | solution.py:155
  107.5 6.1 %collective-permute-done.31.refs_2_ = bf16[2,96,1792]{2,1,0:T(8,128)(2,1)S(1)} collective-permute-done((bf16[2,96,1792]{2,1,0:T(8,128)(2,1)S(1)}, bf16[2,96,1792]{2,1,0:T(8,128)(2,1)S(1)}, u32[]{:S(2)}, u32[]{:S(2)}) %collective-permute-start.31) | collective-permute-done | bytes 688160 | tf_op jit(solution)/shard_map/ppermute | solution.py:26
  116.8 2.9 %collective-permute-start.38 = (bf16[48,2048]{1,0:T(8,128)(2,1)S(1)}, bf16[48,2048]{1,0:T(8,128)(2,1)S(1)}, u32[]{:S(2)}, u32[]{:S(2)}) collective-permute-start(bf16[48,2048]{1,0:T(8,128)(2,1)S(1)} %get-tuple-element.219), channel_id=1, source_target_pairs={{0,2},{1,3},{2,0},{3,1},{4,6},{5,7},{6,4},{7,5},{8,10},{9,11},{10,... | collective-permute-start | bytes 589832 | tf_op jit(solution)/shard_map/ppermute | solution.py:26
  121.1 7.0 %shard_map.143 = f32[1792,2048]{1,0:T(8,128)} custom-call(bf16[384,1792]{1,0:T(8,128)(2,1)S(1)} %bitcast.14, bf16[384,2048]{1,0:T(8,128)(2,1)S(1)} %get-tuple-element.227.right_ref, bf16[7,2,2048]{2,1,0:T(2,128)(2,1)S(1)} %convert_element_type.130.mask_ref), custom_call_target="tpu_custom_call" | custom-call | tf_op jit(solution)/shard_map/pallas_call | solution.py:218
  128.2 5.9 %shard_map.144 = (bf16[2,384,1792]{2,1,0:T(8,128)(2,1)S(1)}, f32[192,2048]{1,0:T(8,128)S(1)}, bf16[192,2048]{1,0:T(8,128)(2,1)S(1)}) custom-call(bf16[2,96,1792]{2,1,0:T(8,128)(2,1)S(1)} %get-tuple-element.203.refs_0_, bf16[2,96,1792]{2,1,0:T(8,128)(2,1)S(1)} %collective-permute-done.30.refs_1_, bf16[2,96,1792]{2,1,0:T(8,128)(2,1)S(1)} %collective-permute-done.31.refs_2_, ...), custom_call_target="tpu_custom_call" | custom-call | tf_op jit(solution)/shard_map/pallas_call | solution.py:155
  138.2 3.7 %collective-permute-start.46 = (f32[1,2048]{1,0:T(1,128)S(1)}, f32[1,2048]{1,0:T(1,128)S(1)}, u32[]{:S(2)}, u32[]{:S(2)}) collective-permute-start(f32[1,2048]{1,0:T(1,128)S(1)} %get-tuple-element.249), channel_id=1, source_target_pairs={{0,1},{1,0},{2,3},{3,2},{4,5},{5,4},{6,7},{7,6},{8,9},{9,8},{10,11... | collective-permute-start | bytes 24584 | tf_op jit(solution)/shard_map/ppermute | solution.py:26
  141.9 2.9 %collective-permute-start.44 = (bf16[48,2048]{1,0:T(8,128)(2,1)S(1)}, bf16[48,2048]{1,0:T(8,128)(2,1)S(1)}, u32[]{:S(2)}, u32[]{:S(2)}) collective-permute-start(bf16[48,2048]{1,0:T(8,128)(2,1)S(1)} %get-tuple-element.246), channel_id=1, source_target_pairs={{0,2},{1,3},{2,0},{3,1},{4,6},{5,7},{6,4},{7,5},{8,10},{9,11},{10,... | collective-permute-start | bytes 589832 | tf_op jit(solution)/shard_map/ppermute | solution.py:26
  148.5 11.4 %shard_map.146 = (f32[2048,1792]{1,0:T(8,128)}, f32[2048,1792]{1,0:T(8,128)}) custom-call(bf16[384,2048]{1,0:T(8,128)(2,1)S(1)} %get-tuple-element.161.refs_0_.left_ref, bf16[2,384,1792]{2,1,0:T(8,128)(2,1)S(1)} %get-tuple-element.253.right_ref, bf16[8,2,1792]{2,1,0:T(2,128)(2,1)S(1)} %convert_element_type.128.refs_0_, ...), custom_call_target="tpu_custom_call" | custom-call | tf_op jit(solution)/shard_map/pallas_call | solution.py:184
  159.9 2.3 %collective-permute-done.48 = f32[1,2048]{1,0:T(1,128)S(1)} collective-permute-done((f32[1,2048]{1,0:T(1,128)S(1)}, f32[1,2048]{1,0:T(1,128)S(1)}, u32[]{:S(2)}, u32[]{:S(2)}) %collective-permute-start.48) | collective-permute-done | bytes 8224 | tf_op jit(solution)/shard_map/ppermute | solution.py:26
  (146 shorter events, 58.6 us)
Async XLA Ops:
  4.7 20.1 %collective-permute-start.2 = (bf16[48,2048]{1,0:T(8,128)(2,1)}, bf16[48,2048]{1,0:T(8,128)(2,1)S(1)}, u32[]{:S(2)}, u32[]{:S(2)}) collective-permute-start(bf16[48,2048]{1,0:T(8,128)(2,1)} %refs_0_.3), channel_id=1, source_target_pairs={{0,3},{1,2},{2,1},{3,0},{4,7},{5,6},{6,5},{7,4},{8,11},{9,10},{10,... | collective-permute-start | bytes 589832 | tf_op jit(solution)/shard_map/ppermute | solution.py:26
  8.3 16.6 %collective-permute-start.1 = (bf16[48,2048]{1,0:T(8,128)(2,1)}, bf16[48,2048]{1,0:T(8,128)(2,1)S(1)}, u32[]{:S(2)}, u32[]{:S(2)}) collective-permute-start(bf16[48,2048]{1,0:T(8,128)(2,1)} %refs_0_.3), channel_id=1, source_target_pairs={{0,2},{1,3},{2,0},{3,1},{4,6},{5,7},{6,4},{7,5},{8,10},{9,11},{10,... | collective-permute-start | bytes 589832 | tf_op jit(solution)/shard_map/ppermute | solution.py:26
  8.3 16.6 %collective-permute-start = (bf16[48,2048]{1,0:T(8,128)(2,1)}, bf16[48,2048]{1,0:T(8,128)(2,1)S(1)}, u32[]{:S(2)}, u32[]{:S(2)}) collective-permute-start(bf16[48,2048]{1,0:T(8,128)(2,1)} %refs_0_.3), channel_id=1, source_target_pairs={{0,1},{1,0},{2,3},{3,2},{4,5},{5,4},{6,7},{7,6},{8,9},{9,8},{10,11... | collective-permute-start | bytes 589832 | tf_op jit(solution)/shard_map/ppermute | solution.py:26
  9.1 15.8 %collective-permute-start.3 = (bf16[48,2048]{1,0:T(8,128)(2,1)}, bf16[48,2048]{1,0:T(8,128)(2,1)S(1)}, u32[]{:S(2)}, u32[]{:S(2)}) collective-permute-start(bf16[48,2048]{1,0:T(8,128)(2,1)} %refs_0_.3), channel_id=1, source_target_pairs={{0,16},{16,0},{1,17},{17,1},{2,18},{18,2},{3,19},{19,3},{4,20},{20... | collective-permute-start | bytes 589832 | tf_op jit(solution)/shard_map/ppermute | solution.py:26
  13.8 11.2 %collective-permute-start.6 = (bf16[48,2048]{1,0:T(8,128)(2,1)S(1)}, bf16[48,2048]{1,0:T(8,128)(2,1)S(1)}, u32[]{:S(2)}, u32[]{:S(2)}) collective-permute-start(bf16[48,2048]{1,0:T(8,128)(2,1)S(1)} %fusion.2.refs_0_), channel_id=1, source_target_pairs={{0,16},{16,0},{1,17},{17,1},{2,18},{18,2},{3,19},{19,3},{4,20},{20... | collective-permute-start | bytes 589832 | tf_op jit(solution)/shard_map/ppermute | solution.py:26
  29.6 16.6 %collective-permute-start.8 = (bf16[48,2048]{1,0:T(8,128)(2,1)S(1)}, bf16[48,2048]{1,0:T(8,128)(2,1)S(1)}, u32[]{:S(2)}, u32[]{:S(2)}) collective-permute-start(bf16[48,2048]{1,0:T(8,128)(2,1)S(1)} %fusion.2.refs_0_), channel_id=1, source_target_pairs={{0,2},{1,3},{2,0},{3,1},{4,6},{5,7},{6,4},{7,5},{8,10},{9,11},{10,... | collective-permute-start | bytes 589832 | tf_op jit(solution)/shard_map/ppermute | solution.py:26
  29.6 16.6 %collective-permute-start.7 = (bf16[48,2048]{1,0:T(8,128)(2,1)S(1)}, bf16[48,2048]{1,0:T(8,128)(2,1)S(1)}, u32[]{:S(2)}, u32[]{:S(2)}) collective-permute-start(bf16[48,2048]{1,0:T(8,128)(2,1)S(1)} %fusion.2.refs_0_), channel_id=1, source_target_pairs={{0,1},{1,0},{2,3},{3,2},{4,5},{5,4},{6,7},{7,6},{8,9},{9,8},{10,11... | collective-permute-start | bytes 589832 | tf_op jit(solution)/shard_map/ppermute | solution.py:26
  34.3 23.8 %collective-permute-start.18 = (bf16[1,96,1792]{2,1,0:T(8,128)(2,1)S(1)}, bf16[1,96,1792]{2,1,0:T(8,128)(2,1)S(1)}, u32[]{:S(2)}, u32[]{:S(2)}) collective-permute-start(bf16[1,96,1792]{2,1,0:T(8,128)(2,1)S(1)} %get-tuple-element.157), channel_id=1, source_target_pairs={{0,4},{4,0},{8,12},{12,8},{1,5},{5,1},{9,13},{13,9},{2,6},{6,2},{1... | collective-permute-start | bytes 1032200 | tf_op jit(solution)/shard_map/ppermute | solution.py:26
  34.6 23.5 %collective-permute-start.19 = (bf16[1,96,1792]{2,1,0:T(8,128)(2,1)S(1)}, bf16[1,96,1792]{2,1,0:T(8,128)(2,1)S(1)}, u32[]{:S(2)}, u32[]{:S(2)}) collective-permute-start(bf16[1,96,1792]{2,1,0:T(8,128)(2,1)S(1)} %get-tuple-element.158), channel_id=1, source_target_pairs={{0,8},{4,12},{8,0},{12,4},{1,9},{5,13},{9,1},{13,5},{2,10},{6,14},... | collective-permute-start | bytes 1032200 | tf_op jit(solution)/shard_map/ppermute | solution.py:26
  58.1 12.4 %collective-permute-start.22 = (bf16[1,96,1792]{2,1,0:T(8,128)(2,1)S(1)}, bf16[1,96,1792]{2,1,0:T(8,128)(2,1)S(1)}, u32[]{:S(2)}, u32[]{:S(2)}) collective-permute-start(bf16[1,96,1792]{2,1,0:T(8,128)(2,1)S(1)} %get-tuple-element.168), channel_id=1, source_target_pairs={{0,4},{4,0},{8,12},{12,8},{1,5},{5,1},{9,13},{13,9},{2,6},{6,2},{1... | collective-permute-start | bytes 1032200 | tf_op jit(solution)/shard_map/ppermute | solution.py:26
  59.7 11.4 %collective-permute-start.23 = (bf16[1,96,1792]{2,1,0:T(8,128)(2,1)S(1)}, bf16[1,96,1792]{2,1,0:T(8,128)(2,1)S(1)}, u32[]{:S(2)}, u32[]{:S(2)}) collective-permute-start(bf16[1,96,1792]{2,1,0:T(8,128)(2,1)S(1)} %get-tuple-element.169), channel_id=1, source_target_pairs={{0,8},{4,12},{8,0},{12,4},{1,9},{5,13},{9,1},{13,5},{2,10},{6,14},... | collective-permute-start | bytes 1032200 | tf_op jit(solution)/shard_map/ppermute | solution.py:26
  63.8 11.0 %collective-permute-start.21 = (bf16[1,48,1792]{2,1,0:T(8,128)(2,1)S(1)}, bf16[1,48,1792]{2,1,0:T(8,128)(2,1)S(1)}, u32[]{:S(2)}, u32[]{:S(2)}) collective-permute-start(bf16[1,48,1792]{2,1,0:T(8,128)(2,1)S(1)} %add_convert_fusion.3), channel_id=1, source_target_pairs={{0,4},{4,0},{8,12},{12,8},{1,5},{5,1},{9,13},{13,9},{2,6},{6,2},{1... | collective-permute-start | bytes 516104 | tf_op jit(solution)/shard_map/ppermute | solution.py:26
  95.5 18.1 %collective-permute-start.31 = (bf16[2,96,1792]{2,1,0:T(8,128)(2,1)S(1)}, bf16[2,96,1792]{2,1,0:T(8,128)(2,1)S(1)}, u32[]{:S(2)}, u32[]{:S(2)}) collective-permute-start(bf16[2,96,1792]{2,1,0:T(8,128)(2,1)S(1)} %get-tuple-element.203.refs_0_), channel_id=1, source_target_pairs={{0,8},{4,12},{8,0},{12,4},{1,9},{5,13},{9,1},{13,5},{2,10},{6,14},... | collective-permute-start | bytes 2064392 | tf_op jit(solution)/shard_map/ppermute | solution.py:26
  97.0 16.6 %collective-permute-start.30 = (bf16[2,96,1792]{2,1,0:T(8,128)(2,1)S(1)}, bf16[2,96,1792]{2,1,0:T(8,128)(2,1)S(1)}, u32[]{:S(2)}, u32[]{:S(2)}) collective-permute-start(bf16[2,96,1792]{2,1,0:T(8,128)(2,1)S(1)} %get-tuple-element.203.refs_0_), channel_id=1, source_target_pairs={{0,4},{4,0},{8,12},{12,8},{1,5},{5,1},{9,13},{13,9},{2,6},{6,2},{1... | collective-permute-start | bytes 2064392 | tf_op jit(solution)/shard_map/ppermute | solution.py:26
  113.7 14.5 %collective-permute-start.40 = (bf16[2,48,1792]{2,1,0:T(8,128)(2,1)S(1)}, bf16[2,48,1792]{2,1,0:T(8,128)(2,1)S(1)}, u32[]{:S(2)}, u32[]{:S(2)}) collective-permute-start(bf16[2,48,1792]{2,1,0:T(8,128)(2,1)S(1)} %slice.49), channel_id=1, source_target_pairs={{0,4},{4,0},{8,12},{12,8},{1,5},{5,1},{9,13},{13,9},{2,6},{6,2},{1... | collective-permute-start | bytes 1032200 | tf_op jit(solution)/shard_map/ppermute | solution.py:26
  114.3 13.9 %collective-permute-start.41 = (bf16[2,48,1792]{2,1,0:T(8,128)(2,1)S(1)}, bf16[2,48,1792]{2,1,0:T(8,128)(2,1)S(1)}, u32[]{:S(2)}, u32[]{:S(2)}) collective-permute-start(bf16[2,48,1792]{2,1,0:T(8,128)(2,1)S(1)} %slice.50), channel_id=1, source_target_pairs={{0,8},{4,12},{8,0},{12,4},{1,9},{5,13},{9,1},{13,5},{2,10},{6,14},... | collective-permute-start | bytes 1032200 | tf_op jit(solution)/shard_map/ppermute | solution.py:26
  116.7 17.5 %collective-permute-start.37 = (bf16[48,2048]{1,0:T(8,128)(2,1)S(1)}, bf16[48,2048]{1,0:T(8,128)(2,1)S(1)}, u32[]{:S(2)}, u32[]{:S(2)}) collective-permute-start(bf16[48,2048]{1,0:T(8,128)(2,1)S(1)} %get-tuple-element.218), channel_id=1, source_target_pairs={{0,1},{1,0},{2,3},{3,2},{4,5},{5,4},{6,7},{7,6},{8,9},{9,8},{10,11... | collective-permute-start | bytes 589832 | tf_op jit(solution)/shard_map/ppermute | solution.py:26
  116.8 17.4 %collective-permute-start.38 = (bf16[48,2048]{1,0:T(8,128)(2,1)S(1)}, bf16[48,2048]{1,0:T(8,128)(2,1)S(1)}, u32[]{:S(2)}, u32[]{:S(2)}) collective-permute-start(bf16[48,2048]{1,0:T(8,128)(2,1)S(1)} %get-tuple-element.219), channel_id=1, source_target_pairs={{0,2},{1,3},{2,0},{3,1},{4,6},{5,7},{6,4},{7,5},{8,10},{9,11},{10,... | collective-permute-start | bytes 589832 | tf_op jit(solution)/shard_map/ppermute | solution.py:26
  119.7 14.5 %collective-permute-start.39 = (bf16[48,2048]{1,0:T(8,128)(2,1)S(1)}, bf16[48,2048]{1,0:T(8,128)(2,1)S(1)}, u32[]{:S(2)}, u32[]{:S(2)}) collective-permute-start(bf16[48,2048]{1,0:T(8,128)(2,1)S(1)} %get-tuple-element.220), channel_id=1, source_target_pairs={{0,3},{1,2},{2,1},{3,0},{4,7},{5,6},{6,5},{7,4},{8,11},{9,10},{10,... | collective-permute-start | bytes 589832 | tf_op jit(solution)/shard_map/ppermute | solution.py:26
  141.8 20.4 %collective-permute-start.43 = (bf16[48,2048]{1,0:T(8,128)(2,1)S(1)}, bf16[48,2048]{1,0:T(8,128)(2,1)S(1)}, u32[]{:S(2)}, u32[]{:S(2)}) collective-permute-start(bf16[48,2048]{1,0:T(8,128)(2,1)S(1)} %get-tuple-element.245), channel_id=1, source_target_pairs={{0,1},{1,0},{2,3},{3,2},{4,5},{5,4},{6,7},{7,6},{8,9},{9,8},{10,11... | collective-permute-start | bytes 589832 | tf_op jit(solution)/shard_map/ppermute | solution.py:26
  141.9 20.3 %collective-permute-start.44 = (bf16[48,2048]{1,0:T(8,128)(2,1)S(1)}, bf16[48,2048]{1,0:T(8,128)(2,1)S(1)}, u32[]{:S(2)}, u32[]{:S(2)}) collective-permute-start(bf16[48,2048]{1,0:T(8,128)(2,1)S(1)} %get-tuple-element.246), channel_id=1, source_target_pairs={{0,2},{1,3},{2,0},{3,1},{4,6},{5,7},{6,4},{7,5},{8,10},{9,11},{10,... | collective-permute-start | bytes 589832 | tf_op jit(solution)/shard_map/ppermute | solution.py:26
  144.8 17.4 %collective-permute-start.45 = (bf16[48,2048]{1,0:T(8,128)(2,1)S(1)}, bf16[48,2048]{1,0:T(8,128)(2,1)S(1)}, u32[]{:S(2)}, u32[]{:S(2)}) collective-permute-start(bf16[48,2048]{1,0:T(8,128)(2,1)S(1)} %get-tuple-element.247), channel_id=1, source_target_pairs={{0,3},{1,2},{2,1},{3,0},{4,7},{5,6},{6,5},{7,4},{8,11},{9,10},{10,... | collective-permute-start | bytes 589832 | tf_op jit(solution)/shard_map/ppermute | solution.py:26
  146.3 15.9 %collective-permute-start.48 = (f32[1,2048]{1,0:T(1,128)S(1)}, f32[1,2048]{1,0:T(1,128)S(1)}, u32[]{:S(2)}, u32[]{:S(2)}) collective-permute-start(f32[1,2048]{1,0:T(1,128)S(1)} %add.81), channel_id=1, source_target_pairs={{0,2},{1,3},{2,0},{3,1},{4,6},{5,7},{6,4},{7,5},{8,10},{9,11},{10,... | collective-permute-start | bytes 24584 | tf_op jit(solution)/shard_map/ppermute | solution.py:26
  146.6 15.6 %collective-permute-start.49 = (f32[48,128]{1,0:T(8,128)S(1)}, f32[48,128]{1,0:T(8,128)S(1)}, u32[]{:S(2)}, u32[]{:S(2)}) collective-permute-start(f32[48,128]{1,0:T(8,128)S(1)} %add.82), channel_id=1, source_target_pairs={{0,8},{4,12},{8,0},{12,4},{1,9},{5,13},{9,1},{13,5},{2,10},{6,14},... | collective-permute-start | bytes 73736 | tf_op jit(solution)/shard_map/ppermute | solution.py:26
  (37 other events, 251.1 us)
